TPU v7x, 128 devices: a whole 4x4x4 slice. The times are simulated.
128 devices in a mesh: row: 8 (over z, x_hi), blk: 16 (over y, x_lo, core).
Axes of the slice: x: 4 (x_hi: 2, x_lo: 2; x = x_hi * 2 + x_lo), y: 4, z: 4, core: 2. Of those that a mesh axis runs over, the one named last changes fastest.
Arguments:
- amplitudes: bfloat16 [8192, 131072], P('blk', 'row'), may hold values from -6 to 6
- integrals: bfloat16 [131072, 512], P('row', 'blk'), may hold values from -0.0234375 to 0.0234375
- live_pairs: int32 [32], P('row'), may hold values from 0 to 1, as said below
- slab_amplitudes: bfloat16 [64, 128, 512], P('row', 'blk'), may hold values from -6 to 6
- cycle_integrals: bfloat16 [2048, 2048], P('row', 'blk'), may hold values from -0.125 to 0.125
Outputs:
- residual: bfloat16 [8192, 512], P('blk', 'row')
Inputs may be any that keep to these rules, and one draw needn't show every extreme that they name: `live_pairs`: within each aligned group of 4 slots (slots g * 4 to g * 4 + 3) exactly 2 slots are live.
All inputs are finite; a program needn't handle non-finite values.
Results may differ from a plain program's by a relative error of at most 0.001.
Values may be sent and summed in bfloat16 or wider, within the bound.
No kernel may reach another device: no remote copies, remote signals or barrier semaphores. Data moves between devices by JAX's collectives and lax.ppermute only.
A program may use at most 192 MiB of HBM per device.

v0:
```python
import jax
import jax.numpy as jnp
from jax import lax
from jax.sharding import PartitionSpec as P

OW = 64
TS = 64
SB = 32


def per_device(amplitudes, integrals, live_pairs, slab_amplitudes, cycle_integrals):
    tile_size = TS * TS
    slot_count = live_pairs.shape[0]
    shard_rows = lax.all_gather(integrals, "blk", axis=1, tiled=True)
    blocks = shard_rows.reshape(slot_count, tile_size, shard_rows.shape[1])
    blocks = blocks * live_pairs.astype(jnp.bfloat16)[:, None, None]
    partial_sums = jnp.dot(
        amplitudes,
        blocks.reshape(slot_count * tile_size, shard_rows.shape[1]),
        preferred_element_type=jnp.float32,
    )
    cycle_local = lax.all_gather(cycle_integrals, "blk", axis=1, tiled=True)
    i_local = slab_amplitudes.shape[1]
    summed = lax.psum_scatter(partial_sums, "row", scatter_dimension=1, tiled=True)
    moved_amps = lax.all_to_all(slab_amplitudes, "row", split_axis=2, concat_axis=0, tiled=True)
    a_local = moved_amps.shape[2] // SB
    along_rows = moved_amps.reshape(OW, i_local, a_local, SB).transpose(0, 3, 1, 2)
    along_rows = along_rows.reshape(OW * SB, i_local * a_local)
    cycle_full = lax.dot_general(
        along_rows,
        lax.all_gather(cycle_local, "row", axis=0, tiled=True),
        (((0,), (0,)), ((), ())),
        preferred_element_type=jnp.float32,
    )
    cycle_block = cycle_full.reshape(i_local, a_local, OW, SB).transpose(0, 2, 1, 3)
    summed = summed + cycle_block.reshape(i_local * OW, a_local * SB)
    return summed.astype(jnp.bfloat16)


def solution(mesh):
    return jax.shard_map(
        per_device,
        mesh=mesh,
        in_specs=(
            P("blk", "row"),
            P("row", "blk"),
            P("row"),
            P("row", "blk", None),
            P("row", "blk"),
        ),
        out_specs=P("blk", "row"),
        check_vma=False,
    )
```

profile of v0, /device:TPU:0, one launch (start us, length us, event | category | flops | bytes accessed | tf_op | source)
XLA Modules:
  0.0 335.9 jit_solution(14165697484937154450)
XLA Ops:
  6.5 0.0 all-gather.6.cloned.1.call-start
  6.5 1.6 copy.14
  8.1 0.0 all-gather.6.cloned.1.call-update
  8.1 0.0 all-gather.4.cloned.1.call-start
  8.2 0.7 all-gather.4.cloned.1.call-update
  8.9 0.0 all-gather.8.cloned.1.call-start
  8.9 35.0 %all-gather.6.cloned.1.call-done = bf16[256,2048]{0,1:T(8,128)(2,1)} async-done(((bf16[256,128]{0,1:T(8,128)(2,1)}), bf16[256,2048]{0,1:T(8,128)(2,1)}) %all-gather.6.cloned.1.call-update) | async-done | bytes 1048592 | tf_op jit(solution)/shard_map/all_gather | solution.py:22
  44.0 0.0 all-gather.8.cloned.1.call-update
  44.0 0.0 reduce-scatter.2.cloned.1.call-start
  44.0 0.7 convert_element_type.6
  44.7 0.1 broadcast_bitcast_fusion
  44.8 92.6 %all-gather.4.cloned.1.call-done = bf16[16384,512]{0,1:T(8,128)(2,1)} async-done(((bf16[16384,32]{0,1:T(8,128)(2,1)}), bf16[16384,512]{0,1:T(8,128)(2,1)}) %all-gather.4.cloned.1.call-update) | async-done | bytes 16777232 | tf_op jit(solution)/shard_map/all_gather | solution.py:14
  137.4 0.0 copy-start
  137.4 16.0 %fusion.6 = f32[512,512]{0,1:T(8,128)} fusion(bf16[512,16384]{1,0:T(8,128)(2,1)} %param.5, bf16[16384,512]{0,1:T(8,128)(2,1)} %all-gather.4.cloned.1.call-done, bf16[16384]{0:T(1024)(128)(2,1)S(1)} %bitcast.39), kind=kOutput, calls=%fused_computation.6 | convolution fusion | flops 8598323200 | bytes 34635776 | tf_op jit(solution)/shard_map/dot_general | solution.py:17
  153.4 0.0 reduce-scatter.2.cloned.1.call-update
  153.4 0.0 copy-done
  153.4 0.7 copy.11
  154.2 1.1 reshape.22
  155.2 14.5 %all_to_all.15 = bf16[8,2,2048]{2,1,0:T(2,128)(2,1)S(1)} all-to-all(bf16[8,2,2048]{2,1,0:T(2,128)(2,1)S(1)} %reshape.22), channel_id=1, replica_groups=mesh['row'=8,'blk'=16] {'row'}, dimensions={0} | all-to-all | bytes 131072 | tf_op jit(solution)/shard_map/all_to_all | solution.py:25
  169.7 1.2 reshape.23
  170.9 0.6 copy.12
  171.5 0.1 reshape.17
  171.7 0.1 copy.13
  171.8 0.3 reshape.18
  172.0 0.1 dot_general.19
  172.1 82.6 %all-gather.8.cloned.1.call-done = bf16[2048,2048]{0,1:T(8,128)(2,1)} async-done(((bf16[256,2048]{0,1:T(8,128)(2,1)}), bf16[2048,2048]{0,1:T(8,128)(2,1)}) %all-gather.8.cloned.1.call-update) | async-done | bytes 8388624 | tf_op jit(solution)/shard_map/all_gather | solution.py:31
  254.7 12.2 %fusion.9 = f32[8,64,2,32]{1,0,3,2:T(8,128)S(1)} fusion(bf16[64,32,2048]{2,1,0:T(8,128)(2,1)} %bitcast.40, bf16[8,2,2048,1]{2,1,0,3:T(2,128)(2,1)S(1)} %bitcast.38), kind=kOutput, calls=%fused_computation.7 | convolution fusion | flops 134217728 | bytes 8585216 | tf_op jit(solution)/shard_map/dot_general | solution.py:29
  266.9 0.1 reshape.19
  267.0 60.8 %reduce-scatter.2.cloned.1.call-done = f32[512,64]{0,1:T(8,128)} async-done(((f32[512,512]{0,1:T(8,128)}), f32[512,64]{0,1:T(8,128)}) %reduce-scatter.2.cloned.1.call-update) | async-done | bytes 131088 | tf_op jit(solution)/shard_map/reduce_scatter | solution.py:24
  327.8 1.6 add_convert_fusion
  (1 shorter events, 0.0 us)
Async XLA Ops:
  6.5 37.4 %all-gather.6.cloned.1.call-start = ((), (), s32[]{:S(2)}) async-start(), calls=%async_computation.4 | async-start | bytes 1114112 | tf_op jit(solution)/shard_map/all_gather | solution.py:22
  8.1 129.2 %all-gather.4.cloned.1.call-start = ((), (), s32[]{:S(2)}) async-start(), calls=%async_computation.2 | async-start | bytes 17825792 | tf_op jit(solution)/shard_map/all_gather | solution.py:14
  8.9 245.8 %all-gather.8.cloned.1.call-start = ((), (), s32[]{:S(2)}) async-start(), calls=%async_computation.5 | async-start | bytes 9437184 | tf_op jit(solution)/shard_map/all_gather | solution.py:31
  44.0 283.8 %reduce-scatter.2.cloned.1.call-start = ((), (), s32[]{:S(2)}) async-start(), calls=%async_computation.3 | async-start | bytes 1179648 | tf_op jit(solution)/shard_map/reduce_scatter | solution.py:24
  137.4 16.1 %copy-start = (bf16[8,8,512]{2,1,0:T(8,128)(2,1)S(1)}, bf16[8,8,512]{2,1,0:T(8,128)(2,1)}, u32[]{:S(2)}) copy-start(bf16[8,8,512]{2,1,0:T(8,128)(2,1)} %param.8) | copy-start | bytes 196612
Sparse Core Ops, SparseCore 0:
  9.1 34.8 all-gather.5
  45.7 91.6 all-gather.3
  139.6 115.1 all-gather.7
  258.2 69.5 reduce-scatter.1
where the time goes:
time: 336 us
  waiting for transfers between devices  272 us (81%)
  matrix products  28.2 us (8%)
  blocking collectives  14.5 us (4%)
  between operations  13.2 us (4%)
  local copies, waits for them, and re-layouts  5.91 us (2%)
    all_gather x1, waiting for transfers between devices, per_device(): shard_rows = lax.all_gather(integrals, 'blk', axis=1, tiled=True)  92.6 us
    all_gather x1, waiting for transfers between devices, per_device(): lax.all_gather(cycle_local, 'row', axis=0, tiled=True)  82.6 us
    reduce_scatter x1, waiting for transfers between devices, per_device(): lax.psum_scatter(partial_sums, 'row', scatter_dimension=1, tiled=True)  60.8 us
    all_gather x1, waiting for transfers between devices, per_device(): cycle_local = lax.all_gather(cycle_integrals, 'blk', axis=1, tiled=True)  35 us
    dot_general x1, matrix products, per_device(): jnp.dot(amplitudes, blocks.reshape(slot_count * tile_size, shard_rows.sha...  16 us
    all_to_all x1, blocking collectives, per_device(): lax.all_to_all(slab_amplitudes, 'row', split_axis=2, concat_axis=0, tiled...  14.5 us
    dot_general x1, matrix products, per_device(): lax.dot_general(along_rows, lax.all_gather(cycle_local, 'row', axis=0, ti...  12.2 us
  transfers between devices with their start and end apart: 4, of which 4 were waited for; matrix products, arithmetic and copies ran while one was open for 10% of the time, Pallas kernels for 0%

commit v1 on v0

v1 whole, which is shorter than its diff:
```python
import jax
import jax.numpy as jnp
from jax import lax
from jax.sharding import PartitionSpec as P

OW = 64
TS = 64
SB = 32
LIVE = 2


def per_device(amplitudes, integrals, live_pairs, slab_amplitudes, cycle_integrals):
    tile = TS * TS
    slots = live_pairs.shape[0]
    order = jnp.argsort(1 - live_pairs, stable=True)[:LIVE]
    columns = integrals.T.reshape(-1, slots, tile)
    live_columns = jnp.concatenate(
        [lax.dynamic_index_in_dim(columns, order[n], 1, keepdims=False) for n in range(LIVE)], axis=1
    )
    live_amps = jnp.concatenate(
        [lax.dynamic_slice_in_dim(amplitudes, order[n] * tile, tile, 1) for n in range(LIVE)], axis=1
    )
    cycle_local = lax.all_gather(cycle_integrals, "blk", axis=1, tiled=True)
    gathered = lax.all_gather(live_columns, "blk", axis=0, tiled=True)

    k_local, i_local, ac = slab_amplitudes.shape
    a_all = ac // SB
    slab = slab_amplitudes.reshape(k_local, i_local, a_all, SB).transpose(2, 1, 0, 3)
    slab = slab.reshape(a_all * i_local, k_local * SB)
    cycle = jnp.dot(slab, cycle_local, preferred_element_type=jnp.float32)
    cycle = cycle.reshape(a_all, i_local, OW, SB).transpose(0, 3, 1, 2).reshape(a_all * SB, i_local * OW)

    partial_sums = lax.dot_general(
        gathered, live_amps, (((1,), (1,)), ((), ())), preferred_element_type=jnp.float32
    )
    partial_sums = partial_sums + cycle
    rows = lax.psum(1, "row")
    parts = lax.all_to_all(partial_sums.reshape(rows, -1, partial_sums.shape[1]), "row", 0, 0)
    return jnp.sum(parts, axis=0).astype(jnp.bfloat16).T


def solution(mesh):
    return jax.shard_map(
        per_device,
        mesh=mesh,
        in_specs=(
            P("blk", "row"),
            P("row", "blk"),
            P("row"),
            P("row", "blk", None),
            P("row", "blk"),
        ),
        out_specs=P("blk", "row"),
        check_vma=False,
    )
```

time: 336 us -> 140 us (0.42)
  waiting for transfers between devices: 272 us -> 65.9 us
  matrix products: 28.2 us -> 12.2 us
  blocking collectives: 14.5 us -> 24.3 us
  local copies, waits for them, and re-layouts: 5.91 us -> 15.6 us
  between operations: 13.2 us -> 18.3 us
    all_gather x2 -> x1, waiting for transfers between devices: 175 us -> 50.7 us  [per_device(): gathered = lax.all_gather(live_columns, 'blk', axis=0, tiled=True)]
    reduce_scatter x1 -> x0, waiting for transfers between devices: 60.8 us -> none  [per_device(): lax.psum_scatter(partial_sums, 'row', scatter_dimension=1, tiled=True)]
    all_gather x1, waiting for transfers between devices: 35 us -> 15.1 us  [per_device(): cycle_local = lax.all_gather(cycle_integrals, 'blk', axis=1, tiled=True)]
    dot_general x2, matrix products: 28.2 us -> 12.2 us  [the longest x1 9.56 us: per_device(): lax.dot_general(gathered, live_amps, (((1,), (1,)), ((), ())), preferred_...]
    all_to_all x1, blocking collectives: 14.5 us -> 24.3 us  [per_device(): lax.all_to_all(partial_sums.reshape(rows, -1, partial_sums.shape[1]), 'ro...]
    dynamic_slice x0 -> x2, local copies, waits for them, and re-layouts: none -> 9.08 us  [the longest x1 7.84 us: per_device(): lax.dynamic_slice_in_dim(amplitudes, order[n] * tile, tile, 1)]
  transfers between devices with their start and end apart: 4 -> 2, of which waited for: 4 -> 2; matrix products, arithmetic and copies ran while one was open for 10% -> 14% of each run, Pallas kernels for 0% -> 0%
where the time goes in v1:
time: 140 us; the launch traced here: 139 us
  waiting for transfers between devices  65.9 us (47%)
  blocking collectives  24.3 us (17%)
  between operations  18.3 us (13%)
  local copies, waits for them, and re-layouts  15.6 us (11%)
  matrix products  12.2 us (9%)
  other arithmetic  3.04 us (2%)
    all_gather x1, waiting for transfers between devices, per_device(): gathered = lax.all_gather(live_columns, 'blk', axis=0, tiled=True)  50.7 us
    all_to_all x1, blocking collectives, per_device(): lax.all_to_all(partial_sums.reshape(rows, -1, partial_sums.shape[1]), 'ro...  24.3 us
    all_gather x1, waiting for transfers between devices, per_device(): cycle_local = lax.all_gather(cycle_integrals, 'blk', axis=1, tiled=True)  15.1 us
    dot_general x1, matrix products, per_device(): lax.dot_general(gathered, live_amps, (((1,), (1,)), ((), ())), preferred_...  9.56 us
    dynamic_slice x1, local copies, waits for them, and re-layouts, per_device(): lax.dynamic_slice_in_dim(amplitudes, order[n] * tile, tile, 1)  7.84 us
  transfers between devices with their start and end apart: 2, of which 2 were waited for; matrix products, arithmetic and copies ran while one was open for 14% of the time, Pallas kernels for 0%

profile of v1, /device:TPU:0, one launch (start us, length us, event | category | flops | bytes accessed | tf_op | source)
XLA Modules:
  0.0 139.2 jit_solution(17027962581198020309)
XLA Ops:
  6.5 0.0 all-gather.5.cloned.1.call-start
  6.5 1.6 %copy.11 = bf16[256,128]{0,1:T(8,128)(2,1)} copy(bf16[256,128]{1,0:T(8,128)(2,1)} %param.9) | data formatting | bytes 131072 | tf_op args[4]
  8.1 0.0 all-gather.5.cloned.1.call-update
  8.1 0.0 all-gather.3.cloned.1.call-start
  8.2 0.7 broadcast_subtract_fusion
  8.8 0.8 sort.17
  9.7 0.6 fusion.11
  12.7 1.8 %reshape.17 = bf16[32,4,4096]{2,1,0:T(4,128)(2,1)S(1)} reshape(bf16[32,16384]{1,0:T(8,128)(2,1)} %bitcast.30) | data formatting | bytes 2097152 | tf_op jit(solution)/shard_map/reshape | solution.py:16
  15.7 1.2 constant_dynamic-slice_fusion.3
  17.0 0.6 copy_bitcast_fusion
  17.5 0.9 pad_maximum_fusion
  18.4 0.0 all-gather.3.cloned.1.call-update
  19.6 1.0 reshape.18
  20.7 0.2 copy.10
  20.9 0.2 reshape.21
  21.0 7.8 %constant_dynamic-slice_fusion.1 = (bf16[512,4096]{1,0:T(8,128)(2,1)}, bf16[512,4096]{1,0:T(8,128)(2,1)}) fusion(bf16[512,16384]{1,0:T(8,128)(2,1)} %param.5, s32[]{:T(128)S(6)} %select_n.15, s32[]{:T(128)S(6)} %select_n.16), kind=kLoop, calls=%fused_computation.14 | loop fusion | bytes 16777224 | tf_op jit(solution)/shard_map/dynamic_slice | solution.py:21
  28.9 15.1 %all-gather.5.cloned.1.call-done = bf16[256,2048]{0,1:T(8,128)(2,1)} async-done(((bf16[256,128]{0,1:T(8,128)(2,1)}), bf16[256,2048]{0,1:T(8,128)(2,1)}) %all-gather.5.cloned.1.call-update) | async-done | bytes 1048592 | tf_op jit(solution)/shard_map/all_gather | solution.py:23
  44.0 2.6 %convolution_bitcast_fusion = f32[16,32,8,64]{3,2,1,0:T(8,128)S(1)} fusion(bf16[64,32,256]{2,1,0:T(8,128)(2,1)} %bitcast.28, bf16[16,8,256,1]{2,1,0,3:T(8,128)(2,1)S(1)} %reshape.21), kind=kOutput, calls=%fused_computation.4 | convolution fusion | flops 134217728 | bytes 2162688 | tf_op jit(solution)/shard_map/dot_general | solution.py:30
  46.6 0.5 reshape.19
  47.1 50.7 %all-gather.3.cloned.1.call-done = bf16[512,8192]{1,0:T(8,128)(2,1)} async-done(((bf16[32,8192]{1,0:T(8,128)(2,1)}), bf16[512,8192]{1,0:T(8,128)(2,1)}) %all-gather.3.cloned.1.call-update) | async-done | bytes 8388624 | tf_op jit(solution)/shard_map/all_gather | solution.py:24
  97.9 9.6 %fusion.4 = f32[512,512]{1,0:T(8,128)S(1)} fusion(f32[512,512]{1,0:T(8,128)S(1)} %reshape.19, bf16[512,8192]{1,0:T(8,128)(2,1)} %all-gather.3.cloned.1.call-done, bf16[512,4096]{1,0:T(8,128)(2,1)} %get-tuple-element.8, bf16[512,4096]{1,0:T(8,128)(2,1)} %get-tuple-element.7), kind=kOutput, calls=%fused_computation.5 | convolution fusion | flops 4312006656 | bytes 18874368 | tf_op jit(solution)/shard_map/dot_general | solution.py:33
  107.4 24.3 %all_to_all.5 = f32[8,64,512]{2,1,0:T(8,128)S(1)} all-to-all(f32[8,64,512]{2,1,0:T(8,128)S(1)} %bitcast.31), channel_id=1, replica_groups=mesh['row'=8,'blk'=16] {'row'}, dimensions={0} | all-to-all | bytes 2097152 | tf_op jit(solution)/shard_map/all_to_all | solution.py:38
  131.7 0.7 reduce_sum.9
  (1 shorter events, 0.0 us)
Async XLA Ops:
  6.5 37.5 %all-gather.5.cloned.1.call-start = ((), (), s32[]{:S(2)}) async-start(), calls=%async_computation.2 | async-start | bytes 1114112 | tf_op jit(solution)/shard_map/all_gather | solution.py:23
  8.1 89.7 %all-gather.3.cloned.1.call-start = ((), (), s32[]{:S(2)}) async-start(), calls=%async_computation.1 | async-start | bytes 8912896 | tf_op jit(solution)/shard_map/all_gather | solution.py:24
Sparse Core Ops, SparseCore 0:
  9.1 34.8 all-gather.4
  45.7 52.1 all-gather.2

commit v2 on v1

v2 whole, which is shorter than its diff:
```python
import functools

import jax
import jax.numpy as jnp
from jax import lax
from jax.experimental import pallas as pl
from jax.experimental.pallas import tpu as pltpu
from jax.sharding import PartitionSpec as P

OW = 64
TS = 64
SB = 32
TILE = TS * TS
NY, NX, NC = 4, 2, 2
NZ, NH = 4, 2
HALF = SB // 2
STEP = 1024
KT = TILE // STEP
MIB = 1 << 20


def blk_moves(dy, dx, dc):
    spots = [(y, x, c) for y in range(NY) for x in range(NX) for c in range(NC)]
    index = lambda y, x, c: ((y % NY) * NX + x % NX) * NC + c % NC
    return [(index(y, x, c), index(y + dy, x + dx, c + dc)) for y, x, c in spots]


def row_moves(dz, dx):
    spots = [(z, x) for z in range(NZ) for x in range(NH)]
    index = lambda z, x: (z % NZ) * NH + x % NH
    return [(index(z, x), index(z + dz, x + dx)) for z, x in spots]


def move(value, dy=0, dx=0, dc=0):
    return lax.ppermute(value, "blk", blk_moves(dy, dx, dc))


def move_row(value, dz=0, dx=0):
    return lax.ppermute(value, "row", row_moves(dz, dx))


def live_slot(live, n):
    if n == 0:
        return jnp.where(live[0] == 1, 0, jnp.where(live[1] == 1, 1, 2))
    return jnp.where(live[3] == 1, 3, jnp.where(live[2] == 1, 2, 1))


def pick_kernel(live, columns, first, second, sems):
    copies = []
    for n in range(2):
        start = pl.multiple_of(live_slot(live, n) * TILE, TILE)
        for h, out in enumerate((first, second)):
            copies.append(
                pltpu.make_async_copy(
                    columns.at[pl.ds(h * HALF, HALF), pl.ds(start, TILE)], out.at[n], sems.at[n, h]
                )
            )
    for copy in copies:
        copy.start()
    for copy in copies:
        copy.wait()


def pick_live(live_pairs, columns):
    shape = jax.ShapeDtypeStruct((2, HALF, TILE), columns.dtype)
    return pl.pallas_call(
        pick_kernel,
        out_shape=(shape, shape),
        in_specs=[pl.BlockSpec(memory_space=pltpu.SMEM), pl.BlockSpec(memory_space=pl.ANY)],
        out_specs=(pl.BlockSpec(memory_space=pltpu.VMEM),) * 2,
        scratch_shapes=[pltpu.SemaphoreType.DMA((2, 2))],
        name="pick_live",
    )(live_pairs, columns)


def load_kernel(live, amps, after, out, sems):
    copies = []
    for n in range(2):
        for k in range(KT):
            start = pl.multiple_of(live_slot(live, n) * TILE + k * STEP, STEP)
            at = n * KT + k
            copies.append(pltpu.make_async_copy(amps.at[:, pl.ds(start, STEP)], out.at[at], sems.at[at]))
    for copy in copies:
        copy.start()
    for copy in copies:
        copy.wait()


def load_live(live_pairs, amplitudes, after):
    rows = amplitudes.shape[0]
    return pl.pallas_call(
        load_kernel,
        out_shape=jax.ShapeDtypeStruct((2 * KT, rows, STEP), amplitudes.dtype),
        in_specs=[pl.BlockSpec(memory_space=pltpu.SMEM)] + [pl.BlockSpec(memory_space=pl.ANY)] * 2,
        out_specs=pl.BlockSpec(memory_space=pltpu.VMEM),
        scratch_shapes=[pltpu.SemaphoreType.DMA((2 * KT,))],
        compiler_params=pltpu.CompilerParams(vmem_limit_bytes=40 * MIB),
        name="load_live",
    )(live_pairs, amplitudes, after)


def ladder_kernel(places, count, half, amps, cycle, *refs):
    pieces, outs, total = refs[:count], refs[count : count + NZ], refs[count + NZ]
    for n in range(2):
        held = {tuple(place): pieces[piece].at[index] for piece, index, slot, *place in places if slot == n}
        for k in range(KT):
            cols = slice(k * STEP, (k + 1) * STEP)
            block = jnp.concatenate(
                [held[dy, e, g][:, cols] for dy in range(NY) for e in range(NX) for g in range(NC)]
            )
            term = lax.dot_general(
                block, amps[n * KT + k], (((1,), (1,)), ((), ())), preferred_element_type=jnp.float32
            )
            if n == k == 0:
                total[...] = term
            else:
                total[...] += term

    spot = lax.axis_index("blk")
    y, x, c = spot // (NX * NC), (spot // NC) % NX, spot % NC
    line = lax.axis_index("row")
    z, xh = line // NH, line % NH
    for dz in range(NZ):
        for f in range(NH):
            for core in range(NC):
                dy, e, g = (z + dz + NY - y) % NY, (xh + f + NX - x) % NX, (core + NC - c) % NC
                here = ((dy * NX + e) * NC + g) * HALF
                there = (((z + dz) % NZ) * NH + (xh + f) % NH) * NC + core
                there = there * SB + half * HALF
                there = pl.ds(pl.multiple_of(there, HALF), HALF)
                outs[dz][f, core * HALF : (core + 1) * HALF, :] = total[
                    pl.ds(pl.multiple_of(here, HALF), HALF), :
                ] + jnp.concatenate([cycle[n, there, :] for n in range(cycle.shape[0])], axis=1)


def ladder(half, amplitudes, cycle, pieces):
    places = [(n, *place) for n, (_, held) in enumerate(pieces) for place in held]
    places = [(n, index, slot, dy % NY, e, g) for n, index, slot, dy, e, g in places]
    arrays = [array for array, _ in pieces]
    rows = amplitudes.shape[1]
    q = NY * NX * NC * HALF
    out = jax.ShapeDtypeStruct((NH, q // (NZ * NH), rows), jnp.float32)
    return pl.pallas_call(
        functools.partial(ladder_kernel, places, len(arrays), half),
        out_shape=(out,) * NZ,
        in_specs=[pl.BlockSpec(memory_space=pltpu.VMEM)] * (2 + len(arrays)),
        out_specs=[pl.BlockSpec(memory_space=pltpu.VMEM)] * NZ,
        scratch_shapes=[pltpu.VMEM((q, rows), jnp.float32)],
        compiler_params=pltpu.CompilerParams(vmem_limit_bytes=24 * MIB),
        cost_estimate=pl.CostEstimate(
            flops=2 * q * rows * 2 * TILE, bytes_accessed=2 * q * 2 * TILE, transcendentals=0
        ),
        name="ladder",
    )(amplitudes, cycle, *arrays)


def gather_cycle(cycle_integrals, ready):
    pair = jnp.stack([cycle_integrals, move(cycle_integrals, dx=1)])
    pair, _ = lax.optimization_barrier((pair, ready))
    four = jnp.stack([pair, move(pair, dy=-1), move(pair, dy=2), move(pair, dy=1)])
    return jnp.stack([four, move(four, dc=1)])


def cycle_kernel(slab, blocks, out, turned):
    spot = lax.axis_index("blk")
    y, x, c = spot // (NX * NC), (spot // NC) % NX, spot % NC
    width = blocks.shape[-1]
    pairs = slab.shape[0]
    for block in range(NY * NX * NC):
        dy = (block // (NX * NC) + NY - y) % NY
        e = (block // NC + NX - x) % NX
        g = (block + NC - c) % NC
        term = jnp.dot(slab[...], blocks[g, dy, e], preferred_element_type=jnp.float32)
        turned[block * width : (block + 1) * width, :] = term.T
    a_all = pairs // (2 * out.shape[0])
    for b in range(SB):
        rows = turned[pl.ds(b, OW, stride=SB), :].T
        for i in range(0, pairs // a_all, 2):
            both = [rows[at * a_all : (at + 1) * a_all] for at in (i, i + 1)]
            out[i // 2, pl.ds(b, a_all, stride=SB), :] = jnp.concatenate(both, axis=1)


def cycle_sums(slab_amplitudes, blocks):
    k_local, i_local, ac = slab_amplitudes.shape
    a_all = ac // SB
    slab = slab_amplitudes.reshape(k_local, i_local, a_all, SB).transpose(1, 2, 0, 3)
    slab = slab.reshape(i_local * a_all, k_local * SB)
    return pl.pallas_call(
        cycle_kernel,
        out_shape=jax.ShapeDtypeStruct((i_local // 2, a_all * SB, 2 * OW), jnp.float32),
        in_specs=[pl.BlockSpec(memory_space=pltpu.VMEM)] * 2,
        out_specs=pl.BlockSpec(memory_space=pltpu.VMEM),
        scratch_shapes=[pltpu.VMEM((OW * SB, i_local * a_all), jnp.float32)],
        compiler_params=pltpu.CompilerParams(vmem_limit_bytes=16 * MIB),
        cost_estimate=pl.CostEstimate(flops=1 << 28, bytes_accessed=1 << 23, transcendentals=0),
        name="cycle",
    )(slab, blocks)


def sum_rows(parts):
    total = parts[0]
    for dz in range(1, NZ):
        total = total + move_row(parts[dz], dz=dz)
    return total[0] + move_row(total[1], dx=1)


def per_device(amplitudes, integrals, live_pairs, slab_amplitudes, cycle_integrals):
    x0, y0 = pick_live(live_pairs, integrals.T)
    y_below, y_above, x1 = move(y0, dy=1), move(y0, dy=-1), move(x0, dx=1)
    y1 = move(y0, dx=1)
    slab_amplitudes, _ = lax.optimization_barrier((slab_amplitudes, x1))
    y_far = jnp.stack([move(y_below[0], dy=1), move(y_above[1], dy=-1)])
    x_pair = jnp.stack([x0, x1])
    x_below, x_above = move(x_pair, dy=1), move(x_pair, dy=-1)
    cycle_blocks = gather_cycle(cycle_integrals, x1)
    y_near = jnp.stack([y_below, y_above])
    y_near_1 = move(y_near, dx=1)
    amplitudes, _ = lax.optimization_barrier((amplitudes, y_far))
    live_amps = load_live(live_pairs, amplitudes, y0)
    x_far = jnp.stack([move(x_below[0], dy=1), move(x_above[1], dy=-1)])
    y_far_1 = move(y_far, dx=1)
    cycle = cycle_sums(slab_amplitudes, cycle_blocks)

    def cores(array, spots):
        return [
            (both, [(index, slot, dy, e, g) for index, slot, dy, e in spots])
            for g, both in enumerate((array, move(array, dc=1)))
        ]

    first = []
    for dy, array in ((0, x_pair), (-1, x_below), (1, x_above), (2, x_far)):
        first += cores(array, [((e, n), n, dy, e) for e in range(2) for n in range(2)])
    first = sum_rows(ladder(0, live_amps, cycle, first))

    second = []
    for e, array in enumerate((y0, y1)):
        second += cores(array, [((n,), n, 0, e) for n in range(2)])
    for e, array in enumerate((y_near, y_near_1)):
        second += cores(array, [((d, n), n, dy, e) for d, dy in enumerate((-1, 1)) for n in range(2)])
    for e, array in enumerate((y_far, y_far_1)):
        second += cores(array, [((n,), n, 2, e) for n in range(2)])
    second = sum_rows(ladder(1, live_amps, cycle, second))

    rows = amplitudes.shape[0]
    out = jnp.stack([first.reshape(NC, HALF, rows), second.reshape(NC, HALF, rows)], axis=1)
    return out.reshape(NC * SB, rows).astype(jnp.bfloat16).T


def solution(mesh):
    return jax.shard_map(
        per_device,
        mesh=mesh,
        in_specs=(
            P("blk", "row"),
            P("row", "blk"),
            P("row"),
            P("row", "blk", None),
            P("row", "blk"),
        ),
        out_specs=P("blk", "row"),
        check_vma=False,
    )
```

time: 140 us -> 102 us (0.73)
  starting transfers between devices: 0.04 us -> 41.1 us
  waiting for transfers between devices: 65.9 us -> 41.1 us
  blocking collectives: 24.3 us -> 0 us
  between operations: 18.3 us -> 0.27 us
  Pallas kernels: 0 us -> 13.5 us
  matrix products: 12.2 us -> 0 us
  local copies, waits for them, and re-layouts: 15.6 us -> 3.69 us
    all_gather x2 -> x0, waiting for transfers between devices: 65.8 us -> none  [the longest x1 50.7 us: per_device(): gathered = lax.all_gather(live_columns, 'blk', axis=0, tiled=True)]
    ppermute x0 -> x35, waiting for transfers between devices: none -> 41.1 us  [the longest x27 22.6 us: move(): return lax.ppermute(value, 'blk', blk_moves(dy, dx, dc))]
    ppermute x0 -> x35, starting transfers between devices: none -> 41.1 us  [the longest x27 24.6 us: move(): return lax.ppermute(value, 'blk', blk_moves(dy, dx, dc))]
    all_to_all x1 -> x0, blocking collectives: 24.3 us -> none  [per_device(): lax.all_to_all(partial_sums.reshape(rows, -1, partial_sums.shape[1]), 'ro...]
    pallas_call x0 -> x5, Pallas kernels: none -> 13.5 us  [the longest x2 4.81 us: ladder(): pl.pallas_call(functools.partial(ladder_kernel, places, len(arrays), half...]
    dot_general x2 -> x0, matrix products: 12.2 us -> none  [the longest x1 9.56 us: per_device(): lax.dot_general(gathered, live_amps, (((1,), (1,)), ((), ())), preferred_...]
    dynamic_slice x2 -> x0, local copies, waits for them, and re-layouts: 9.08 us -> none  [the longest x1 7.84 us: per_device(): lax.dynamic_slice_in_dim(amplitudes, order[n] * tile, tile, 1)]
    another operation x0 -> x10, other arithmetic: none -> 2.2 us  [the longest x1 1 us: per_device(): x_pair = jnp.stack([x0, x1])]
  transfers between devices with their start and end apart: 2 -> 35, of which waited for: 2 -> 12; matrix products, arithmetic and copies ran while one was open for 14% -> 4% of each run, Pallas kernels for 0% -> 8%
where the time goes in v2:
time: 102 us
  starting transfers between devices  41.1 us (40%)
  waiting for transfers between devices  41.1 us (40%)
  Pallas kernels  13.5 us (13%)
  local copies, waits for them, and re-layouts  3.69 us (4%)
  other arithmetic  2.27 us (2%)
    ppermute x27, starting transfers between devices, move(): return lax.ppermute(value, 'blk', blk_moves(dy, dx, dc))  24.6 us
    ppermute x27, waiting for transfers between devices, move(): return lax.ppermute(value, 'blk', blk_moves(dy, dx, dc))  22.6 us
    ppermute x8, waiting for transfers between devices, move_row(): return lax.ppermute(value, 'row', row_moves(dz, dx))  18.5 us
    ppermute x8, starting transfers between devices, move_row(): return lax.ppermute(value, 'row', row_moves(dz, dx))  16.6 us
    pallas_call x2, Pallas kernels, ladder(): pl.pallas_call(functools.partial(ladder_kernel, places, len(arrays), half...  4.81 us
    pallas_call x1, Pallas kernels, load_live(): pl.pallas_call(load_kernel, out_shape=jax.ShapeDtypeStruct((2 * KT, rows,...  4.05 us
    pallas_call x1, Pallas kernels, pick_live(): pl.pallas_call(pick_kernel, out_shape=(shape, shape), in_specs=[pl.BlockS...  2.6 us
    pallas_call x1, Pallas kernels, cycle_sums(): pl.pallas_call(cycle_kernel, out_shape=jax.ShapeDtypeStruct((i_local // 2...  2.07 us
  transfers between devices with their start and end apart: 35, of which 12 were waited for; matrix products, arithmetic and copies ran while one was open for 4% of the time, Pallas kernels for 8%

profile of v2, /device:TPU:0, one launch (start us, length us, event | category | flops | bytes accessed | tf_op | source)
XLA Modules:
  0.0 102.0 jit_solution(1249770493611490249)
XLA Ops:
  0.0 2.6 %pick_live.1 = (bf16[2,16,4096]{2,1,0:T(8,128)(2,1)}, bf16[2,16,4096]{2,1,0:T(8,128)(2,1)}) custom-call(s32[4]{0:T(128)} %live.3, bf16[32,16384]{1,0:T(8,128)(2,1)} %bitcast.53), custom_call_target="tpu_custom_call" | custom-call | tf_op jit(solution)/shard_map/pick_live/pallas_call | solution.py:66
  2.6 1.7 %collective-permute-start.4 = (bf16[2,16,4096]{2,1,0:T(8,128)(2,1)}, bf16[2,16,4096]{2,1,0:T(8,128)(2,1)S(1)}, u32[]{:S(2)}, u32[]{:S(2)}) collective-permute-start(bf16[2,16,4096]{2,1,0:T(8,128)(2,1)} %get-tuple-element.20), channel_id=1, source_target_pairs={{0,2},{1,3},{2,0},{3,1},{4,6},{5,7},{6,4},{7,5},{8,10},{9,11},{10,... | collective-permute-start | bytes 786440 | tf_op jit(solution)/shard_map/ppermute | solution.py:35
  4.3 3.0 %collective-permute-start.2 = (bf16[2,16,4096]{2,1,0:T(8,128)(2,1)}, bf16[2,16,4096]{2,1,0:T(8,128)(2,1)S(1)}, u32[]{:S(2)}, u32[]{:S(2)}) collective-permute-start(bf16[2,16,4096]{2,1,0:T(8,128)(2,1)} %get-tuple-element.18.after.refs_0_), channel_id=1, source_target_pairs={{0,12},{1,13},{2,14},{3,15},{4,0},{5,1},{6,2},{7,3},{8,4},{9,5},{1... | collective-permute-start | bytes 786440 | tf_op jit(solution)/shard_map/ppermute | solution.py:35
  7.3 0.5 collective-permute-start.5
  7.8 0.0 collective-permute-start
  7.8 1.5 %collective-permute-start.23 = (bf16[2,16,4096]{2,1,0:T(8,128)(2,1)}, bf16[2,16,4096]{2,1,0:T(8,128)(2,1)S(1)}, u32[]{:S(2)}, u32[]{:S(2)}) collective-permute-start(bf16[2,16,4096]{2,1,0:T(8,128)(2,1)} %get-tuple-element.18.after.refs_0_), channel_id=1, source_target_pairs={{0,2},{1,3},{2,0},{3,1},{4,6},{5,7},{6,4},{7,5},{8,10},{9,11},{10,... | collective-permute-start | bytes 786440 | tf_op jit(solution)/shard_map/ppermute | solution.py:35
  9.3 4.2 %collective-permute-done.5 = bf16[256,128]{1,0:T(8,128)(2,1)S(1)} collective-permute-done((bf16[256,128]{1,0:T(8,128)(2,1)}, bf16[256,128]{1,0:T(8,128)(2,1)S(1)}, u32[]{:S(2)}, u32[]{:S(2)}) %collective-permute-start.5) | collective-permute-done | bytes 65568 | tf_op jit(solution)/shard_map/ppermute | solution.py:35
  13.5 0.9 pad_maximum_fusion.6
  14.4 0.0 collective-permute-done.4
  14.4 1.7 %collective-permute-start.8 = (bf16[2,256,128]{2,1,0:T(8,128)(2,1)S(1)}, bf16[2,256,128]{2,1,0:T(8,128)(2,1)S(1)}, u32[]{:S(2)}, u32[]{:S(2)}) collective-permute-start(bf16[2,256,128]{2,1,0:T(8,128)(2,1)S(1)} %pad_maximum_fusion.6), channel_id=1, source_target_pairs={{0,4},{1,5},{2,6},{3,7},{4,8},{5,9},{6,10},{7,11},{8,12},{9,13},{1... | collective-permute-start | bytes 393224 | tf_op jit(solution)/shard_map/ppermute | solution.py:35
  16.1 2.9 %collective-permute-start.7 = (bf16[2,256,128]{2,1,0:T(8,128)(2,1)S(1)}, bf16[2,256,128]{2,1,0:T(8,128)(2,1)S(1)}, u32[]{:S(2)}, u32[]{:S(2)}) collective-permute-start(bf16[2,256,128]{2,1,0:T(8,128)(2,1)S(1)} %pad_maximum_fusion.6), channel_id=1, source_target_pairs={{0,8},{1,9},{2,10},{3,11},{4,12},{5,13},{6,14},{7,15},{8,0},{9,1},... | collective-permute-start | bytes 393224 | tf_op jit(solution)/shard_map/ppermute | solution.py:35
  19.0 0.0 collective-permute-done.2
  19.0 1.4 %collective-permute-start.3 = (bf16[16,4096]{1,0:T(8,128)(2,1)S(1)}, bf16[16,4096]{1,0:T(8,128)(2,1)S(1)}, u32[]{:S(2)}, u32[]{:S(2)}) collective-permute-start(bf16[16,4096]{1,0:T(8,128)(2,1)S(1)} %slice_bitcast_fusion.2), channel_id=1, source_target_pairs={{0,12},{1,13},{2,14},{3,15},{4,0},{5,1},{6,2},{7,3},{8,4},{9,5},{1... | collective-permute-start | bytes 393224 | tf_op jit(solution)/shard_map/ppermute | solution.py:35
  20.4 0.7 collective-permute-start.1
  21.2 0.1 pad_maximum_fusion.4.refs_4_
  21.2 1.0 pad_maximum_fusion.2.refs_0_
  22.2 1.0 %reshape.8 = bf16[8,8,16,32]{3,2,1,0:T(8,128)(2,1)S(1)} reshape(bf16[8,8,512]{2,1,0:T(8,128)(2,1)} %param.8) | data formatting | bytes 131072 | tf_op jit(solution)/shard_map/reshape | solution.py:186
  23.3 0.2 copy.9
  23.5 0.2 reshape.9.slab
  23.7 1.2 %collective-permute-done.3 = bf16[16,4096]{1,0:T(8,128)(2,1)S(1)} collective-permute-done((bf16[16,4096]{1,0:T(8,128)(2,1)S(1)}, bf16[16,4096]{1,0:T(8,128)(2,1)S(1)}, u32[]{:S(2)}, u32[]{:S(2)}) %collective-permute-start.3) | collective-permute-done | bytes 131104 | tf_op jit(solution)/shard_map/ppermute | solution.py:35
  24.9 1.7 %collective-permute-start.6 = (bf16[2,256,128]{2,1,0:T(8,128)(2,1)S(1)}, bf16[2,256,128]{2,1,0:T(8,128)(2,1)S(1)}, u32[]{:S(2)}, u32[]{:S(2)}) collective-permute-start(bf16[2,256,128]{2,1,0:T(8,128)(2,1)S(1)} %pad_maximum_fusion.6), channel_id=1, source_target_pairs={{0,12},{1,13},{2,14},{3,15},{4,0},{5,1},{6,2},{7,3},{8,4},{9,5},{1... | collective-permute-start | bytes 393224 | tf_op jit(solution)/shard_map/ppermute | solution.py:35
  26.6 0.1 collective-permute-done.1
  26.7 0.7 collective-permute-start.13
  27.5 0.9 copy-done
  28.4 0.7 copy-done.1
  29.1 4.0 %load_live.1.amps = bf16[8,512,1024]{2,1,0:T(8,128)(2,1)S(1)} custom-call(s32[4]{0:T(128)S(1)} %copy-done.1, bf16[512,16384]{1,0:T(8,128)(2,1)} %amps, bf16[2,16,4096]{2,1,0:T(8,128)(2,1)S(1)} %copy-done), custom_call_target="tpu_custom_call" | custom-call | tf_op jit(solution)/shard_map/load_live/pallas_call | solution.py:91
  33.1 0.1 collective-permute-start.22
  33.2 1.4 %collective-permute-start.11 = (bf16[2,2,16,4096]{3,2,1,0:T(8,128)(2,1)S(1)}, bf16[2,2,16,4096]{3,2,1,0:T(8,128)(2,1)S(1)}, u32[]{:S(2)}, u32[]{:S(2)}) collective-permute-start(bf16[2,2,16,4096]{3,2,1,0:T(8,128)(2,1)S(1)} %pad_maximum_fusion.2.refs_0_), channel_id=1, source_target_pairs={{0,4},{1,5},{2,6},{3,7},{4,8},{5,9},{6,10},{7,11},{8,12},{9,13},{1... | collective-permute-start | bytes 1572872 | tf_op jit(solution)/shard_map/ppermute | solution.py:35
  34.6 0.0 collective-permute-done.7
  34.6 1.5 %collective-permute-start.26 = (bf16[2,2,16,4096]{3,2,1,0:T(8,128)(2,1)S(1)}, bf16[2,2,16,4096]{3,2,1,0:T(8,128)(2,1)S(1)}, u32[]{:S(2)}, u32[]{:S(2)}) collective-permute-start(bf16[2,2,16,4096]{3,2,1,0:T(8,128)(2,1)S(1)} %pad_maximum_fusion.4.refs_4_), channel_id=1, source_target_pairs={{0,2},{1,3},{2,0},{3,1},{4,6},{5,7},{6,4},{7,5},{8,10},{9,11},{10,... | collective-permute-start | bytes 1572872 | tf_op jit(solution)/shard_map/ppermute | solution.py:35
  36.1 0.1 fusion.4
  36.2 1.9 %collective-permute-done.13.refs_4_ = bf16[2,2,16,4096]{3,2,1,0:T(8,128)(2,1)S(1)} collective-permute-done((bf16[2,2,16,4096]{3,2,1,0:T(8,128)(2,1)S(1)}, bf16[2,2,16,4096]{3,2,1,0:T(8,128)(2,1)S(1)}, u32[]{:S(2)}, u32[]{:S(2)}) %collective-permute-start.13) | collective-permute-done | bytes 524320 | tf_op jit(solution)/shard_map/ppermute | solution.py:35
  38.1 1.5 %collective-permute-start.29 = (bf16[2,16,4096]{2,1,0:T(8,128)(2,1)S(1)}, bf16[2,16,4096]{2,1,0:T(8,128)(2,1)S(1)}, u32[]{:S(2)}, u32[]{:S(2)}) collective-permute-start(bf16[2,16,4096]{2,1,0:T(8,128)(2,1)S(1)} %pad_maximum_fusion.5.refs_8_), channel_id=1, source_target_pairs={{0,2},{1,3},{2,0},{3,1},{4,6},{5,7},{6,4},{7,5},{8,10},{9,11},{10,... | collective-permute-start | bytes 786440 | tf_op jit(solution)/shard_map/ppermute | solution.py:35
  39.6 0.1 collective-permute-start.25
  39.7 0.5 collective-permute-start.28
  40.2 14.0 %collective-permute-done.29.refs_10_ = bf16[2,16,4096]{2,1,0:T(8,128)(2,1)S(1)} collective-permute-done((bf16[2,16,4096]{2,1,0:T(8,128)(2,1)S(1)}, bf16[2,16,4096]{2,1,0:T(8,128)(2,1)S(1)}, u32[]{:S(2)}, u32[]{:S(2)}) %collective-permute-start.29) | collective-permute-done | bytes 262176 | tf_op jit(solution)/shard_map/ppermute | solution.py:35
  54.2 0.5 collective-permute-start.30
  54.7 0.1 collective-permute-start.27
  54.8 2.0 %collective-permute-start.16 = (bf16[2,16,4096]{2,1,0:T(8,128)(2,1)S(1)}, bf16[2,16,4096]{2,1,0:T(8,128)(2,1)S(1)}, u32[]{:S(2)}, u32[]{:S(2)}) collective-permute-start(bf16[2,16,4096]{2,1,0:T(8,128)(2,1)S(1)} %slice_bitcast_fusion), channel_id=1, source_target_pairs={{0,12},{1,13},{2,14},{3,15},{4,0},{5,1},{6,2},{7,3},{8,4},{9,5},{1... | collective-permute-start | bytes 786440 | tf_op jit(solution)/shard_map/ppermute | solution.py:35
  56.8 0.1 collective-permute-start.15
  56.9 0.1 pad_maximum_fusion.blocks
  57.0 2.1 %cycle.1 = f32[4,512,128]{2,1,0:T(8,128)S(1)} custom-call(bf16[128,256]{1,0:T(8,128)(2,1)S(1)} %reshape.9.slab, bf16[2,4,2,256,128]{4,3,2,1,0:T(8,128)(2,1)S(1)} %pad_maximum_fusion.blocks), custom_call_target="tpu_custom_call" | custom-call | flops 268435456 | bytes 8388608 | tf_op jit(solution)/shard_map/cycle/pallas_call | solution.py:188
  59.1 0.2 collective-permute-start.10
  59.3 0.4 collective-permute-start.12
  59.7 0.3 collective-permute-start.14
  60.0 2.4 %ladder.3 = (f32[2,32,512]{2,1,0:T(8,128)S(1)}, f32[2,32,512]{2,1,0:T(8,128)S(1)}, f32[2,32,512]{2,1,0:T(8,128)S(1)}, f32[2,32,512]{2,1,0:T(8,128)S(1)}) custom-call(bf16[8,512,1024]{2,1,0:T(8,128)(2,1)S(1)} %load_live.1.amps, f32[4,512,128]{2,1,0:T(8,128)S(1)} %cycle.1, bf16[2,16,4096]{2,1,0:T(8,128)(2,1)S(1)} %copy-done, ...), custom_call_target="tpu_custom_call" | custom-call | flops 2147483648 | bytes 4194304 | tf_op jit(solution)/shard_map/ladder/pallas_call | solution.py:143
  62.4 1.2 %collective-permute-done.16 = bf16[2,16,4096]{2,1,0:T(8,128)(2,1)S(1)} collective-permute-done((bf16[2,16,4096]{2,1,0:T(8,128)(2,1)S(1)}, bf16[2,16,4096]{2,1,0:T(8,128)(2,1)S(1)}, u32[]{:S(2)}, u32[]{:S(2)}) %collective-permute-start.16) | collective-permute-done | bytes 262176 | tf_op jit(solution)/shard_map/ppermute | solution.py:35
  63.6 4.0 %collective-permute-start.33 = (f32[2,32,512]{2,1,0:T(8,128)S(1)}, f32[2,32,512]{2,1,0:T(8,128)S(1)}, u32[]{:S(2)}, u32[]{:S(2)}) collective-permute-start(f32[2,32,512]{2,1,0:T(8,128)S(1)} %get-tuple-element.30), channel_id=1, source_target_pairs={{0,96},{16,112},{32,0},{48,16},{64,32},{80,48},{96,64},{112,80},{1... | collective-permute-start | bytes 393224 | tf_op jit(solution)/shard_map/ppermute | solution.py:39
  67.6 0.1 pad_maximum_fusion.3.refs_6_
  67.6 0.1 collective-permute-start.17
  67.7 2.4 %collective-permute-done.33 = f32[2,32,512]{2,1,0:T(8,128)S(1)} collective-permute-done((f32[2,32,512]{2,1,0:T(8,128)S(1)}, f32[2,32,512]{2,1,0:T(8,128)S(1)}, u32[]{:S(2)}, u32[]{:S(2)}) %collective-permute-start.33) | collective-permute-done | bytes 131104 | tf_op jit(solution)/shard_map/ppermute | solution.py:39
  70.2 2.3 %collective-permute-start.32 = (f32[2,32,512]{2,1,0:T(8,128)S(1)}, f32[2,32,512]{2,1,0:T(8,128)S(1)}, u32[]{:S(2)}, u32[]{:S(2)}) collective-permute-start(f32[2,32,512]{2,1,0:T(8,128)S(1)} %get-tuple-element.29), channel_id=1, source_target_pairs={{0,64},{16,80},{32,96},{48,112},{64,0},{80,16},{96,32},{112,48},{1... | collective-permute-start | bytes 393224 | tf_op jit(solution)/shard_map/ppermute | solution.py:39
  72.5 4.1 %collective-permute-done.32 = f32[2,32,512]{2,1,0:T(8,128)S(1)} collective-permute-done((f32[2,32,512]{2,1,0:T(8,128)S(1)}, f32[2,32,512]{2,1,0:T(8,128)S(1)}, u32[]{:S(2)}, u32[]{:S(2)}) %collective-permute-start.32) | collective-permute-done | bytes 131104 | tf_op jit(solution)/shard_map/ppermute | solution.py:39
  76.6 1.0 %collective-permute-start.31 = (f32[2,32,512]{2,1,0:T(8,128)S(1)}, f32[2,32,512]{2,1,0:T(8,128)S(1)}, u32[]{:S(2)}, u32[]{:S(2)}) collective-permute-start(f32[2,32,512]{2,1,0:T(8,128)S(1)} %get-tuple-element.28), channel_id=1, source_target_pairs={{0,32},{16,48},{32,64},{48,80},{64,96},{80,112},{96,0},{112,16},{1... | collective-permute-start | bytes 393224 | tf_op jit(solution)/shard_map/ppermute | solution.py:39
  77.7 5.6 %collective-permute-done.31 = f32[2,32,512]{2,1,0:T(8,128)S(1)} collective-permute-done((f32[2,32,512]{2,1,0:T(8,128)S(1)}, f32[2,32,512]{2,1,0:T(8,128)S(1)}, u32[]{:S(2)}, u32[]{:S(2)}) %collective-permute-start.31) | collective-permute-done | bytes 131104 | tf_op jit(solution)/shard_map/ppermute | solution.py:39
  83.3 2.4 %ladder.2 = (f32[2,32,512]{2,1,0:T(8,128)S(1)}, f32[2,32,512]{2,1,0:T(8,128)S(1)}, f32[2,32,512]{2,1,0:T(8,128)S(1)}, f32[2,32,512]{2,1,0:T(8,128)S(1)}) custom-call(bf16[8,512,1024]{2,1,0:T(8,128)(2,1)S(1)} %load_live.1.amps, f32[4,512,128]{2,1,0:T(8,128)S(1)} %cycle.1, bf16[2,2,16,4096]{3,2,1,0:T(8,128)(2,1)S(1)} %pad_maximum_fusion.2.refs_0_, ...), custom_call_target="tpu_custom_call" | custom-call | flops 2147483648 | bytes 4194304 | tf_op jit(solution)/shard_map/ladder/pallas_call | solution.py:143
  85.8 2.1 %collective-permute-start.20 = (f32[2,32,512]{2,1,0:T(8,128)S(1)}, f32[2,32,512]{2,1,0:T(8,128)S(1)}, u32[]{:S(2)}, u32[]{:S(2)}) collective-permute-start(f32[2,32,512]{2,1,0:T(8,128)S(1)} %get-tuple-element.26), channel_id=1, source_target_pairs={{0,96},{16,112},{32,0},{48,16},{64,32},{80,48},{96,64},{112,80},{1... | collective-permute-start | bytes 393224 | tf_op jit(solution)/shard_map/ppermute | solution.py:39
  87.9 0.9 collective-permute-start.18
  88.8 3.0 %collective-permute-start.34 = (f32[32,512]{1,0:T(8,128)S(1)}, f32[32,512]{1,0:T(8,128)S(1)}, u32[]{:S(2)}, u32[]{:S(2)}) collective-permute-start(f32[32,512]{1,0:T(8,128)S(1)} %slice_bitcast_fusion.4), channel_id=1, source_target_pairs={{0,16},{16,0},{32,48},{48,32},{64,80},{80,64},{96,112},{112,96},{1... | collective-permute-start | bytes 196616 | tf_op jit(solution)/shard_map/ppermute | solution.py:39
  91.8 2.6 %collective-permute-done.19 = f32[2,32,512]{2,1,0:T(8,128)S(1)} collective-permute-done((f32[2,32,512]{2,1,0:T(8,128)S(1)}, f32[2,32,512]{2,1,0:T(8,128)S(1)}, u32[]{:S(2)}, u32[]{:S(2)}) %collective-permute-start.19) | collective-permute-done | bytes 131104 | tf_op jit(solution)/shard_map/ppermute | solution.py:39
  94.4 1.0 collective-permute-done.18
  95.5 3.1 %collective-permute-start.21 = (f32[32,512]{1,0:T(8,128)S(1)}, f32[32,512]{1,0:T(8,128)S(1)}, u32[]{:S(2)}, u32[]{:S(2)}) collective-permute-start(f32[32,512]{1,0:T(8,128)S(1)} %slice_bitcast_fusion.6), channel_id=1, source_target_pairs={{0,16},{16,0},{32,48},{48,32},{64,80},{80,64},{96,112},{112,96},{1... | collective-permute-start | bytes 196616 | tf_op jit(solution)/shard_map/ppermute | solution.py:39
  98.6 2.7 %collective-permute-done.21 = f32[32,512]{1,0:T(8,128)S(1)} collective-permute-done((f32[32,512]{1,0:T(8,128)S(1)}, f32[32,512]{1,0:T(8,128)S(1)}, u32[]{:S(2)}, u32[]{:S(2)}) %collective-permute-start.21) | collective-permute-done | bytes 65568 | tf_op jit(solution)/shard_map/ppermute | solution.py:39
  101.4 0.6 copy.7
  (37 shorter events, 0.3 us)
Async XLA Ops:
  2.6 11.8 %collective-permute-start.4 = (bf16[2,16,4096]{2,1,0:T(8,128)(2,1)}, bf16[2,16,4096]{2,1,0:T(8,128)(2,1)S(1)}, u32[]{:S(2)}, u32[]{:S(2)}) collective-permute-start(bf16[2,16,4096]{2,1,0:T(8,128)(2,1)} %get-tuple-element.20), channel_id=1, source_target_pairs={{0,2},{1,3},{2,0},{3,1},{4,6},{5,7},{6,4},{7,5},{8,10},{9,11},{10,... | collective-permute-start | bytes 786440 | tf_op jit(solution)/shard_map/ppermute | solution.py:35
  4.3 14.7 %collective-permute-start.2 = (bf16[2,16,4096]{2,1,0:T(8,128)(2,1)}, bf16[2,16,4096]{2,1,0:T(8,128)(2,1)S(1)}, u32[]{:S(2)}, u32[]{:S(2)}) collective-permute-start(bf16[2,16,4096]{2,1,0:T(8,128)(2,1)} %get-tuple-element.18.after.refs_0_), channel_id=1, source_target_pairs={{0,12},{1,13},{2,14},{3,15},{4,0},{5,1},{6,2},{7,3},{8,4},{9,5},{1... | collective-permute-start | bytes 786440 | tf_op jit(solution)/shard_map/ppermute | solution.py:35
  7.3 6.2 %collective-permute-start.5 = (bf16[256,128]{1,0:T(8,128)(2,1)}, bf16[256,128]{1,0:T(8,128)(2,1)S(1)}, u32[]{:S(2)}, u32[]{:S(2)}) collective-permute-start(bf16[256,128]{1,0:T(8,128)(2,1)} %param.9), channel_id=1, source_target_pairs={{0,2},{1,3},{2,0},{3,1},{4,6},{5,7},{6,4},{7,5},{8,10},{9,11},{10,... | collective-permute-start | bytes 196616 | tf_op jit(solution)/shard_map/ppermute | solution.py:35
  7.8 12.6 %collective-permute-start = (bf16[2,16,4096]{2,1,0:T(8,128)(2,1)}, bf16[2,16,4096]{2,1,0:T(8,128)(2,1)S(1)}, u32[]{:S(2)}, u32[]{:S(2)}) collective-permute-start(bf16[2,16,4096]{2,1,0:T(8,128)(2,1)} %get-tuple-element.18.after.refs_0_), channel_id=1, source_target_pairs={{0,4},{1,5},{2,6},{3,7},{4,8},{5,9},{6,10},{7,11},{8,12},{9,13},{1... | collective-permute-start | bytes 786440 | tf_op jit(solution)/shard_map/ppermute | solution.py:35
  7.8 25.3 %collective-permute-start.23 = (bf16[2,16,4096]{2,1,0:T(8,128)(2,1)}, bf16[2,16,4096]{2,1,0:T(8,128)(2,1)S(1)}, u32[]{:S(2)}, u32[]{:S(2)}) collective-permute-start(bf16[2,16,4096]{2,1,0:T(8,128)(2,1)} %get-tuple-element.18.after.refs_0_), channel_id=1, source_target_pairs={{0,2},{1,3},{2,0},{3,1},{4,6},{5,7},{6,4},{7,5},{8,10},{9,11},{10,... | collective-permute-start | bytes 786440 | tf_op jit(solution)/shard_map/ppermute | solution.py:35
  14.4 18.8 %collective-permute-start.8 = (bf16[2,256,128]{2,1,0:T(8,128)(2,1)S(1)}, bf16[2,256,128]{2,1,0:T(8,128)(2,1)S(1)}, u32[]{:S(2)}, u32[]{:S(2)}) collective-permute-start(bf16[2,256,128]{2,1,0:T(8,128)(2,1)S(1)} %pad_maximum_fusion.6), channel_id=1, source_target_pairs={{0,4},{1,5},{2,6},{3,7},{4,8},{5,9},{6,10},{7,11},{8,12},{9,13},{1... | collective-permute-start | bytes 393224 | tf_op jit(solution)/shard_map/ppermute | solution.py:35
  16.1 18.5 %collective-permute-start.7 = (bf16[2,256,128]{2,1,0:T(8,128)(2,1)S(1)}, bf16[2,256,128]{2,1,0:T(8,128)(2,1)S(1)}, u32[]{:S(2)}, u32[]{:S(2)}) collective-permute-start(bf16[2,256,128]{2,1,0:T(8,128)(2,1)S(1)} %pad_maximum_fusion.6), channel_id=1, source_target_pairs={{0,8},{1,9},{2,10},{3,11},{4,12},{5,13},{6,14},{7,15},{8,0},{9,1},... | collective-permute-start | bytes 393224 | tf_op jit(solution)/shard_map/ppermute | solution.py:35
  19.0 5.9 %collective-permute-start.3 = (bf16[16,4096]{1,0:T(8,128)(2,1)S(1)}, bf16[16,4096]{1,0:T(8,128)(2,1)S(1)}, u32[]{:S(2)}, u32[]{:S(2)}) collective-permute-start(bf16[16,4096]{1,0:T(8,128)(2,1)S(1)} %slice_bitcast_fusion.2), channel_id=1, source_target_pairs={{0,12},{1,13},{2,14},{3,15},{4,0},{5,1},{6,2},{7,3},{8,4},{9,5},{1... | collective-permute-start | bytes 393224 | tf_op jit(solution)/shard_map/ppermute | solution.py:35
  20.4 6.2 %collective-permute-start.1 = (bf16[16,4096]{1,0:T(8,128)(2,1)S(1)}, bf16[16,4096]{1,0:T(8,128)(2,1)S(1)}, u32[]{:S(2)}, u32[]{:S(2)}) collective-permute-start(bf16[16,4096]{1,0:T(8,128)(2,1)S(1)} %slice_bitcast_fusion.3), channel_id=1, source_target_pairs={{0,4},{1,5},{2,6},{3,7},{4,8},{5,9},{6,10},{7,11},{8,12},{9,13},{1... | collective-permute-start | bytes 393224 | tf_op jit(solution)/shard_map/ppermute | solution.py:35
  24.9 11.2 %collective-permute-start.6 = (bf16[2,256,128]{2,1,0:T(8,128)(2,1)S(1)}, bf16[2,256,128]{2,1,0:T(8,128)(2,1)S(1)}, u32[]{:S(2)}, u32[]{:S(2)}) collective-permute-start(bf16[2,256,128]{2,1,0:T(8,128)(2,1)S(1)} %pad_maximum_fusion.6), channel_id=1, source_target_pairs={{0,12},{1,13},{2,14},{3,15},{4,0},{5,1},{6,2},{7,3},{8,4},{9,5},{1... | collective-permute-start | bytes 393224 | tf_op jit(solution)/shard_map/ppermute | solution.py:35
  26.7 11.4 %collective-permute-start.13 = (bf16[2,2,16,4096]{3,2,1,0:T(8,128)(2,1)S(1)}, bf16[2,2,16,4096]{3,2,1,0:T(8,128)(2,1)S(1)}, u32[]{:S(2)}, u32[]{:S(2)}) collective-permute-start(bf16[2,2,16,4096]{3,2,1,0:T(8,128)(2,1)S(1)} %pad_maximum_fusion.2.refs_0_), channel_id=1, source_target_pairs={{0,12},{1,13},{2,14},{3,15},{4,0},{5,1},{6,2},{7,3},{8,4},{9,5},{1... | collective-permute-start | bytes 1572872 | tf_op jit(solution)/shard_map/ppermute | solution.py:35
  27.4 1.0 copy-start
  28.4 0.7 copy-start.1
  33.1 6.5 %collective-permute-start.22 = (bf16[2,16,4096]{2,1,0:T(8,128)(2,1)S(1)}, bf16[2,16,4096]{2,1,0:T(8,128)(2,1)S(1)}, u32[]{:S(2)}, u32[]{:S(2)}) collective-permute-start(bf16[2,16,4096]{2,1,0:T(8,128)(2,1)S(1)} %copy-done), channel_id=1, source_target_pairs={{0,1},{1,0},{2,3},{3,2},{4,5},{5,4},{6,7},{7,6},{8,9},{9,8},{10,11... | collective-permute-start | bytes 786440 | tf_op jit(solution)/shard_map/ppermute | solution.py:35
  33.2 21.5 %collective-permute-start.11 = (bf16[2,2,16,4096]{3,2,1,0:T(8,128)(2,1)S(1)}, bf16[2,2,16,4096]{3,2,1,0:T(8,128)(2,1)S(1)}, u32[]{:S(2)}, u32[]{:S(2)}) collective-permute-start(bf16[2,2,16,4096]{3,2,1,0:T(8,128)(2,1)S(1)} %pad_maximum_fusion.2.refs_0_), channel_id=1, source_target_pairs={{0,4},{1,5},{2,6},{3,7},{4,8},{5,9},{6,10},{7,11},{8,12},{9,13},{1... | collective-permute-start | bytes 1572872 | tf_op jit(solution)/shard_map/ppermute | solution.py:35
  34.6 19.6 %collective-permute-start.26 = (bf16[2,2,16,4096]{3,2,1,0:T(8,128)(2,1)S(1)}, bf16[2,2,16,4096]{3,2,1,0:T(8,128)(2,1)S(1)}, u32[]{:S(2)}, u32[]{:S(2)}) collective-permute-start(bf16[2,2,16,4096]{3,2,1,0:T(8,128)(2,1)S(1)} %pad_maximum_fusion.4.refs_4_), channel_id=1, source_target_pairs={{0,2},{1,3},{2,0},{3,1},{4,6},{5,7},{6,4},{7,5},{8,10},{9,11},{10,... | collective-permute-start | bytes 1572872 | tf_op jit(solution)/shard_map/ppermute | solution.py:35
  36.1 3.6 %collective-permute-start.24 = (bf16[2,16,4096]{2,1,0:T(8,128)(2,1)S(1)}, bf16[2,16,4096]{2,1,0:T(8,128)(2,1)S(1)}, u32[]{:S(2)}, u32[]{:S(2)}) collective-permute-start(bf16[2,16,4096]{2,1,0:T(8,128)(2,1)S(1)} %collective-permute-done.23.refs_2_), channel_id=1, source_target_pairs={{0,1},{1,0},{2,3},{3,2},{4,5},{5,4},{6,7},{7,6},{8,9},{9,8},{10,11... | collective-permute-start | bytes 786440 | tf_op jit(solution)/shard_map/ppermute | solution.py:35
  38.1 16.1 %collective-permute-start.29 = (bf16[2,16,4096]{2,1,0:T(8,128)(2,1)S(1)}, bf16[2,16,4096]{2,1,0:T(8,128)(2,1)S(1)}, u32[]{:S(2)}, u32[]{:S(2)}) collective-permute-start(bf16[2,16,4096]{2,1,0:T(8,128)(2,1)S(1)} %pad_maximum_fusion.5.refs_8_), channel_id=1, source_target_pairs={{0,2},{1,3},{2,0},{3,1},{4,6},{5,7},{6,4},{7,5},{8,10},{9,11},{10,... | collective-permute-start | bytes 786440 | tf_op jit(solution)/shard_map/ppermute | solution.py:35
  39.6 19.5 %collective-permute-start.25 = (bf16[2,2,16,4096]{3,2,1,0:T(8,128)(2,1)S(1)}, bf16[2,2,16,4096]{3,2,1,0:T(8,128)(2,1)S(1)}, u32[]{:S(2)}, u32[]{:S(2)}) collective-permute-start(bf16[2,2,16,4096]{3,2,1,0:T(8,128)(2,1)S(1)} %pad_maximum_fusion.4.refs_4_), channel_id=1, source_target_pairs={{0,1},{1,0},{2,3},{3,2},{4,5},{5,4},{6,7},{7,6},{8,9},{9,8},{10,11... | collective-permute-start | bytes 1572872 | tf_op jit(solution)/shard_map/ppermute | solution.py:35
  39.7 15.1 %collective-permute-start.28 = (bf16[2,16,4096]{2,1,0:T(8,128)(2,1)S(1)}, bf16[2,16,4096]{2,1,0:T(8,128)(2,1)S(1)}, u32[]{:S(2)}, u32[]{:S(2)}) collective-permute-start(bf16[2,16,4096]{2,1,0:T(8,128)(2,1)S(1)} %pad_maximum_fusion.5.refs_8_), channel_id=1, source_target_pairs={{0,1},{1,0},{2,3},{3,2},{4,5},{5,4},{6,7},{7,6},{8,9},{9,8},{10,11... | collective-permute-start | bytes 786440 | tf_op jit(solution)/shard_map/ppermute | solution.py:35
  54.2 2.6 %collective-permute-start.9 = (bf16[4,2,256,128]{3,2,1,0:T(8,128)(2,1)S(1)}, bf16[4,2,256,128]{3,2,1,0:T(8,128)(2,1)S(1)}, u32[]{:S(2)}, u32[]{:S(2)}) collective-permute-start(bf16[4,2,256,128]{3,2,1,0:T(8,128)(2,1)S(1)} %get-tuple-element.32), channel_id=1, source_target_pairs={{0,1},{1,0},{2,3},{3,2},{4,5},{5,4},{6,7},{7,6},{8,9},{9,8},{10,11... | collective-permute-start | bytes 1572872 | tf_op jit(solution)/shard_map/ppermute | solution.py:35
  54.2 5.1 %collective-permute-start.30 = (bf16[2,16,4096]{2,1,0:T(8,128)(2,1)S(1)}, bf16[2,16,4096]{2,1,0:T(8,128)(2,1)S(1)}, u32[]{:S(2)}, u32[]{:S(2)}) collective-permute-start(bf16[2,16,4096]{2,1,0:T(8,128)(2,1)S(1)} %collective-permute-done.29.refs_10_), channel_id=1, source_target_pairs={{0,1},{1,0},{2,3},{3,2},{4,5},{5,4},{6,7},{7,6},{8,9},{9,8},{10,11... | collective-permute-start | bytes 786440 | tf_op jit(solution)/shard_map/ppermute | solution.py:35
  54.7 5.0 %collective-permute-start.27 = (bf16[2,2,16,4096]{3,2,1,0:T(8,128)(2,1)S(1)}, bf16[2,2,16,4096]{3,2,1,0:T(8,128)(2,1)S(1)}, u32[]{:S(2)}, u32[]{:S(2)}) collective-permute-start(bf16[2,2,16,4096]{3,2,1,0:T(8,128)(2,1)S(1)} %collective-permute-done.26.refs_6_), channel_id=1, source_target_pairs={{0,1},{1,0},{2,3},{3,2},{4,5},{5,4},{6,7},{7,6},{8,9},{9,8},{10,11... | collective-permute-start | bytes 1572872 | tf_op jit(solution)/shard_map/ppermute | solution.py:35
  54.8 8.7 %collective-permute-start.16 = (bf16[2,16,4096]{2,1,0:T(8,128)(2,1)S(1)}, bf16[2,16,4096]{2,1,0:T(8,128)(2,1)S(1)}, u32[]{:S(2)}, u32[]{:S(2)}) collective-permute-start(bf16[2,16,4096]{2,1,0:T(8,128)(2,1)S(1)} %slice_bitcast_fusion), channel_id=1, source_target_pairs={{0,12},{1,13},{2,14},{3,15},{4,0},{5,1},{6,2},{7,3},{8,4},{9,5},{1... | collective-permute-start | bytes 786440 | tf_op jit(solution)/shard_map/ppermute | solution.py:35
  56.8 10.7 %collective-permute-start.15 = (bf16[2,16,4096]{2,1,0:T(8,128)(2,1)S(1)}, bf16[2,16,4096]{2,1,0:T(8,128)(2,1)S(1)}, u32[]{:S(2)}, u32[]{:S(2)}) collective-permute-start(bf16[2,16,4096]{2,1,0:T(8,128)(2,1)S(1)} %slice_bitcast_fusion.1), channel_id=1, source_target_pairs={{0,4},{1,5},{2,6},{3,7},{4,8},{5,9},{6,10},{7,11},{8,12},{9,13},{1... | collective-permute-start | bytes 786440 | tf_op jit(solution)/shard_map/ppermute | solution.py:35
  59.1 24.2 %collective-permute-start.10 = (bf16[2,2,16,4096]{3,2,1,0:T(8,128)(2,1)S(1)}, bf16[2,2,16,4096]{3,2,1,0:T(8,128)(2,1)S(1)}, u32[]{:S(2)}, u32[]{:S(2)}) collective-permute-start(bf16[2,2,16,4096]{3,2,1,0:T(8,128)(2,1)S(1)} %pad_maximum_fusion.2.refs_0_), channel_id=1, source_target_pairs={{0,1},{1,0},{2,3},{3,2},{4,5},{5,4},{6,7},{7,6},{8,9},{9,8},{10,11... | collective-permute-start | bytes 1572872 | tf_op jit(solution)/shard_map/ppermute | solution.py:35
  59.3 24.0 %collective-permute-start.12 = (bf16[2,2,16,4096]{3,2,1,0:T(8,128)(2,1)S(1)}, bf16[2,2,16,4096]{3,2,1,0:T(8,128)(2,1)S(1)}, u32[]{:S(2)}, u32[]{:S(2)}) collective-permute-start(bf16[2,2,16,4096]{3,2,1,0:T(8,128)(2,1)S(1)} %collective-permute-done.11.refs_2_), channel_id=1, source_target_pairs={{0,1},{1,0},{2,3},{3,2},{4,5},{5,4},{6,7},{7,6},{8,9},{9,8},{10,11... | collective-permute-start | bytes 1572872 | tf_op jit(solution)/shard_map/ppermute | solution.py:35
  59.7 23.6 %collective-permute-start.14 = (bf16[2,2,16,4096]{3,2,1,0:T(8,128)(2,1)S(1)}, bf16[2,2,16,4096]{3,2,1,0:T(8,128)(2,1)S(1)}, u32[]{:S(2)}, u32[]{:S(2)}) collective-permute-start(bf16[2,2,16,4096]{3,2,1,0:T(8,128)(2,1)S(1)} %collective-permute-done.13.refs_4_), channel_id=1, source_target_pairs={{0,1},{1,0},{2,3},{3,2},{4,5},{5,4},{6,7},{7,6},{8,9},{9,8},{10,11... | collective-permute-start | bytes 1572872 | tf_op jit(solution)/shard_map/ppermute | solution.py:35
  63.6 6.6 %collective-permute-start.33 = (f32[2,32,512]{2,1,0:T(8,128)S(1)}, f32[2,32,512]{2,1,0:T(8,128)S(1)}, u32[]{:S(2)}, u32[]{:S(2)}) collective-permute-start(f32[2,32,512]{2,1,0:T(8,128)S(1)} %get-tuple-element.30), channel_id=1, source_target_pairs={{0,96},{16,112},{32,0},{48,16},{64,32},{80,48},{96,64},{112,80},{1... | collective-permute-start | bytes 393224 | tf_op jit(solution)/shard_map/ppermute | solution.py:39
  67.6 15.7 %collective-permute-start.17 = (bf16[2,2,16,4096]{3,2,1,0:T(8,128)(2,1)S(1)}, bf16[2,2,16,4096]{3,2,1,0:T(8,128)(2,1)S(1)}, u32[]{:S(2)}, u32[]{:S(2)}) collective-permute-start(bf16[2,2,16,4096]{3,2,1,0:T(8,128)(2,1)S(1)} %pad_maximum_fusion.3.refs_6_), channel_id=1, source_target_pairs={{0,1},{1,0},{2,3},{3,2},{4,5},{5,4},{6,7},{7,6},{8,9},{9,8},{10,11... | collective-permute-start | bytes 1572872 | tf_op jit(solution)/shard_map/ppermute | solution.py:35
  70.2 6.5 %collective-permute-start.32 = (f32[2,32,512]{2,1,0:T(8,128)S(1)}, f32[2,32,512]{2,1,0:T(8,128)S(1)}, u32[]{:S(2)}, u32[]{:S(2)}) collective-permute-start(f32[2,32,512]{2,1,0:T(8,128)S(1)} %get-tuple-element.29), channel_id=1, source_target_pairs={{0,64},{16,80},{32,96},{48,112},{64,0},{80,16},{96,32},{112,48},{1... | collective-permute-start | bytes 393224 | tf_op jit(solution)/shard_map/ppermute | solution.py:39
  76.6 6.6 %collective-permute-start.31 = (f32[2,32,512]{2,1,0:T(8,128)S(1)}, f32[2,32,512]{2,1,0:T(8,128)S(1)}, u32[]{:S(2)}, u32[]{:S(2)}) collective-permute-start(f32[2,32,512]{2,1,0:T(8,128)S(1)} %get-tuple-element.28), channel_id=1, source_target_pairs={{0,32},{16,48},{32,64},{48,80},{64,96},{80,112},{96,0},{112,16},{1... | collective-permute-start | bytes 393224 | tf_op jit(solution)/shard_map/ppermute | solution.py:39
  85.8 6.1 %collective-permute-start.20 = (f32[2,32,512]{2,1,0:T(8,128)S(1)}, f32[2,32,512]{2,1,0:T(8,128)S(1)}, u32[]{:S(2)}, u32[]{:S(2)}) collective-permute-start(f32[2,32,512]{2,1,0:T(8,128)S(1)} %get-tuple-element.26), channel_id=1, source_target_pairs={{0,96},{16,112},{32,0},{48,16},{64,32},{80,48},{96,64},{112,80},{1... | collective-permute-start | bytes 393224 | tf_op jit(solution)/shard_map/ppermute | solution.py:39
  87.9 6.6 %collective-permute-start.19 = (f32[2,32,512]{2,1,0:T(8,128)S(1)}, f32[2,32,512]{2,1,0:T(8,128)S(1)}, u32[]{:S(2)}, u32[]{:S(2)}) collective-permute-start(f32[2,32,512]{2,1,0:T(8,128)S(1)} %get-tuple-element.25), channel_id=1, source_target_pairs={{0,64},{16,80},{32,96},{48,112},{64,0},{80,16},{96,32},{112,48},{1... | collective-permute-start | bytes 393224 | tf_op jit(solution)/shard_map/ppermute | solution.py:39
  87.9 7.6 %collective-permute-start.18 = (f32[2,32,512]{2,1,0:T(8,128)S(1)}, f32[2,32,512]{2,1,0:T(8,128)S(1)}, u32[]{:S(2)}, u32[]{:S(2)}) collective-permute-start(f32[2,32,512]{2,1,0:T(8,128)S(1)} %get-tuple-element.24), channel_id=1, source_target_pairs={{0,32},{16,48},{32,64},{48,80},{64,96},{80,112},{96,0},{112,16},{1... | collective-permute-start | bytes 393224 | tf_op jit(solution)/shard_map/ppermute | solution.py:39
  88.8 9.8 %collective-permute-start.34 = (f32[32,512]{1,0:T(8,128)S(1)}, f32[32,512]{1,0:T(8,128)S(1)}, u32[]{:S(2)}, u32[]{:S(2)}) collective-permute-start(f32[32,512]{1,0:T(8,128)S(1)} %slice_bitcast_fusion.4), channel_id=1, source_target_pairs={{0,16},{16,0},{32,48},{48,32},{64,80},{80,64},{96,112},{112,96},{1... | collective-permute-start | bytes 196616 | tf_op jit(solution)/shard_map/ppermute | solution.py:39
  95.5 5.8 %collective-permute-start.21 = (f32[32,512]{1,0:T(8,128)S(1)}, f32[32,512]{1,0:T(8,128)S(1)}, u32[]{:S(2)}, u32[]{:S(2)}) collective-permute-start(f32[32,512]{1,0:T(8,128)S(1)} %slice_bitcast_fusion.6), channel_id=1, source_target_pairs={{0,16},{16,0},{32,48},{48,32},{64,80},{80,64},{96,112},{112,96},{1... | collective-permute-start | bytes 196616 | tf_op jit(solution)/shard_map/ppermute | solution.py:39

commit v3 on v2

v3 whole, which is shorter than its diff:
```python
import functools

import jax
import jax.numpy as jnp
from jax import lax
from jax.experimental import pallas as pl
from jax.experimental.pallas import tpu as pltpu
from jax.sharding import PartitionSpec as P

OW = 64
TS = 64
SB = 32
TILE = TS * TS
NY, NX, NC = 4, 2, 2
NZ, NH = 4, 2
HALF = SB // 2
STEP = 1024
KT = TILE // STEP
MIB = 1 << 20


def blk_moves(dy, dx, dc):
    spots = [(y, x, c) for y in range(NY) for x in range(NX) for c in range(NC)]
    index = lambda y, x, c: ((y % NY) * NX + x % NX) * NC + c % NC
    return [(index(y, x, c), index(y + dy, x + dx, c + dc)) for y, x, c in spots]


def row_moves(dz, dx):
    spots = [(z, x) for z in range(NZ) for x in range(NH)]
    index = lambda z, x: (z % NZ) * NH + x % NH
    return [(index(z, x), index(z + dz, x + dx)) for z, x in spots]


def move(value, dy=0, dx=0, dc=0):
    return lax.ppermute(value, "blk", blk_moves(dy, dx, dc))


def move_row(value, dz=0, dx=0):
    return lax.ppermute(value, "row", row_moves(dz, dx))


def together(*values):
    return lax.optimization_barrier(values)


def live_slot(live, n):
    if n == 0:
        return jnp.where(live[0] == 1, 0, jnp.where(live[1] == 1, 1, 2))
    return jnp.where(live[3] == 1, 3, jnp.where(live[2] == 1, 2, 1))


def pick_kernel(live, columns, out, sems):
    copies = []
    for n in range(2):
        start = pl.multiple_of(live_slot(live, n) * TILE, TILE)
        for h in range(2):
            source = columns.at[pl.ds(h * HALF, HALF), pl.ds(start, TILE)]
            copies.append(pltpu.make_async_copy(source, out.at[h, n], sems.at[n, h]))
    for copy in copies:
        copy.start()
    for copy in copies:
        copy.wait()


def pick_live(live_pairs, columns):
    return pl.pallas_call(
        pick_kernel,
        out_shape=jax.ShapeDtypeStruct((2, 2, HALF, TILE), columns.dtype),
        in_specs=[pl.BlockSpec(memory_space=pltpu.SMEM), pl.BlockSpec(memory_space=pl.ANY)],
        out_specs=pl.BlockSpec(memory_space=pltpu.VMEM),
        scratch_shapes=[pltpu.SemaphoreType.DMA((2, 2))],
        compiler_params=pltpu.CompilerParams(vmem_limit_bytes=4 * MIB),
        name="pick_live",
    )(live_pairs, columns)


def load_kernel(live, amps, out, token, sems):
    token[...] = jnp.zeros_like(token)
    copies = []
    for n in range(2):
        for k in range(KT):
            start = pl.multiple_of(live_slot(live, n) * TILE + k * STEP, STEP)
            at = n * KT + k
            copies.append(pltpu.make_async_copy(amps.at[:, pl.ds(start, STEP)], out.at[at], sems.at[at]))
    for copy in copies:
        copy.start()
    for copy in copies:
        copy.wait()


def load_live(live_pairs, amplitudes):
    rows = amplitudes.shape[0]
    return pl.pallas_call(
        load_kernel,
        out_shape=(
            jax.ShapeDtypeStruct((2 * KT, rows, STEP), amplitudes.dtype),
            jax.ShapeDtypeStruct((8, 128), jnp.float32),
        ),
        in_specs=[pl.BlockSpec(memory_space=pltpu.SMEM), pl.BlockSpec(memory_space=pl.ANY)],
        out_specs=(pl.BlockSpec(memory_space=pltpu.VMEM),) * 2,
        scratch_shapes=[pltpu.SemaphoreType.DMA((2 * KT,))],
        compiler_params=pltpu.CompilerParams(vmem_limit_bytes=40 * MIB),
        name="load_live",
    )(live_pairs, amplitudes)


def ladder_kernel(places, e, count, amps, cycle, before, *refs):
    pieces, outs, (token, total) = refs[:count], refs[count : count + NZ], refs[count + NZ :]
    token[...] = jnp.zeros_like(token)
    for n in range(2):
        held = {}
        for piece, index, slot, *place in places:
            if slot == n:
                held[tuple(place)] = pieces[piece].at[index] if index else pieces[piece]
        for k in range(KT):
            cols = slice(k * STEP, (k + 1) * STEP)
            block = jnp.concatenate(
                [held[dy, g, h][:, cols] for dy in range(NY) for g in range(NC) for h in range(2)]
            )
            term = lax.dot_general(
                block, amps[n * KT + k], (((1,), (1,)), ((), ())), preferred_element_type=jnp.float32
            )
            if n == k == 0:
                total[...] = term
            else:
                total[...] += term

    spot = lax.axis_index("blk")
    y, x, c = spot // (NX * NC), (spot // NC) % NX, spot % NC
    z = lax.axis_index("row") // NH
    for dz in range(NZ):
        dy = (z + dz + NY - y) % NY
        for core in range(NC):
            here = (dy * NC + (core + NC - c) % NC) * SB
            there = ((((z + dz) % NZ) * NX + (x + e) % NX) * NC + core) * SB
            there = pl.ds(pl.multiple_of(there, SB), SB)
            outs[dz][core * SB : (core + 1) * SB, :] = total[
                pl.ds(pl.multiple_of(here, SB), SB), :
            ] + jnp.concatenate([cycle[n, there, :] for n in range(cycle.shape[0])], axis=1)


def ladder(e, amplitudes, cycle, before, pieces):
    places = [(n, *place) for n, (_, held) in enumerate(pieces) for place in held]
    places = [(n, index, slot, dy % NY, g, h) for n, index, slot, dy, g, h in places]
    rows, q = amplitudes.shape[1], NY * NC * SB
    out = jax.ShapeDtypeStruct((q // NZ, rows), jnp.float32)
    return pl.pallas_call(
        functools.partial(ladder_kernel, places, e, len(pieces)),
        out_shape=(out,) * NZ + (jax.ShapeDtypeStruct((8, 128), jnp.float32),),
        in_specs=[pl.BlockSpec(memory_space=pltpu.VMEM)] * (3 + len(pieces)),
        out_specs=[pl.BlockSpec(memory_space=pltpu.VMEM)] * (NZ + 1),
        scratch_shapes=[pltpu.VMEM((q, rows), jnp.float32)],
        compiler_params=pltpu.CompilerParams(vmem_limit_bytes=24 * MIB),
        cost_estimate=pl.CostEstimate(
            flops=2 * q * rows * 2 * TILE, bytes_accessed=2 * q * 2 * TILE, transcendentals=0
        ),
        name="ladder",
    )(amplitudes, cycle, before, *[array for array, _ in pieces])


def pack_kernel(own, beside, out):
    for e, block in enumerate((own, beside)):
        for n in range(block.shape[0] // HALF):
            at = (e * (block.shape[0] // HALF) + n) * block.shape[1]
            out[:, at : at + block.shape[1]] = block[n * HALF : (n + 1) * HALF, :]


def pack_pair(own, beside):
    return pl.pallas_call(
        pack_kernel,
        out_shape=jax.ShapeDtypeStruct((HALF, TILE), own.dtype),
        in_specs=[pl.BlockSpec(memory_space=pltpu.VMEM)] * 2,
        out_specs=pl.BlockSpec(memory_space=pltpu.VMEM),
        compiler_params=pltpu.CompilerParams(vmem_limit_bytes=4 * MIB),
        name="pack_pair",
    )(own, beside)


def cycle_kernel(places, width, slab, token, *refs):
    blocks, out, turned = refs[:-2], refs[-2], refs[-1]
    spot = lax.axis_index("blk")
    y, x, c = spot // (NX * NC), (spot // NC) % NX, spot % NC
    pairs, depth = slab.shape
    for piece, index, dy, g in places:
        for e in range(NX):
            tiles = []
            for n in range(depth // HALF):
                at = (e * (depth // HALF) + n) * width
                tiles.append(blocks[piece][(*index, slice(None), slice(at, at + width))])
            term = jnp.dot(slab[...], jnp.concatenate(tiles), preferred_element_type=jnp.float32)
            block = ((y + dy) % NY * NX + (x + e) % NX) * NC + (c + g) % NC
            turned[pl.ds(pl.multiple_of(block * width, width), width), :] = term.T
    a_all = pairs // (2 * out.shape[0])
    for b in range(SB):
        rows = turned[pl.ds(b, OW, stride=SB), :].T
        for i in range(0, pairs // a_all, 2):
            both = [rows[at * a_all : (at + 1) * a_all] for at in (i, i + 1)]
            out[i // 2, pl.ds(b, a_all, stride=SB), :] = jnp.concatenate(both, axis=1)


def slab_matrix(slab_amplitudes):
    k_local, i_local, ac = slab_amplitudes.shape
    slab = slab_amplitudes.reshape(k_local, i_local, ac // SB, SB).transpose(1, 2, 0, 3)
    return slab.reshape(i_local * ac // SB, k_local * SB)


def cycle_sums(slab, pieces, token, i_local):
    a_all, depth = slab.shape[0] // i_local, slab.shape[1]
    places = [(n, index, dy % NY, g) for n, (_, index, dy, g) in enumerate(pieces)]
    width = OW * SB // (NY * NX * NC)
    return pl.pallas_call(
        functools.partial(cycle_kernel, places, width),
        out_shape=jax.ShapeDtypeStruct((i_local // 2, a_all * SB, 2 * OW), jnp.float32),
        in_specs=[pl.BlockSpec(memory_space=pltpu.VMEM)] * (2 + len(pieces)),
        out_specs=pl.BlockSpec(memory_space=pltpu.VMEM),
        scratch_shapes=[pltpu.VMEM((OW * SB, i_local * a_all), jnp.float32)],
        compiler_params=pltpu.CompilerParams(vmem_limit_bytes=16 * MIB),
        cost_estimate=pl.CostEstimate(
            flops=2 * slab.shape[0] * depth * OW * SB, bytes_accessed=8 * MIB, transcendentals=0
        ),
        name="cycle",
    )(slab, token, *[array for array, *_ in pieces])


def sum_along_z(parts):
    total = parts[0]
    for dz in range(1, NZ):
        total = total + move_row(parts[dz], dz=dz)
    return total


def per_device(amplitudes, integrals, live_pairs, slab_amplitudes, cycle_integrals):
    swapped = {}

    def swap(array):
        return move(array, dc=1)

    def cores(array, *spots):
        return [
            (both, [(index, slot, dy, g, h) for index, slot, dy, h in spots])
            for g, both in enumerate((array, swapped[id(array)] if id(array) in swapped else swap(array)))
        ]

    own = pick_live(live_pairs, integrals.T)
    below, above, beside = move(own, dy=1), move(own, dy=-1), move(own, dx=1)
    cycle_beside = move(cycle_integrals, dx=1)
    amplitudes, own_swap = together(amplitudes, swap(own))
    swapped[id(own)] = own_swap
    live_amps, token = load_live(live_pairs, amplitudes)
    slab_rows = slab_matrix(slab_amplitudes)
    cycle_beside, token, slab_rows = together(cycle_beside, token, slab_rows)
    pair = pack_pair(cycle_integrals, cycle_beside)

    below, above, beside, token, slab_rows, pair = together(below, above, beside, token, slab_rows, pair)
    from_below = move(jnp.concatenate([below[0], beside[0], pair[None]]), dy=1)
    from_above = move(jnp.concatenate([above[1], beside[0], pair[None]]), dy=-1)
    across = move(jnp.stack([below[1], above[1]]), dx=1)
    pair_far = move(pair, dy=2)

    pair_far, below, above, beside = together(pair_far, below, above, beside)
    shadow = [swap(array) for array in (below, above, beside)]
    from_below, from_above, across, *shadow = together(from_below, from_above, across, *shadow)
    for array, other in zip((below, above, beside), shadow):
        swapped[id(array)] = other
    last_below = move(jnp.stack([from_below[2], across[0, 0]]), dy=1)
    last_above = move(jnp.stack([from_above[3], across[1, 1]]), dy=-1)

    pairs = jnp.stack([pair, pair_far])
    blocks = []
    for g, array in enumerate((pairs, swap(pairs))):
        blocks += [(array, (0,), 0, g), (array, (1,), 2, g)]
    for dy, array in ((-1, from_below), (1, from_above)):
        swapped[id(array)] = swap(array)
        blocks += [(array, (4,), dy, 0), (swapped[id(array)], (4,), dy, 1)]
    cycle = cycle_sums(slab_rows, blocks, token, slab_amplitudes.shape[1])

    halves = [(h, n) for h in range(2) for n in range(2)]
    near = []
    for dy, array in ((0, own), (-1, below), (1, above)):
        near += cores(array, *[((h, n), n, dy, h) for h, n in halves])
    for h, array in enumerate((from_below, from_above)):
        near += cores(array, *[((n,), n, 2, h) for n in range(2)])
    *near, token = ladder(0, live_amps, cycle, token, near)
    near = sum_along_z(near)

    last_below, last_above, token = together(last_below, last_above, token)
    far = cores(beside, *[((h, n), n, 0, h) for h, n in halves])
    for dy, array in ((-1, from_below), (1, from_above)):
        far += cores(array, *[((2 + n,), n, dy, 0) for n in range(2)])
    far += cores(across, *[((d, n), n, dy, 1) for d, dy in enumerate((-1, 1)) for n in range(2)])
    for n, array in enumerate((last_below, last_above)):
        far += cores(array, *[((h,), n, 2, h) for h in range(2)])
    far = sum_along_z(ladder(1, live_amps, cycle, token, far)[:NZ])

    mine = lax.axis_index("row") % NH == (lax.axis_index("blk") // NC) % NX
    total = jnp.where(mine, near, far) + move_row(jnp.where(mine, far, near), dx=1)
    return total.astype(jnp.bfloat16).T


def solution(mesh):
    return jax.shard_map(
        per_device,
        mesh=mesh,
        in_specs=(
            P("blk", "row"),
            P("row", "blk"),
            P("row"),
            P("row", "blk", None),
            P("row", "blk"),
        ),
        out_specs=P("blk", "row"),
        check_vma=False,
    )
```

time: 102 us -> 80.5 us (0.79)
  starting transfers between devices: 41.1 us -> 30 us
  waiting for transfers between devices: 41.1 us -> 32.6 us
  other arithmetic: 2.27 us -> 1 us
  Pallas kernels: 13.5 us -> 12.3 us
    ppermute x8 -> x7, waiting for transfers between devices: 18.5 us -> 10.2 us  [move_row(): return lax.ppermute(value, 'row', row_moves(dz, dx))]
    ppermute x27 -> x20, starting transfers between devices: 24.6 us -> 17.4 us  [move(): return lax.ppermute(value, 'blk', blk_moves(dy, dx, dc))]
    ppermute x8 -> x7, starting transfers between devices: 16.6 us -> 12.7 us  [move_row(): return lax.ppermute(value, 'row', row_moves(dz, dx))]
    another operation x10 -> x4, other arithmetic: 2.2 us -> 0.13 us  [the longest x1 0.05 us: per_device(): across = move(jnp.stack([below[1], above[1]]), dx=1)]
    pallas_call x5 -> x6, Pallas kernels: 13.5 us -> 12.3 us  [the longest x2 5.23 us: ladder(): pl.pallas_call(functools.partial(ladder_kernel, places, e, len(pieces)),...]
    unnamed x4 -> x8, local copies, waits for them, and re-layouts: 1.6 us -> 2.53 us
    ppermute x27 -> x20, waiting for transfers between devices: 22.6 us -> 22.4 us  [move(): return lax.ppermute(value, 'blk', blk_moves(dy, dx, dc))]
  transfers between devices with their start and end apart: 35 -> 27, of which waited for: 12 -> 10; matrix products, arithmetic and copies ran while one was open for 4% -> 2% of each run, Pallas kernels for 8% -> 14%
where the time goes in v3:
time: 80.5 us; the launch traced here: 80.3 us
  waiting for transfers between devices  32.6 us (40%)
  starting transfers between devices  30 us (37%)
  Pallas kernels  12.3 us (15%)
  local copies, waits for them, and re-layouts  4.09 us (5%)
  other arithmetic  1 us (1%)
    ppermute x20, waiting for transfers between devices, move(): return lax.ppermute(value, 'blk', blk_moves(dy, dx, dc))  22.4 us
    ppermute x20, starting transfers between devices, move(): return lax.ppermute(value, 'blk', blk_moves(dy, dx, dc))  17.4 us
    ppermute x7, starting transfers between devices, move_row(): return lax.ppermute(value, 'row', row_moves(dz, dx))  12.7 us
    ppermute x7, waiting for transfers between devices, move_row(): return lax.ppermute(value, 'row', row_moves(dz, dx))  10.2 us
    pallas_call x2, Pallas kernels, ladder(): pl.pallas_call(functools.partial(ladder_kernel, places, e, len(pieces)),...  5.23 us
    pallas_call x1, Pallas kernels, load_live(): pl.pallas_call(load_kernel, out_shape=(jax.ShapeDtypeStruct((2 * KT, rows...  4.05 us
    unnamed x8, local copies, waits for them, and re-layouts  2.53 us
    pallas_call x1, Pallas kernels, cycle_sums(): pl.pallas_call(functools.partial(cycle_kernel, places, width), out_shape=...  2.08 us
  transfers between devices with their start and end apart: 27, of which 10 were waited for; matrix products, arithmetic and copies ran while one was open for 2% of the time, Pallas kernels for 14%

profile of v3, /device:TPU:0, one launch (start us, length us, event | category | flops | bytes accessed | tf_op | source)
XLA Modules:
  0.0 80.3 jit_solution(693474991416288001)
XLA Ops:
  0.0 1.2 %copy-done = bf16[16384,32]{0,1:T(8,128)(2,1)S(1)} copy-done((bf16[16384,32]{0,1:T(8,128)(2,1)S(1)}, bf16[16384,32]{0,1:T(8,128)(2,1)}, u32[]{:S(2)}) %copy-start) | copy-done | bytes 1048600
  1.2 0.7 copy-done.2
  1.9 0.9 %pick_live.1.refs_0_ = bf16[2,2,16,4096]{3,2,1,0:T(8,128)(2,1)S(1)} custom-call(s32[4]{0:T(128)S(1)} %copy-done.2, bf16[32,16384]{1,0:T(8,128)(2,1)S(1)} %bitcast.22), custom_call_target="tpu_custom_call" | custom-call | tf_op jit(solution)/shard_map/pick_live/pallas_call | solution.py:66
  2.8 0.1 collective-permute-start
  2.9 1.7 %collective-permute-start.1 = (bf16[2,2,16,4096]{3,2,1,0:T(8,128)(2,1)S(1)}, bf16[2,2,16,4096]{3,2,1,0:T(8,128)(2,1)S(1)}, u32[]{:S(2)}, u32[]{:S(2)}) collective-permute-start(bf16[2,2,16,4096]{3,2,1,0:T(8,128)(2,1)S(1)} %pick_live.1.refs_0_), channel_id=1, source_target_pairs={{0,4},{1,5},{2,6},{3,7},{4,8},{5,9},{6,10},{7,11},{8,12},{9,13},{1... | collective-permute-start | bytes 1572872 | tf_op jit(solution)/shard_map/ppermute | solution.py:35
  4.6 1.6 %collective-permute-start.2 = (bf16[2,2,16,4096]{3,2,1,0:T(8,128)(2,1)S(1)}, bf16[2,2,16,4096]{3,2,1,0:T(8,128)(2,1)S(1)}, u32[]{:S(2)}, u32[]{:S(2)}) collective-permute-start(bf16[2,2,16,4096]{3,2,1,0:T(8,128)(2,1)S(1)} %pick_live.1.refs_0_), channel_id=1, source_target_pairs={{0,12},{1,13},{2,14},{3,15},{4,0},{5,1},{6,2},{7,3},{8,4},{9,5},{1... | collective-permute-start | bytes 1572872 | tf_op jit(solution)/shard_map/ppermute | solution.py:35
  6.2 1.6 %collective-permute-start.3 = (bf16[2,2,16,4096]{3,2,1,0:T(8,128)(2,1)S(1)}, bf16[2,2,16,4096]{3,2,1,0:T(8,128)(2,1)S(1)}, u32[]{:S(2)}, u32[]{:S(2)}) collective-permute-start(bf16[2,2,16,4096]{3,2,1,0:T(8,128)(2,1)S(1)} %pick_live.1.refs_0_), channel_id=1, source_target_pairs={{0,2},{1,3},{2,0},{3,1},{4,6},{5,7},{6,4},{7,5},{8,10},{9,11},{10,... | collective-permute-start | bytes 1572872 | tf_op jit(solution)/shard_map/ppermute | solution.py:35
  7.8 0.5 collective-permute-start.4
  8.2 1.0 %reshape.6 = bf16[8,8,16,32]{3,2,1,0:T(8,128)(2,1)S(1)} reshape(bf16[8,8,512]{2,1,0:T(8,128)(2,1)} %param.8) | data formatting | bytes 131072 | tf_op jit(solution)/shard_map/reshape | solution.py:203
  9.3 0.2 copy.8
  9.5 0.2 reshape.7.slab
  9.7 0.0 copy-start.3
  9.7 0.6 copy-done.3
  10.3 4.0 %load_live.1 = (bf16[8,512,1024]{2,1,0:T(8,128)(2,1)S(1)}, f32[8,128]{1,0:T(8,128)S(1)}) custom-call(s32[4]{0:T(128)S(1)} %copy-done.3, bf16[512,16384]{1,0:T(8,128)(2,1)} %amps), custom_call_target="tpu_custom_call" | custom-call | tf_op jit(solution)/shard_map/load_live/pallas_call | solution.py:93
  14.4 7.1 %collective-permute-done.4.beside = bf16[256,128]{1,0:T(8,128)(2,1)S(1)} collective-permute-done((bf16[256,128]{1,0:T(8,128)(2,1)}, bf16[256,128]{1,0:T(8,128)(2,1)S(1)}, u32[]{:S(2)}, u32[]{:S(2)}) %collective-permute-start.4) | collective-permute-done | bytes 65568 | tf_op jit(solution)/shard_map/ppermute | solution.py:35
  21.5 0.0 collective-permute-done.1.refs_2_
  21.5 0.0 collective-permute-done.3.refs_0_
  21.5 2.0 %collective-permute-start.5 = (bf16[16,4096]{1,0:T(8,128)(2,1)S(1)}, bf16[16,4096]{1,0:T(8,128)(2,1)S(1)}, u32[]{:S(2)}, u32[]{:S(2)}) collective-permute-start(bf16[16,4096]{1,0:T(8,128)(2,1)S(1)} %pack_pair.1), channel_id=1, source_target_pairs={{0,8},{1,9},{2,10},{3,11},{4,12},{5,13},{6,14},{7,15},{8,0},{9,1},... | collective-permute-start | bytes 393224 | tf_op jit(solution)/shard_map/ppermute | solution.py:35
  23.6 0.1 fusion.1
  23.7 0.1 pad_maximum_fusion.4
  23.7 1.6 %collective-permute-start.9 = (bf16[2,2,16,4096]{3,2,1,0:T(8,128)(2,1)S(1)}, bf16[2,2,16,4096]{3,2,1,0:T(8,128)(2,1)S(1)}, u32[]{:S(2)}, u32[]{:S(2)}) collective-permute-start(bf16[2,2,16,4096]{3,2,1,0:T(8,128)(2,1)S(1)} %pad_maximum_fusion.4), channel_id=1, source_target_pairs={{0,2},{1,3},{2,0},{3,1},{4,6},{5,7},{6,4},{7,5},{8,10},{9,11},{10,... | collective-permute-start | bytes 1572872 | tf_op jit(solution)/shard_map/ppermute | solution.py:35
  25.3 0.1 pad_maximum_fusion
  25.4 0.7 collective-permute-start.7
  26.2 2.6 %collective-permute-start.8 = (bf16[5,16,4096]{2,1,0:T(8,128)(2,1)S(1)}, bf16[5,16,4096]{2,1,0:T(8,128)(2,1)S(1)}, u32[]{:S(2)}, u32[]{:S(2)}) collective-permute-start(bf16[5,16,4096]{2,1,0:T(8,128)(2,1)S(1)} %get-tuple-element.84), channel_id=1, source_target_pairs={{0,12},{1,13},{2,14},{3,15},{4,0},{5,1},{6,2},{7,3},{8,4},{9,5},{1... | collective-permute-start | bytes 1966088 | tf_op jit(solution)/shard_map/ppermute | solution.py:35
  28.7 0.5 collective-permute-done.5
  29.2 0.0 collective-permute-start.10
  29.2 0.5 collective-permute-start.11
  29.7 6.7 %collective-permute-done.9.refs_6_ = bf16[2,2,16,4096]{3,2,1,0:T(8,128)(2,1)S(1)} collective-permute-done((bf16[2,2,16,4096]{3,2,1,0:T(8,128)(2,1)S(1)}, bf16[2,2,16,4096]{3,2,1,0:T(8,128)(2,1)S(1)}, u32[]{:S(2)}, u32[]{:S(2)}) %collective-permute-start.9) | collective-permute-done | bytes 524320 | tf_op jit(solution)/shard_map/ppermute | solution.py:35
  36.4 6.1 %collective-permute-done.7.refs_4_.refs_6_.refs_2_ = bf16[5,16,4096]{2,1,0:T(8,128)(2,1)S(1)} collective-permute-done((bf16[5,16,4096]{2,1,0:T(8,128)(2,1)S(1)}, bf16[5,16,4096]{2,1,0:T(8,128)(2,1)S(1)}, u32[]{:S(2)}, u32[]{:S(2)}) %collective-permute-start.7) | collective-permute-done | bytes 655392 | tf_op jit(solution)/shard_map/ppermute | solution.py:35
  42.5 0.0 collective-permute-done.8.refs_6_.refs_8_.refs_4_
  42.5 0.0 collective-permute-done.10.refs_3_
  42.5 0.0 collective-permute-done.11.refs_5_
  42.6 0.0 collective-permute-done.12.refs_1_
  42.6 0.6 collective-permute-start.13
  43.2 0.1 collective-permute-start.14
  43.3 0.1 collective-permute-start.18
  43.5 3.3 %collective-permute-start.19 = (bf16[2,16,4096]{2,1,0:T(8,128)(2,1)S(1)}, bf16[2,16,4096]{2,1,0:T(8,128)(2,1)S(1)}, u32[]{:S(2)}, u32[]{:S(2)}) collective-permute-start(bf16[2,16,4096]{2,1,0:T(8,128)(2,1)S(1)} %pad_maximum_fusion.7), channel_id=1, source_target_pairs={{0,12},{1,13},{2,14},{3,15},{4,0},{5,1},{6,2},{7,3},{8,4},{9,5},{1... | collective-permute-start | bytes 786440 | tf_op jit(solution)/shard_map/ppermute | solution.py:35
  46.7 0.0 collective-permute-done.6.refs_2_.refs_3_
  46.7 0.0 collective-permute-start.20
  46.7 0.0 collective-permute-done.14.refs_7_.refs_9_.refs_5_
  46.8 2.1 %cycle.1 = f32[4,512,128]{2,1,0:T(8,128)S(1)} custom-call(bf16[128,256]{1,0:T(8,128)(2,1)S(1)} %reshape.7.slab, f32[8,128]{1,0:T(8,128)S(1)} %get-tuple-element.47.token.before, bf16[2,16,4096]{2,1,0:T(8,128)(2,1)S(1)} %pad_maximum_fusion.5.refs_0_.refs_1_, bf16[2,16,4096]{2,1,0:T(8,128)(2,1)S(1)} %pad_maximum_fusion.5.refs_0_.refs_1_, ...), custom_call_target="tpu_custom_call" | custom-call | flops 134217728 | bytes 8388608 | tf_op jit(solution)/shard_map/cycle/pallas_call | solution.py:211
  48.8 2.4 %ladder.2 = (f32[64,512]{1,0:T(8,128)S(1)}, f32[64,512]{1,0:T(8,128)S(1)}, f32[64,512]{1,0:T(8,128)S(1)}, f32[64,512]{1,0:T(8,128)S(1)}, f32[8,128]{1,0:T(8,128)S(1)}) custom-call(bf16[8,512,1024]{2,1,0:T(8,128)(2,1)S(1)} %get-tuple-element.41.amps, f32[4,512,128]{2,1,0:T(8,128)S(1)} %cycle.1, f32[8,128]{1,0:T(8,128)S(1)} %get-tuple-element.47.token.before, ...), custom_call_target="tpu_custom_call" | custom-call | flops 2147483648 | bytes 4194304 | tf_op jit(solution)/shard_map/ladder/pallas_call | solution.py:147
  51.3 2.0 %collective-permute-done.18.refs_8_ = bf16[2,16,4096]{2,1,0:T(8,128)(2,1)S(1)} collective-permute-done((bf16[2,16,4096]{2,1,0:T(8,128)(2,1)S(1)}, bf16[2,16,4096]{2,1,0:T(8,128)(2,1)S(1)}, u32[]{:S(2)}, u32[]{:S(2)}) %collective-permute-start.18) | collective-permute-done | bytes 262176 | tf_op jit(solution)/shard_map/ppermute | solution.py:35
  53.3 0.0 collective-permute-done.19.refs_10_
  53.3 0.0 collective-permute-start.21
  53.3 0.5 collective-permute-start.22
  53.8 4.0 %collective-permute-start.17 = (f32[64,512]{1,0:T(8,128)S(1)}, f32[64,512]{1,0:T(8,128)S(1)}, u32[]{:S(2)}, u32[]{:S(2)}) collective-permute-start(f32[64,512]{1,0:T(8,128)S(1)} %get-tuple-element.64), channel_id=1, source_target_pairs={{0,96},{16,112},{32,0},{48,16},{64,32},{80,48},{96,64},{112,80},{1... | collective-permute-start | bytes 393224 | tf_op jit(solution)/shard_map/ppermute | solution.py:39
  57.9 0.0 collective-permute-start.16
  57.9 0.0 collective-permute-done.20.refs_7_
  57.9 1.3 %collective-permute-start.15 = (f32[64,512]{1,0:T(8,128)S(1)}, f32[64,512]{1,0:T(8,128)S(1)}, u32[]{:S(2)}, u32[]{:S(2)}) collective-permute-start(f32[64,512]{1,0:T(8,128)S(1)} %get-tuple-element.62), channel_id=1, source_target_pairs={{0,32},{16,48},{32,64},{48,80},{64,96},{80,112},{96,0},{112,16},{1... | collective-permute-start | bytes 393224 | tf_op jit(solution)/shard_map/ppermute | solution.py:39
  59.1 0.0 collective-permute-done.21.refs_9_
  59.1 0.0 collective-permute-done.22.refs_11_
  59.1 2.8 %ladder.3 = (f32[64,512]{1,0:T(8,128)S(1)}, f32[64,512]{1,0:T(8,128)S(1)}, f32[64,512]{1,0:T(8,128)S(1)}, f32[64,512]{1,0:T(8,128)S(1)}, f32[8,128]{1,0:T(8,128)}) custom-call(bf16[8,512,1024]{2,1,0:T(8,128)(2,1)S(1)} %get-tuple-element.41.amps, f32[4,512,128]{2,1,0:T(8,128)S(1)} %cycle.1, f32[8,128]{1,0:T(8,128)S(1)} %get-tuple-element.67.before, ...), custom_call_target="tpu_custom_call" | custom-call | flops 2147483648 | bytes 4194304 | tf_op jit(solution)/shard_map/ladder/pallas_call | solution.py:147
  62.0 2.0 %collective-permute-start.25 = (f32[64,512]{1,0:T(8,128)S(1)}, f32[64,512]{1,0:T(8,128)S(1)}, u32[]{:S(2)}, u32[]{:S(2)}) collective-permute-start(f32[64,512]{1,0:T(8,128)S(1)} %get-tuple-element.74), channel_id=1, source_target_pairs={{0,96},{16,112},{32,0},{48,16},{64,32},{80,48},{96,64},{112,80},{1... | collective-permute-start | bytes 393224 | tf_op jit(solution)/shard_map/ppermute | solution.py:39
  63.9 2.3 %collective-permute-start.24 = (f32[64,512]{1,0:T(8,128)S(1)}, f32[64,512]{1,0:T(8,128)S(1)}, u32[]{:S(2)}, u32[]{:S(2)}) collective-permute-start(f32[64,512]{1,0:T(8,128)S(1)} %get-tuple-element.73), channel_id=1, source_target_pairs={{0,64},{16,80},{32,96},{48,112},{64,0},{80,16},{96,32},{112,48},{1... | collective-permute-start | bytes 393224 | tf_op jit(solution)/shard_map/ppermute | solution.py:39
  66.3 0.0 collective-permute-done.17
  66.3 0.8 collective-permute-done.15
  67.0 2.2 %collective-permute-done.25 = f32[64,512]{1,0:T(8,128)S(1)} collective-permute-done((f32[64,512]{1,0:T(8,128)S(1)}, f32[64,512]{1,0:T(8,128)S(1)}, u32[]{:S(2)}, u32[]{:S(2)}) %collective-permute-start.25) | collective-permute-done | bytes 131104 | tf_op jit(solution)/shard_map/ppermute | solution.py:39
  69.2 2.5 %collective-permute-done.24 = f32[64,512]{1,0:T(8,128)S(1)} collective-permute-done((f32[64,512]{1,0:T(8,128)S(1)}, f32[64,512]{1,0:T(8,128)S(1)}, u32[]{:S(2)}, u32[]{:S(2)}) %collective-permute-start.24) | collective-permute-done | bytes 131104 | tf_op jit(solution)/shard_map/ppermute | solution.py:39
  71.7 1.2 %collective-permute-done.23 = f32[64,512]{1,0:T(8,128)S(1)} collective-permute-done((f32[64,512]{1,0:T(8,128)S(1)}, f32[64,512]{1,0:T(8,128)S(1)}, u32[]{:S(2)}, u32[]{:S(2)}) %collective-permute-start.23) | collective-permute-done | bytes 131104 | tf_op jit(solution)/shard_map/ppermute | solution.py:39
  73.0 0.1 broadcast_select_fusion
  73.1 3.1 %collective-permute-start.26 = (f32[64,512]{1,0:T(8,128)S(1)}, f32[64,512]{1,0:T(8,128)S(1)}, u32[]{:S(2)}, u32[]{:S(2)}) collective-permute-start(f32[64,512]{1,0:T(8,128)S(1)} %get-tuple-element.75), channel_id=1, source_target_pairs={{0,16},{16,0},{32,48},{48,32},{64,80},{80,64},{96,112},{112,96},{1... | collective-permute-start | bytes 393224 | tf_op jit(solution)/shard_map/ppermute | solution.py:39
  76.1 3.5 %collective-permute-done.26 = f32[64,512]{1,0:T(8,128)S(1)} collective-permute-done((f32[64,512]{1,0:T(8,128)S(1)}, f32[64,512]{1,0:T(8,128)S(1)}, u32[]{:S(2)}, u32[]{:S(2)}) %collective-permute-start.26) | collective-permute-done | bytes 131104 | tf_op jit(solution)/shard_map/ppermute | solution.py:39
  79.6 0.7 fusion
  (19 shorter events, 0.2 us)
Async XLA Ops:
  0.0 1.2 %copy-start = (bf16[16384,32]{0,1:T(8,128)(2,1)S(1)}, bf16[16384,32]{0,1:T(8,128)(2,1)}, u32[]{:S(2)}) copy-start(bf16[16384,32]{0,1:T(8,128)(2,1)} %param.6) | copy-start | bytes 3145732
  1.2 0.7 copy-start.2
  1.9 19.6 %copy-start.1 = (bf16[256,128]{1,0:T(8,128)(2,1)S(1)}, bf16[256,128]{1,0:T(8,128)(2,1)}, u32[]{:S(2)}) copy-start(bf16[256,128]{1,0:T(8,128)(2,1)} %own.1) | copy-start | bytes 196612
  2.8 6.8 %collective-permute-start = (bf16[2,2,16,4096]{3,2,1,0:T(8,128)(2,1)S(1)}, bf16[2,2,16,4096]{3,2,1,0:T(8,128)(2,1)S(1)}, u32[]{:S(2)}, u32[]{:S(2)}) collective-permute-start(bf16[2,2,16,4096]{3,2,1,0:T(8,128)(2,1)S(1)} %pick_live.1.refs_0_), channel_id=1, source_target_pairs={{0,1},{1,0},{2,3},{3,2},{4,5},{5,4},{6,7},{7,6},{8,9},{9,8},{10,11... | collective-permute-start | bytes 1572872 | tf_op jit(solution)/shard_map/ppermute | solution.py:35
  2.9 18.6 %collective-permute-start.1 = (bf16[2,2,16,4096]{3,2,1,0:T(8,128)(2,1)S(1)}, bf16[2,2,16,4096]{3,2,1,0:T(8,128)(2,1)S(1)}, u32[]{:S(2)}, u32[]{:S(2)}) collective-permute-start(bf16[2,2,16,4096]{3,2,1,0:T(8,128)(2,1)S(1)} %pick_live.1.refs_0_), channel_id=1, source_target_pairs={{0,4},{1,5},{2,6},{3,7},{4,8},{5,9},{6,10},{7,11},{8,12},{9,13},{1... | collective-permute-start | bytes 1572872 | tf_op jit(solution)/shard_map/ppermute | solution.py:35
  4.6 16.9 %collective-permute-start.2 = (bf16[2,2,16,4096]{3,2,1,0:T(8,128)(2,1)S(1)}, bf16[2,2,16,4096]{3,2,1,0:T(8,128)(2,1)S(1)}, u32[]{:S(2)}, u32[]{:S(2)}) collective-permute-start(bf16[2,2,16,4096]{3,2,1,0:T(8,128)(2,1)S(1)} %pick_live.1.refs_0_), channel_id=1, source_target_pairs={{0,12},{1,13},{2,14},{3,15},{4,0},{5,1},{6,2},{7,3},{8,4},{9,5},{1... | collective-permute-start | bytes 1572872 | tf_op jit(solution)/shard_map/ppermute | solution.py:35
  6.2 15.3 %collective-permute-start.3 = (bf16[2,2,16,4096]{3,2,1,0:T(8,128)(2,1)S(1)}, bf16[2,2,16,4096]{3,2,1,0:T(8,128)(2,1)S(1)}, u32[]{:S(2)}, u32[]{:S(2)}) collective-permute-start(bf16[2,2,16,4096]{3,2,1,0:T(8,128)(2,1)S(1)} %pick_live.1.refs_0_), channel_id=1, source_target_pairs={{0,2},{1,3},{2,0},{3,1},{4,6},{5,7},{6,4},{7,5},{8,10},{9,11},{10,... | collective-permute-start | bytes 1572872 | tf_op jit(solution)/shard_map/ppermute | solution.py:35
  7.8 13.7 %collective-permute-start.4 = (bf16[256,128]{1,0:T(8,128)(2,1)}, bf16[256,128]{1,0:T(8,128)(2,1)S(1)}, u32[]{:S(2)}, u32[]{:S(2)}) collective-permute-start(bf16[256,128]{1,0:T(8,128)(2,1)} %own.1), channel_id=1, source_target_pairs={{0,2},{1,3},{2,0},{3,1},{4,6},{5,7},{6,4},{7,5},{8,10},{9,11},{10,... | collective-permute-start | bytes 196616 | tf_op jit(solution)/shard_map/ppermute | solution.py:35
  9.7 0.7 copy-start.3
  21.5 7.7 %collective-permute-start.5 = (bf16[16,4096]{1,0:T(8,128)(2,1)S(1)}, bf16[16,4096]{1,0:T(8,128)(2,1)S(1)}, u32[]{:S(2)}, u32[]{:S(2)}) collective-permute-start(bf16[16,4096]{1,0:T(8,128)(2,1)S(1)} %pack_pair.1), channel_id=1, source_target_pairs={{0,8},{1,9},{2,10},{3,11},{4,12},{5,13},{6,14},{7,15},{8,0},{9,1},... | collective-permute-start | bytes 393224 | tf_op jit(solution)/shard_map/ppermute | solution.py:35
  23.7 12.6 %collective-permute-start.9 = (bf16[2,2,16,4096]{3,2,1,0:T(8,128)(2,1)S(1)}, bf16[2,2,16,4096]{3,2,1,0:T(8,128)(2,1)S(1)}, u32[]{:S(2)}, u32[]{:S(2)}) collective-permute-start(bf16[2,2,16,4096]{3,2,1,0:T(8,128)(2,1)S(1)} %pad_maximum_fusion.4), channel_id=1, source_target_pairs={{0,2},{1,3},{2,0},{3,1},{4,6},{5,7},{6,4},{7,5},{8,10},{9,11},{10,... | collective-permute-start | bytes 1572872 | tf_op jit(solution)/shard_map/ppermute | solution.py:35
  25.4 17.1 %collective-permute-start.7 = (bf16[5,16,4096]{2,1,0:T(8,128)(2,1)S(1)}, bf16[5,16,4096]{2,1,0:T(8,128)(2,1)S(1)}, u32[]{:S(2)}, u32[]{:S(2)}) collective-permute-start(bf16[5,16,4096]{2,1,0:T(8,128)(2,1)S(1)} %get-tuple-element.85), channel_id=1, source_target_pairs={{0,4},{1,5},{2,6},{3,7},{4,8},{5,9},{6,10},{7,11},{8,12},{9,13},{1... | collective-permute-start | bytes 1966088 | tf_op jit(solution)/shard_map/ppermute | solution.py:35
  26.2 16.3 %collective-permute-start.8 = (bf16[5,16,4096]{2,1,0:T(8,128)(2,1)S(1)}, bf16[5,16,4096]{2,1,0:T(8,128)(2,1)S(1)}, u32[]{:S(2)}, u32[]{:S(2)}) collective-permute-start(bf16[5,16,4096]{2,1,0:T(8,128)(2,1)S(1)} %get-tuple-element.84), channel_id=1, source_target_pairs={{0,12},{1,13},{2,14},{3,15},{4,0},{5,1},{6,2},{7,3},{8,4},{9,5},{1... | collective-permute-start | bytes 1966088 | tf_op jit(solution)/shard_map/ppermute | solution.py:35
  29.2 13.3 %collective-permute-start.10 = (bf16[2,2,16,4096]{3,2,1,0:T(8,128)(2,1)S(1)}, bf16[2,2,16,4096]{3,2,1,0:T(8,128)(2,1)S(1)}, u32[]{:S(2)}, u32[]{:S(2)}) collective-permute-start(bf16[2,2,16,4096]{3,2,1,0:T(8,128)(2,1)S(1)} %collective-permute-done.1.refs_2_), channel_id=1, source_target_pairs={{0,1},{1,0},{2,3},{3,2},{4,5},{5,4},{6,7},{7,6},{8,9},{9,8},{10,11... | collective-permute-start | bytes 1572872 | tf_op jit(solution)/shard_map/ppermute | solution.py:35
  29.2 13.3 %collective-permute-start.11 = (bf16[2,2,16,4096]{3,2,1,0:T(8,128)(2,1)S(1)}, bf16[2,2,16,4096]{3,2,1,0:T(8,128)(2,1)S(1)}, u32[]{:S(2)}, u32[]{:S(2)}) collective-permute-start(bf16[2,2,16,4096]{3,2,1,0:T(8,128)(2,1)S(1)} %collective-permute-done.2.refs_4_), channel_id=1, source_target_pairs={{0,1},{1,0},{2,3},{3,2},{4,5},{5,4},{6,7},{7,6},{8,9},{9,8},{10,11... | collective-permute-start | bytes 1572872 | tf_op jit(solution)/shard_map/ppermute | solution.py:35
  36.4 6.2 %collective-permute-start.12 = (bf16[2,2,16,4096]{3,2,1,0:T(8,128)(2,1)S(1)}, bf16[2,2,16,4096]{3,2,1,0:T(8,128)(2,1)S(1)}, u32[]{:S(2)}, u32[]{:S(2)}) collective-permute-start(bf16[2,2,16,4096]{3,2,1,0:T(8,128)(2,1)S(1)} %collective-permute-done.3.refs_0_), channel_id=1, source_target_pairs={{0,1},{1,0},{2,3},{3,2},{4,5},{5,4},{6,7},{7,6},{8,9},{9,8},{10,11... | collective-permute-start | bytes 1572872 | tf_op jit(solution)/shard_map/ppermute | solution.py:35
  42.5 4.2 %collective-permute-start.6 = (bf16[2,16,4096]{2,1,0:T(8,128)(2,1)S(1)}, bf16[2,16,4096]{2,1,0:T(8,128)(2,1)S(1)}, u32[]{:S(2)}, u32[]{:S(2)}) collective-permute-start(bf16[2,16,4096]{2,1,0:T(8,128)(2,1)S(1)} %pad_maximum_fusion.5.refs_0_.refs_1_), channel_id=1, source_target_pairs={{0,1},{1,0},{2,3},{3,2},{4,5},{5,4},{6,7},{7,6},{8,9},{9,8},{10,11... | collective-permute-start | bytes 786440 | tf_op jit(solution)/shard_map/ppermute | solution.py:35
  42.6 4.2 %collective-permute-start.13 = (bf16[5,16,4096]{2,1,0:T(8,128)(2,1)S(1)}, bf16[5,16,4096]{2,1,0:T(8,128)(2,1)S(1)}, u32[]{:S(2)}, u32[]{:S(2)}) collective-permute-start(bf16[5,16,4096]{2,1,0:T(8,128)(2,1)S(1)} %collective-permute-done.7.refs_4_.refs_6_.refs_2_), channel_id=1, source_target_pairs={{0,1},{1,0},{2,3},{3,2},{4,5},{5,4},{6,7},{7,6},{8,9},{9,8},{10,11... | collective-permute-start | bytes 1966088 | tf_op jit(solution)/shard_map/ppermute | solution.py:35
  43.2 3.6 %collective-permute-start.14 = (bf16[5,16,4096]{2,1,0:T(8,128)(2,1)S(1)}, bf16[5,16,4096]{2,1,0:T(8,128)(2,1)S(1)}, u32[]{:S(2)}, u32[]{:S(2)}) collective-permute-start(bf16[5,16,4096]{2,1,0:T(8,128)(2,1)S(1)} %collective-permute-done.8.refs_6_.refs_8_.refs_4_), channel_id=1, source_target_pairs={{0,1},{1,0},{2,3},{3,2},{4,5},{5,4},{6,7},{7,6},{8,9},{9,8},{10,11... | collective-permute-start | bytes 1966088 | tf_op jit(solution)/shard_map/ppermute | solution.py:35
  43.3 10.0 %collective-permute-start.18 = (bf16[2,16,4096]{2,1,0:T(8,128)(2,1)S(1)}, bf16[2,16,4096]{2,1,0:T(8,128)(2,1)S(1)}, u32[]{:S(2)}, u32[]{:S(2)}) collective-permute-start(bf16[2,16,4096]{2,1,0:T(8,128)(2,1)S(1)} %pad_maximum_fusion.6), channel_id=1, source_target_pairs={{0,4},{1,5},{2,6},{3,7},{4,8},{5,9},{6,10},{7,11},{8,12},{9,13},{1... | collective-permute-start | bytes 786440 | tf_op jit(solution)/shard_map/ppermute | solution.py:35
  43.5 9.9 %collective-permute-start.19 = (bf16[2,16,4096]{2,1,0:T(8,128)(2,1)S(1)}, bf16[2,16,4096]{2,1,0:T(8,128)(2,1)S(1)}, u32[]{:S(2)}, u32[]{:S(2)}) collective-permute-start(bf16[2,16,4096]{2,1,0:T(8,128)(2,1)S(1)} %pad_maximum_fusion.7), channel_id=1, source_target_pairs={{0,12},{1,13},{2,14},{3,15},{4,0},{5,1},{6,2},{7,3},{8,4},{9,5},{1... | collective-permute-start | bytes 786440 | tf_op jit(solution)/shard_map/ppermute | solution.py:35
  46.7 11.1 %collective-permute-start.20 = (bf16[2,2,16,4096]{3,2,1,0:T(8,128)(2,1)S(1)}, bf16[2,2,16,4096]{3,2,1,0:T(8,128)(2,1)S(1)}, u32[]{:S(2)}, u32[]{:S(2)}) collective-permute-start(bf16[2,2,16,4096]{3,2,1,0:T(8,128)(2,1)S(1)} %collective-permute-done.9.refs_6_), channel_id=1, source_target_pairs={{0,1},{1,0},{2,3},{3,2},{4,5},{5,4},{6,7},{7,6},{8,9},{9,8},{10,11... | collective-permute-start | bytes 1572872 | tf_op jit(solution)/shard_map/ppermute | solution.py:35
  53.3 5.8 %collective-permute-start.21 = (bf16[2,16,4096]{2,1,0:T(8,128)(2,1)S(1)}, bf16[2,16,4096]{2,1,0:T(8,128)(2,1)S(1)}, u32[]{:S(2)}, u32[]{:S(2)}) collective-permute-start(bf16[2,16,4096]{2,1,0:T(8,128)(2,1)S(1)} %collective-permute-done.18.refs_8_), channel_id=1, source_target_pairs={{0,1},{1,0},{2,3},{3,2},{4,5},{5,4},{6,7},{7,6},{8,9},{9,8},{10,11... | collective-permute-start | bytes 786440 | tf_op jit(solution)/shard_map/ppermute | solution.py:35
  53.3 5.8 %collective-permute-start.22 = (bf16[2,16,4096]{2,1,0:T(8,128)(2,1)S(1)}, bf16[2,16,4096]{2,1,0:T(8,128)(2,1)S(1)}, u32[]{:S(2)}, u32[]{:S(2)}) collective-permute-start(bf16[2,16,4096]{2,1,0:T(8,128)(2,1)S(1)} %collective-permute-done.19.refs_10_), channel_id=1, source_target_pairs={{0,1},{1,0},{2,3},{3,2},{4,5},{5,4},{6,7},{7,6},{8,9},{9,8},{10,11... | collective-permute-start | bytes 786440 | tf_op jit(solution)/shard_map/ppermute | solution.py:35
  53.8 12.4 %collective-permute-start.17 = (f32[64,512]{1,0:T(8,128)S(1)}, f32[64,512]{1,0:T(8,128)S(1)}, u32[]{:S(2)}, u32[]{:S(2)}) collective-permute-start(f32[64,512]{1,0:T(8,128)S(1)} %get-tuple-element.64), channel_id=1, source_target_pairs={{0,96},{16,112},{32,0},{48,16},{64,32},{80,48},{96,64},{112,80},{1... | collective-permute-start | bytes 393224 | tf_op jit(solution)/shard_map/ppermute | solution.py:39
  57.9 8.4 %collective-permute-start.16 = (f32[64,512]{1,0:T(8,128)S(1)}, f32[64,512]{1,0:T(8,128)S(1)}, u32[]{:S(2)}, u32[]{:S(2)}) collective-permute-start(f32[64,512]{1,0:T(8,128)S(1)} %get-tuple-element.63), channel_id=1, source_target_pairs={{0,64},{16,80},{32,96},{48,112},{64,0},{80,16},{96,32},{112,48},{1... | collective-permute-start | bytes 393224 | tf_op jit(solution)/shard_map/ppermute | solution.py:39
  57.9 9.1 %collective-permute-start.15 = (f32[64,512]{1,0:T(8,128)S(1)}, f32[64,512]{1,0:T(8,128)S(1)}, u32[]{:S(2)}, u32[]{:S(2)}) collective-permute-start(f32[64,512]{1,0:T(8,128)S(1)} %get-tuple-element.62), channel_id=1, source_target_pairs={{0,32},{16,48},{32,64},{48,80},{64,96},{80,112},{96,0},{112,16},{1... | collective-permute-start | bytes 393224 | tf_op jit(solution)/shard_map/ppermute | solution.py:39
  62.0 7.3 %collective-permute-start.25 = (f32[64,512]{1,0:T(8,128)S(1)}, f32[64,512]{1,0:T(8,128)S(1)}, u32[]{:S(2)}, u32[]{:S(2)}) collective-permute-start(f32[64,512]{1,0:T(8,128)S(1)} %get-tuple-element.74), channel_id=1, source_target_pairs={{0,96},{16,112},{32,0},{48,16},{64,32},{80,48},{96,64},{112,80},{1... | collective-permute-start | bytes 393224 | tf_op jit(solution)/shard_map/ppermute | solution.py:39
  63.9 7.8 %collective-permute-start.24 = (f32[64,512]{1,0:T(8,128)S(1)}, f32[64,512]{1,0:T(8,128)S(1)}, u32[]{:S(2)}, u32[]{:S(2)}) collective-permute-start(f32[64,512]{1,0:T(8,128)S(1)} %get-tuple-element.73), channel_id=1, source_target_pairs={{0,64},{16,80},{32,96},{48,112},{64,0},{80,16},{96,32},{112,48},{1... | collective-permute-start | bytes 393224 | tf_op jit(solution)/shard_map/ppermute | solution.py:39
  66.3 6.7 %collective-permute-start.23 = (f32[64,512]{1,0:T(8,128)S(1)}, f32[64,512]{1,0:T(8,128)S(1)}, u32[]{:S(2)}, u32[]{:S(2)}) collective-permute-start(f32[64,512]{1,0:T(8,128)S(1)} %get-tuple-element.72), channel_id=1, source_target_pairs={{0,32},{16,48},{32,64},{48,80},{64,96},{80,112},{96,0},{112,16},{1... | collective-permute-start | bytes 393224 | tf_op jit(solution)/shard_map/ppermute | solution.py:39
  73.1 6.6 %collective-permute-start.26 = (f32[64,512]{1,0:T(8,128)S(1)}, f32[64,512]{1,0:T(8,128)S(1)}, u32[]{:S(2)}, u32[]{:S(2)}) collective-permute-start(f32[64,512]{1,0:T(8,128)S(1)} %get-tuple-element.75), channel_id=1, source_target_pairs={{0,16},{16,0},{32,48},{48,32},{64,80},{80,64},{96,112},{112,96},{1... | collective-permute-start | bytes 393224 | tf_op jit(solution)/shard_map/ppermute | solution.py:39

commit v4 on v3

v4 whole, which is shorter than its diff:
```python
import functools

import jax
import jax.numpy as jnp
from jax import lax
from jax.experimental import pallas as pl
from jax.experimental.pallas import tpu as pltpu
from jax.sharding import PartitionSpec as P

OW = 64
TS = 64
SB = 32
TILE = TS * TS
NY, NX, NC = 4, 2, 2
NZ, NH = 4, 2
HALF = SB // 2
STEP = 1024
KT = TILE // STEP
MIB = 1 << 20
LANES = 128


def blk_moves(dy, dx, dc):
    spots = [(y, x, c) for y in range(NY) for x in range(NX) for c in range(NC)]
    index = lambda y, x, c: ((y % NY) * NX + x % NX) * NC + c % NC
    return [(index(y, x, c), index(y + dy, x + dx, c + dc)) for y, x, c in spots]


def row_moves(dz, dx):
    spots = [(z, x) for z in range(NZ) for x in range(NH)]
    index = lambda z, x: (z % NZ) * NH + x % NH
    return [(index(z, x), index(z + dz, x + dx)) for z, x in spots]


def move(value, dy=0, dx=0, dc=0):
    return lax.ppermute(value, "blk", blk_moves(dy, dx, dc))


def move_row(value, dz=0, dx=0):
    return lax.ppermute(value, "row", row_moves(dz, dx))


def together(*values):
    return lax.optimization_barrier(values)


def live_slot(live, n):
    if n == 0:
        return jnp.where(live[0] == 1, 0, jnp.where(live[1] == 1, 1, 2))
    return jnp.where(live[3] == 1, 3, jnp.where(live[2] == 1, 2, 1))


def pick_kernel(live, columns, out, sems):
    copies = []
    for n in range(2):
        start = pl.multiple_of(live_slot(live, n) * TILE, TILE)
        for h in range(2):
            source = columns.at[pl.ds(h * HALF, HALF), pl.ds(start, TILE)]
            copies.append(pltpu.make_async_copy(source, out.at[2 * h + n], sems.at[n, h]))
    for copy in copies:
        copy.start()
    for copy in copies:
        copy.wait()


def pick_live(live_pairs, columns):
    return pl.pallas_call(
        pick_kernel,
        out_shape=jax.ShapeDtypeStruct((4, HALF, TILE), columns.dtype),
        in_specs=[pl.BlockSpec(memory_space=pltpu.SMEM), pl.BlockSpec(memory_space=pltpu.HBM)],
        out_specs=pl.BlockSpec(memory_space=pltpu.VMEM),
        scratch_shapes=[pltpu.SemaphoreType.DMA((2, 2))],
        compiler_params=pltpu.CompilerParams(vmem_limit_bytes=4 * MIB),
        name="pick_live",
    )(live_pairs, columns)


def load_kernel(live, amps, after, out, token, sems):
    token[...] = jnp.zeros_like(token)
    copies = []
    for n in range(2):
        for k in range(KT):
            start = pl.multiple_of(live_slot(live, n) * TILE + k * STEP, STEP)
            at = n * KT + k
            copies.append(pltpu.make_async_copy(amps.at[:, pl.ds(start, STEP)], out.at[at], sems.at[at]))
    for copy in copies:
        copy.start()
    for copy in copies:
        copy.wait()


def load_live(live_pairs, amplitudes, after):
    rows = amplitudes.shape[0]
    return pl.pallas_call(
        load_kernel,
        out_shape=(
            jax.ShapeDtypeStruct((2 * KT, rows, STEP), amplitudes.dtype),
            jax.ShapeDtypeStruct((8, 128), jnp.float32),
        ),
        in_specs=[pl.BlockSpec(memory_space=pltpu.SMEM)] + [pl.BlockSpec(memory_space=pl.ANY)] * 2,
        out_specs=(pl.BlockSpec(memory_space=pltpu.VMEM),) * 2,
        scratch_shapes=[pltpu.SemaphoreType.DMA((2 * KT,))],
        compiler_params=pltpu.CompilerParams(vmem_limit_bytes=40 * MIB),
        name="load_live",
    )(live_pairs, amplitudes, after)


def ladder_kernel(places, e, count, amps, cycle, before, *refs):
    pieces, outs, (token, total) = refs[:count], refs[count : count + NZ], refs[count + NZ :]
    token[...] = jnp.zeros_like(token)
    for n in range(2):
        held = {}
        for piece, index, slot, *place in places:
            if slot == n:
                held[tuple(place)] = pieces[piece].at[index] if index else pieces[piece]
        for k in range(KT):
            cols = slice(k * STEP, (k + 1) * STEP)
            block = jnp.concatenate(
                [held[dy, g, h][:, cols] for dy in range(NY) for g in range(NC) for h in range(2)]
            )
            term = lax.dot_general(
                block, amps[n * KT + k], (((1,), (1,)), ((), ())), preferred_element_type=jnp.float32
            )
            if n == k == 0:
                total[...] = term
            else:
                total[...] += term

    spot = lax.axis_index("blk")
    y, x, c = spot // (NX * NC), (spot // NC) % NX, spot % NC
    z = lax.axis_index("row") // NH
    for dz in range(NZ):
        dy = (z + dz + NY - y) % NY
        for core in range(NC):
            here = (dy * NC + (core + NC - c) % NC) * SB
            there = ((((z + dz) % NZ) * NX + (x + e) % NX) * NC + core) * SB
            there = pl.ds(pl.multiple_of(there, SB), SB)
            outs[dz][core * SB : (core + 1) * SB, :] = total[
                pl.ds(pl.multiple_of(here, SB), SB), :
            ] + jnp.concatenate([cycle[n, there, :] for n in range(cycle.shape[0])], axis=1)


def ladder(e, amplitudes, cycle, before, pieces):
    places = [(n, *place) for n, (_, held) in enumerate(pieces) for place in held]
    places = [(n, index, slot, dy % NY, g, h) for n, index, slot, dy, g, h in places]
    rows, q = amplitudes.shape[1], NY * NC * SB
    out = jax.ShapeDtypeStruct((q // NZ, rows), jnp.float32)
    return pl.pallas_call(
        functools.partial(ladder_kernel, places, e, len(pieces)),
        out_shape=(out,) * NZ + (jax.ShapeDtypeStruct((8, 128), jnp.float32),),
        in_specs=[pl.BlockSpec(memory_space=pltpu.VMEM)] * (3 + len(pieces)),
        out_specs=[pl.BlockSpec(memory_space=pltpu.VMEM)] * (NZ + 1),
        scratch_shapes=[pltpu.VMEM((q, rows), jnp.float32)],
        compiler_params=pltpu.CompilerParams(vmem_limit_bytes=24 * MIB),
        cost_estimate=pl.CostEstimate(
            flops=2 * q * rows * 2 * TILE, bytes_accessed=2 * q * 2 * TILE, transcendentals=0
        ),
        name="ladder",
    )(amplitudes, cycle, before, *[array for array, _ in pieces])


def pack_kernel(*refs):
    *blocks, out = refs
    for e, block in enumerate(blocks):
        for n in range(block.shape[0] // HALF):
            at = (e * (block.shape[0] // HALF) + n) * block.shape[1]
            out[0, :, at : at + block.shape[1]] = block[n * HALF : (n + 1) * HALF, :]


def pack(*blocks):
    return pl.pallas_call(
        pack_kernel,
        out_shape=jax.ShapeDtypeStruct((1, HALF, TILE), blocks[0].dtype),
        in_specs=[pl.BlockSpec(memory_space=pltpu.VMEM)] * len(blocks),
        out_specs=pl.BlockSpec(memory_space=pltpu.VMEM),
        compiler_params=pltpu.CompilerParams(vmem_limit_bytes=4 * MIB),
        name="pack",
    )(*blocks)


def cycle_kernel(places, width, slab_amps, token, *refs):
    blocks, out, turned, rows_of = refs[:-3], refs[-3], refs[-2], refs[-1]
    k_local, i_local, ac = slab_amps.shape
    a_all, per = ac // SB, rows_of.shape[-1] // SB
    for part in range(k_local // per):
        held = [slab_amps[part * per + n].astype(jnp.float32) for n in range(per)]
        for a in range(a_all):
            row = jnp.concatenate([k[:, a * SB : (a + 1) * SB] for k in held], axis=1)
            rows_of[part, pl.ds(a, i_local, stride=a_all), :] = row
    slab = jnp.concatenate([rows_of[part] for part in range(k_local // per)], axis=1).astype(jnp.bfloat16)
    spot = lax.axis_index("blk")
    y, x, c = spot // (NX * NC), (spot // NC) % NX, spot % NC
    pairs, depth = slab.shape
    for piece, index, half, dy, e, g in places:
        tiles = []
        for n in range(depth // HALF):
            at = (half * (depth // HALF) + n) * width
            tiles.append(blocks[piece][(*index, slice(None), slice(at, at + width))])
        term = jnp.dot(slab, jnp.concatenate(tiles), preferred_element_type=jnp.float32)
        block = ((y + dy) % NY * NX + (x + e) % NX) * NC + (c + g) % NC
        turned[pl.ds(pl.multiple_of(block * width, width), width), :] = term.T
    for b in range(SB):
        rows = turned[pl.ds(b, OW, stride=SB), :].T
        for i in range(0, pairs // a_all, 2):
            both = [rows[at * a_all : (at + 1) * a_all] for at in (i, i + 1)]
            out[i // 2, pl.ds(b, a_all, stride=SB), :] = jnp.concatenate(both, axis=1)


def cycle_sums(slab_amplitudes, pieces, token):
    k_local, i_local, ac = slab_amplitudes.shape
    a_all, depth = ac // SB, k_local * SB
    arrays = list({id(array): array for array, *_ in pieces}.values())
    order = [id(array) for array in arrays]
    places = [(order.index(id(array)), index, half, dy % NY, e, g) for array, index, half, dy, e, g in pieces]
    width = OW * SB // (NY * NX * NC)
    return pl.pallas_call(
        functools.partial(cycle_kernel, places, width),
        out_shape=jax.ShapeDtypeStruct((i_local // 2, a_all * SB, 2 * OW), jnp.float32),
        in_specs=[pl.BlockSpec(memory_space=pltpu.VMEM)] * (2 + len(arrays)),
        out_specs=pl.BlockSpec(memory_space=pltpu.VMEM),
        scratch_shapes=[
            pltpu.VMEM((OW * SB, i_local * a_all), jnp.float32),
            pltpu.VMEM((depth // LANES, i_local * a_all, LANES), jnp.float32),
        ],
        compiler_params=pltpu.CompilerParams(vmem_limit_bytes=16 * MIB),
        cost_estimate=pl.CostEstimate(
            flops=2 * i_local * a_all * depth * OW * SB, bytes_accessed=8 * MIB, transcendentals=0
        ),
        name="cycle",
    )(slab_amplitudes, token, *arrays)


def sum_along_z(parts):
    total = parts[0]
    for dz in range(1, NZ):
        total = total + move_row(parts[dz], dz=dz)
    return total


def per_device(amplitudes, integrals, live_pairs, slab_amplitudes, cycle_integrals):
    def swap(*arrays):
        return (jnp.concatenate(arrays), move(jnp.concatenate(arrays), dc=1))

    own = pick_live(live_pairs, integrals.T)
    below, above, beside = move(own, dy=1), move(own, dy=-1), move(own, dx=1)
    cycle_beside, cycle_far = move(cycle_integrals, dx=1), move(cycle_integrals, dy=2)
    live_amps, token = load_live(live_pairs, amplitudes, own)
    cycle_beside, token = together(cycle_beside, token)
    pair = pack(cycle_integrals, cycle_beside)
    below, above, beside, cycle_far, pair, token = together(below, above, beside, cycle_far, pair, token)

    far = pack(cycle_far)
    from_below = move(jnp.concatenate([below[0:2], beside[0:2], pair]), dy=1)
    from_above = move(jnp.concatenate([above[2:4], beside[0:2], pair]), dy=-1)
    across = move(jnp.concatenate([below[2:4], above[2:4], far]), dx=1)
    hop = swap(own, below, above, beside, pair, far)

    from_below, from_above, across = together(from_below, from_above, across)
    last_below = move(jnp.concatenate([from_below[2:3], across[0:1]]), dy=1)
    last_above = move(jnp.concatenate([from_above[3:4], across[3:4]]), dy=-1)
    hop_near = swap(from_below[0:2], from_above[0:2], from_below[4:5], from_above[4:5], across[4:5])
    hop_far = swap(from_below[2:4], from_above[2:4], across[0:4])

    blocks = []
    for g in range(NC):
        for e in range(2):
            blocks += [(hop[g], (16,), e, 0, e, g), (hop_near[g], (4,), e, -1, e, g), (hop_near[g], (5,), e, 1, e, g)]
        blocks += [(hop[g], (17,), 0, 2, 0, g), (hop_near[g], (6,), 0, 2, 1, g)]
    cycle = cycle_sums(slab_amplitudes, blocks, token)
    token, hop_1 = together(token, hop_far[1])
    hop_far = (hop_far[0], hop_1)

    halves = [(h, n) for h in range(2) for n in range(2)]
    near = []
    for g in range(NC):
        places = [((4 * at + 2 * h + n,), n, dy, g, h) for at, dy in enumerate((0, -1, 1)) for h, n in halves]
        near += [(hop[g], places), (hop_near[g], [((2 * h + n,), n, 2, g, h) for h, n in halves])]
    *near, token = ladder(0, live_amps, cycle, token, near)
    near = sum_along_z(near)

    last_below, last_above, token = together(last_below, last_above, token)
    far = []
    for g in range(NC):
        places = [((2 * at + n,), n, dy, g, 0) for at, dy in enumerate((-1, 1)) for n in range(2)]
        places += [((4 + 2 * at + n,), n, dy, g, 1) for at, dy in enumerate((-1, 1)) for n in range(2)]
        far += [(hop[g], [((12 + 2 * h + n,), n, 0, g, h) for h, n in halves]), (hop_far[g], places)]
    for g, both in enumerate(swap(last_below, last_above)):
        far.append((both, [((2 * n + h,), n, 2, g, h) for h, n in halves]))
    far = sum_along_z(ladder(1, live_amps, cycle, token, far)[:NZ])

    mine = lax.axis_index("row") % NH == (lax.axis_index("blk") // NC) % NX
    total = jnp.where(mine, near, far) + move_row(jnp.where(mine, far, near), dx=1)
    return total.astype(jnp.bfloat16).T


def solution(mesh):
    return jax.shard_map(
        per_device,
        mesh=mesh,
        in_specs=(
            P("blk", "row"),
            P("row", "blk"),
            P("row"),
            P("row", "blk", None),
            P("row", "blk"),
        ),
        out_specs=P("blk", "row"),
        check_vma=False,
    )
```

time: 80.5 us -> 76.7 us (0.953)
  starting transfers between devices: 30 us -> 27.3 us
  local copies, waits for them, and re-layouts: 4.09 us -> 2.36 us
    ppermute x20 -> x14, starting transfers between devices: 17.4 us -> 14.2 us  [move(): return lax.ppermute(value, 'blk', blk_moves(dy, dx, dc))]
    reshape x3 -> x0, local copies, waits for them, and re-layouts: 1.39 us -> none  [the longest x2 1.21 us: slab_matrix(): slab_amplitudes.reshape(k_local, i_local, ac // SB, SB)]
    ppermute x20 -> x14, waiting for transfers between devices: 22.4 us -> 23.5 us  [move(): return lax.ppermute(value, 'blk', blk_moves(dy, dx, dc))]
    unnamed x8 -> x16, local copies, waits for them, and re-layouts: 2.53 us -> 2.08 us
  transfers between devices with their start and end apart: 27 -> 21, of which waited for: 10 -> 9; matrix products, arithmetic and copies ran while one was open for 2% -> 1% of each run, Pallas kernels for 14% -> 15%
where the time goes in v4:
time: 76.7 us; the launch traced here: 76.6 us
  waiting for transfers between devices  33.2 us (43%)
  starting transfers between devices  27.3 us (36%)
  Pallas kernels  12.3 us (16%)
  local copies, waits for them, and re-layouts  2.36 us (3%)
  other arithmetic  1.13 us (1%)
    ppermute x14, waiting for transfers between devices, move(): return lax.ppermute(value, 'blk', blk_moves(dy, dx, dc))  23.5 us
    ppermute x14, starting transfers between devices, move(): return lax.ppermute(value, 'blk', blk_moves(dy, dx, dc))  14.2 us
    ppermute x7, starting transfers between devices, move_row(): return lax.ppermute(value, 'row', row_moves(dz, dx))  13.1 us
    ppermute x7, waiting for transfers between devices, move_row(): return lax.ppermute(value, 'row', row_moves(dz, dx))  9.65 us
    pallas_call x2, Pallas kernels, ladder(): pl.pallas_call(functools.partial(ladder_kernel, places, e, len(pieces)),...  5.24 us
    pallas_call x1, Pallas kernels, load_live(): pl.pallas_call(load_kernel, out_shape=(jax.ShapeDtypeStruct((2 * KT, rows...  4.05 us
    pallas_call x1, Pallas kernels, cycle_sums(): pl.pallas_call(functools.partial(cycle_kernel, places, width), out_shape=...  2.09 us
    unnamed x16, local copies, waits for them, and re-layouts  2.08 us
  transfers between devices with their start and end apart: 21, of which 9 were waited for; matrix products, arithmetic and copies ran while one was open for 1% of the time, Pallas kernels for 15%

profile of v4, /device:TPU:0, one launch (start us, length us, event | category | flops | bytes accessed | tf_op | source)
XLA Modules:
  0.0 76.6 jit_solution(16770759344069150626)
XLA Ops:
  0.0 0.0 copy-start.4
  0.0 0.0 copy-start
  0.0 1.2 %copy-done = bf16[16384,32]{0,1:T(8,128)(2,1)S(1)} copy-done((bf16[16384,32]{0,1:T(8,128)(2,1)S(1)}, bf16[16384,32]{0,1:T(8,128)(2,1)}, u32[]{:S(2)}) %copy-start) | copy-done | bytes 1048600
  1.2 0.0 copy-start.3
  1.2 0.7 copy-done.3
  1.9 0.9 %pick_live.1.after = bf16[4,16,4096]{2,1,0:T(8,128)(2,1)S(1)} custom-call(s32[4]{0:T(128)S(1)} %copy-done.3, bf16[32,16384]{1,0:T(8,128)(2,1)S(1)} %bitcast.3), custom_call_target="tpu_custom_call" | custom-call | tf_op jit(solution)/shard_map/pick_live/pallas_call | solution.py:67
  2.8 1.7 %collective-permute-start.2 = (bf16[4,16,4096]{2,1,0:T(8,128)(2,1)S(1)}, bf16[4,16,4096]{2,1,0:T(8,128)(2,1)S(1)}, u32[]{:S(2)}, u32[]{:S(2)}) collective-permute-start(bf16[4,16,4096]{2,1,0:T(8,128)(2,1)S(1)} %pick_live.1.after), channel_id=1, source_target_pairs={{0,2},{1,3},{2,0},{3,1},{4,6},{5,7},{6,4},{7,5},{8,10},{9,11},{10,... | collective-permute-start | bytes 1572872 | tf_op jit(solution)/shard_map/ppermute | solution.py:36
  4.5 3.0 %collective-permute-start.1 = (bf16[4,16,4096]{2,1,0:T(8,128)(2,1)S(1)}, bf16[4,16,4096]{2,1,0:T(8,128)(2,1)S(1)}, u32[]{:S(2)}, u32[]{:S(2)}) collective-permute-start(bf16[4,16,4096]{2,1,0:T(8,128)(2,1)S(1)} %pick_live.1.after), channel_id=1, source_target_pairs={{0,12},{1,13},{2,14},{3,15},{4,0},{5,1},{6,2},{7,3},{8,4},{9,5},{1... | collective-permute-start | bytes 1572872 | tf_op jit(solution)/shard_map/ppermute | solution.py:36
  7.5 0.0 collective-permute-start
  7.5 2.2 %collective-permute-start.3 = (bf16[256,128]{1,0:T(8,128)(2,1)}, bf16[256,128]{1,0:T(8,128)(2,1)S(1)}, u32[]{:S(2)}, u32[]{:S(2)}) collective-permute-start(bf16[256,128]{1,0:T(8,128)(2,1)} %refs_0_.1), channel_id=1, source_target_pairs={{0,8},{1,9},{2,10},{3,11},{4,12},{5,13},{6,14},{7,15},{8,0},{9,1},... | collective-permute-start | bytes 196616 | tf_op jit(solution)/shard_map/ppermute | solution.py:36
  9.7 0.5 collective-permute-start.4
  10.3 0.0 copy-done.4
  10.3 0.0 copy-start.2
  10.3 4.1 %load_live.1 = (bf16[8,512,1024]{2,1,0:T(8,128)(2,1)S(1)}, f32[8,128]{1,0:T(8,128)S(1)}) custom-call(s32[4]{0:T(128)S(1)} %copy-done.4, bf16[512,16384]{1,0:T(8,128)(2,1)} %amps.1, bf16[4,16,4096]{2,1,0:T(8,128)(2,1)S(1)} %pick_live.1.after), custom_call_target="tpu_custom_call" | custom-call | tf_op jit(solution)/shard_map/load_live/pallas_call | solution.py:94
  14.4 3.4 %collective-permute-done.4.refs_1_ = bf16[256,128]{1,0:T(8,128)(2,1)S(1)} collective-permute-done((bf16[256,128]{1,0:T(8,128)(2,1)}, bf16[256,128]{1,0:T(8,128)(2,1)S(1)}, u32[]{:S(2)}, u32[]{:S(2)}) %collective-permute-start.4) | collective-permute-done | bytes 65568 | tf_op jit(solution)/shard_map/ppermute | solution.py:36
  17.8 0.0 copy-done.2
  17.8 4.5 %collective-permute-done.3.refs_0_ = bf16[256,128]{1,0:T(8,128)(2,1)S(1)} collective-permute-done((bf16[256,128]{1,0:T(8,128)(2,1)}, bf16[256,128]{1,0:T(8,128)(2,1)S(1)}, u32[]{:S(2)}, u32[]{:S(2)}) %collective-permute-start.3) | collective-permute-done | bytes 65568 | tf_op jit(solution)/shard_map/ppermute | solution.py:36
  22.3 0.0 collective-permute-done.2
  22.3 0.0 collective-permute-done.1
  22.3 0.9 %collective-permute-done = bf16[4,16,4096]{2,1,0:T(8,128)(2,1)S(1)} collective-permute-done((bf16[4,16,4096]{2,1,0:T(8,128)(2,1)S(1)}, bf16[4,16,4096]{2,1,0:T(8,128)(2,1)S(1)}, u32[]{:S(2)}, u32[]{:S(2)}) %collective-permute-start) | collective-permute-done | bytes 524320 | tf_op jit(solution)/shard_map/ppermute | solution.py:36
  23.5 0.2 pad_maximum_fusion.1
  23.7 0.4 collective-permute-start.6
  24.1 1.7 %collective-permute-start.5 = (bf16[5,16,4096]{2,1,0:T(8,128)(2,1)S(1)}, bf16[5,16,4096]{2,1,0:T(8,128)(2,1)S(1)}, u32[]{:S(2)}, u32[]{:S(2)}) collective-permute-start(bf16[5,16,4096]{2,1,0:T(8,128)(2,1)S(1)} %get-tuple-element.76), channel_id=1, source_target_pairs={{0,4},{1,5},{2,6},{3,7},{4,8},{5,9},{6,10},{7,11},{8,12},{9,13},{1... | collective-permute-start | bytes 1966088 | tf_op jit(solution)/shard_map/ppermute | solution.py:36
  25.8 0.5 collective-permute-start.7
  26.4 0.1 collective-permute-start.8
  26.5 11.6 %collective-permute-done.6 = bf16[5,16,4096]{2,1,0:T(8,128)(2,1)S(1)} collective-permute-done((bf16[5,16,4096]{2,1,0:T(8,128)(2,1)S(1)}, bf16[5,16,4096]{2,1,0:T(8,128)(2,1)S(1)}, u32[]{:S(2)}, u32[]{:S(2)}) %collective-permute-start.6) | collective-permute-done | bytes 655392 | tf_op jit(solution)/shard_map/ppermute | solution.py:36
  38.1 1.5 %collective-permute-done.5 = bf16[5,16,4096]{2,1,0:T(8,128)(2,1)S(1)} collective-permute-done((bf16[5,16,4096]{2,1,0:T(8,128)(2,1)S(1)}, bf16[5,16,4096]{2,1,0:T(8,128)(2,1)S(1)}, u32[]{:S(2)}, u32[]{:S(2)}) %collective-permute-start.5) | collective-permute-done | bytes 655392 | tf_op jit(solution)/shard_map/ppermute | solution.py:36
  39.6 0.0 collective-permute-done.7
  39.7 0.0 copy-start.1
  39.7 0.1 pad_maximum_fusion.refs_1_
  39.9 0.1 collective-permute-start.10
  40.0 0.6 collective-permute-start.9
  40.6 0.3 collective-permute-start.14
  40.9 3.1 %collective-permute-start.15 = (bf16[2,16,4096]{2,1,0:T(8,128)(2,1)S(1)}, bf16[2,16,4096]{2,1,0:T(8,128)(2,1)S(1)}, u32[]{:S(2)}, u32[]{:S(2)}) collective-permute-start(bf16[2,16,4096]{2,1,0:T(8,128)(2,1)S(1)} %pad_maximum_fusion.7), channel_id=1, source_target_pairs={{0,12},{1,13},{2,14},{3,15},{4,0},{5,1},{6,2},{7,3},{8,4},{9,5},{1... | collective-permute-start | bytes 786440 | tf_op jit(solution)/shard_map/ppermute | solution.py:36
  44.0 0.0 collective-permute-done.10.refs_3_
  44.0 0.0 collective-permute-done.9.refs_3_
  44.0 0.0 collective-permute-done.8.refs_2_
  44.0 0.0 copy-done.1
  44.0 2.1 %cycle.1 = f32[4,512,128]{2,1,0:T(8,128)S(1)} custom-call(bf16[8,8,512]{2,1,0:T(8,128)(2,1)S(1)} %copy-done.1, f32[8,128]{1,0:T(8,128)S(1)} %get-tuple-element.45.token.before, bf16[18,16,4096]{2,1,0:T(8,128)(2,1)S(1)} %constant_dynamic-update-slice_fusion.refs_0_, bf16[7,16,4096]{2,1,0:T(8,128)(2,1)S(1)} %get-tuple-element.66.refs_1_, ...), custom_call_target="tpu_custom_call" | custom-call | flops 134217728 | bytes 8388608 | tf_op jit(solution)/shard_map/cycle/pallas_call | solution.py:216
  46.1 2.4 %ladder.2 = (f32[64,512]{1,0:T(8,128)S(1)}, f32[64,512]{1,0:T(8,128)S(1)}, f32[64,512]{1,0:T(8,128)S(1)}, f32[64,512]{1,0:T(8,128)S(1)}, f32[8,128]{1,0:T(8,128)S(1)}) custom-call(bf16[8,512,1024]{2,1,0:T(8,128)(2,1)S(1)} %get-tuple-element.32.amps, f32[4,512,128]{2,1,0:T(8,128)S(1)} %cycle.1, f32[8,128]{1,0:T(8,128)S(1)} %get-tuple-element.45.token.before, ...), custom_call_target="tpu_custom_call" | custom-call | flops 2147483648 | bytes 4194304 | tf_op jit(solution)/shard_map/ladder/pallas_call | solution.py:148
  48.6 1.6 %collective-permute-done.14 = bf16[2,16,4096]{2,1,0:T(8,128)(2,1)S(1)} collective-permute-done((bf16[2,16,4096]{2,1,0:T(8,128)(2,1)S(1)}, bf16[2,16,4096]{2,1,0:T(8,128)(2,1)S(1)}, u32[]{:S(2)}, u32[]{:S(2)}) %collective-permute-start.14) | collective-permute-done | bytes 262176 | tf_op jit(solution)/shard_map/ppermute | solution.py:36
  50.1 0.0 collective-permute-done.15
  50.2 0.1 collective-permute-start.16
  50.3 2.0 %collective-permute-start.11 = (f32[64,512]{1,0:T(8,128)S(1)}, f32[64,512]{1,0:T(8,128)S(1)}, u32[]{:S(2)}, u32[]{:S(2)}) collective-permute-start(f32[64,512]{1,0:T(8,128)S(1)} %get-tuple-element.47), channel_id=1, source_target_pairs={{0,32},{16,48},{32,64},{48,80},{64,96},{80,112},{96,0},{112,16},{1... | collective-permute-start | bytes 393224 | tf_op jit(solution)/shard_map/ppermute | solution.py:40
  52.3 3.6 %collective-permute-start.12 = (f32[64,512]{1,0:T(8,128)S(1)}, f32[64,512]{1,0:T(8,128)S(1)}, u32[]{:S(2)}, u32[]{:S(2)}) collective-permute-start(f32[64,512]{1,0:T(8,128)S(1)} %get-tuple-element.48), channel_id=1, source_target_pairs={{0,64},{16,80},{32,96},{48,112},{64,0},{80,16},{96,32},{112,48},{1... | collective-permute-start | bytes 393224 | tf_op jit(solution)/shard_map/ppermute | solution.py:40
  55.8 1.0 %collective-permute-start.13 = (f32[64,512]{1,0:T(8,128)S(1)}, f32[64,512]{1,0:T(8,128)S(1)}, u32[]{:S(2)}, u32[]{:S(2)}) collective-permute-start(f32[64,512]{1,0:T(8,128)S(1)} %get-tuple-element.49), channel_id=1, source_target_pairs={{0,96},{16,112},{32,0},{48,16},{64,32},{80,48},{96,64},{112,80},{1... | collective-permute-start | bytes 393224 | tf_op jit(solution)/shard_map/ppermute | solution.py:40
  56.9 0.0 collective-permute-done.16.refs_5_
  56.9 2.8 %ladder.3 = (f32[64,512]{1,0:T(8,128)S(1)}, f32[64,512]{1,0:T(8,128)S(1)}, f32[64,512]{1,0:T(8,128)S(1)}, f32[64,512]{1,0:T(8,128)S(1)}, f32[8,128]{1,0:T(8,128)}) custom-call(bf16[8,512,1024]{2,1,0:T(8,128)(2,1)S(1)} %get-tuple-element.32.amps, f32[4,512,128]{2,1,0:T(8,128)S(1)} %cycle.1, f32[8,128]{1,0:T(8,128)S(1)} %get-tuple-element.51.before, ...), custom_call_target="tpu_custom_call" | custom-call | flops 2147483648 | bytes 4194304 | tf_op jit(solution)/shard_map/ladder/pallas_call | solution.py:148
  59.7 1.0 %collective-permute-start.17 = (f32[64,512]{1,0:T(8,128)S(1)}, f32[64,512]{1,0:T(8,128)S(1)}, u32[]{:S(2)}, u32[]{:S(2)}) collective-permute-start(f32[64,512]{1,0:T(8,128)S(1)} %get-tuple-element.56), channel_id=1, source_target_pairs={{0,32},{16,48},{32,64},{48,80},{64,96},{80,112},{96,0},{112,16},{1... | collective-permute-start | bytes 393224 | tf_op jit(solution)/shard_map/ppermute | solution.py:40
  60.7 0.5 collective-permute-start.18
  61.1 0.0 collective-permute-done.11
  61.1 2.2 %collective-permute-start.19 = (f32[64,512]{1,0:T(8,128)S(1)}, f32[64,512]{1,0:T(8,128)S(1)}, u32[]{:S(2)}, u32[]{:S(2)}) collective-permute-start(f32[64,512]{1,0:T(8,128)S(1)} %get-tuple-element.58), channel_id=1, source_target_pairs={{0,96},{16,112},{32,0},{48,16},{64,32},{80,48},{96,64},{112,80},{1... | collective-permute-start | bytes 393224 | tf_op jit(solution)/shard_map/ppermute | solution.py:40
  63.4 0.0 collective-permute-done.12
  63.4 0.0 collective-permute-done.13
  63.4 5.3 %collective-permute-done.17 = f32[64,512]{1,0:T(8,128)S(1)} collective-permute-done((f32[64,512]{1,0:T(8,128)S(1)}, f32[64,512]{1,0:T(8,128)S(1)}, u32[]{:S(2)}, u32[]{:S(2)}) %collective-permute-start.17) | collective-permute-done | bytes 131104 | tf_op jit(solution)/shard_map/ppermute | solution.py:40
  68.7 0.0 collective-permute-done.18
  68.7 0.6 collective-permute-done.19
  69.3 0.1 broadcast_select_fusion
  69.4 2.8 %collective-permute-start.20 = (f32[64,512]{1,0:T(8,128)S(1)}, f32[64,512]{1,0:T(8,128)S(1)}, u32[]{:S(2)}, u32[]{:S(2)}) collective-permute-start(f32[64,512]{1,0:T(8,128)S(1)} %get-tuple-element.59), channel_id=1, source_target_pairs={{0,16},{16,0},{32,48},{48,32},{64,80},{80,64},{96,112},{112,96},{1... | collective-permute-start | bytes 393224 | tf_op jit(solution)/shard_map/ppermute | solution.py:40
  72.2 3.7 %collective-permute-done.20 = f32[64,512]{1,0:T(8,128)S(1)} collective-permute-done((f32[64,512]{1,0:T(8,128)S(1)}, f32[64,512]{1,0:T(8,128)S(1)}, u32[]{:S(2)}, u32[]{:S(2)}) %collective-permute-start.20) | collective-permute-done | bytes 131104 | tf_op jit(solution)/shard_map/ppermute | solution.py:40
  75.9 0.7 fusion
  (21 shorter events, 0.5 us)
Async XLA Ops:
  0.0 10.3 %copy-start.4 = (s32[4]{0:T(128)S(1)}, s32[4]{0:T(128)}, u32[]{:S(2)}) copy-start(s32[4]{0:T(128)} %live.3) | copy-start | bytes 52
  0.0 1.2 %copy-start = (bf16[16384,32]{0,1:T(8,128)(2,1)S(1)}, bf16[16384,32]{0,1:T(8,128)(2,1)}, u32[]{:S(2)}) copy-start(bf16[16384,32]{0,1:T(8,128)(2,1)} %param.6) | copy-start | bytes 3145732
  1.2 0.7 copy-start.3
  2.8 19.5 %collective-permute-start.2 = (bf16[4,16,4096]{2,1,0:T(8,128)(2,1)S(1)}, bf16[4,16,4096]{2,1,0:T(8,128)(2,1)S(1)}, u32[]{:S(2)}, u32[]{:S(2)}) collective-permute-start(bf16[4,16,4096]{2,1,0:T(8,128)(2,1)S(1)} %pick_live.1.after), channel_id=1, source_target_pairs={{0,2},{1,3},{2,0},{3,1},{4,6},{5,7},{6,4},{7,5},{8,10},{9,11},{10,... | collective-permute-start | bytes 1572872 | tf_op jit(solution)/shard_map/ppermute | solution.py:36
  4.5 17.8 %collective-permute-start.1 = (bf16[4,16,4096]{2,1,0:T(8,128)(2,1)S(1)}, bf16[4,16,4096]{2,1,0:T(8,128)(2,1)S(1)}, u32[]{:S(2)}, u32[]{:S(2)}) collective-permute-start(bf16[4,16,4096]{2,1,0:T(8,128)(2,1)S(1)} %pick_live.1.after), channel_id=1, source_target_pairs={{0,12},{1,13},{2,14},{3,15},{4,0},{5,1},{6,2},{7,3},{8,4},{9,5},{1... | collective-permute-start | bytes 1572872 | tf_op jit(solution)/shard_map/ppermute | solution.py:36
  7.5 15.7 %collective-permute-start = (bf16[4,16,4096]{2,1,0:T(8,128)(2,1)S(1)}, bf16[4,16,4096]{2,1,0:T(8,128)(2,1)S(1)}, u32[]{:S(2)}, u32[]{:S(2)}) collective-permute-start(bf16[4,16,4096]{2,1,0:T(8,128)(2,1)S(1)} %pick_live.1.after), channel_id=1, source_target_pairs={{0,4},{1,5},{2,6},{3,7},{4,8},{5,9},{6,10},{7,11},{8,12},{9,13},{1... | collective-permute-start | bytes 1572872 | tf_op jit(solution)/shard_map/ppermute | solution.py:36
  7.5 14.8 %collective-permute-start.3 = (bf16[256,128]{1,0:T(8,128)(2,1)}, bf16[256,128]{1,0:T(8,128)(2,1)S(1)}, u32[]{:S(2)}, u32[]{:S(2)}) collective-permute-start(bf16[256,128]{1,0:T(8,128)(2,1)} %refs_0_.1), channel_id=1, source_target_pairs={{0,8},{1,9},{2,10},{3,11},{4,12},{5,13},{6,14},{7,15},{8,0},{9,1},... | collective-permute-start | bytes 196616 | tf_op jit(solution)/shard_map/ppermute | solution.py:36
  9.7 8.1 %collective-permute-start.4 = (bf16[256,128]{1,0:T(8,128)(2,1)}, bf16[256,128]{1,0:T(8,128)(2,1)S(1)}, u32[]{:S(2)}, u32[]{:S(2)}) collective-permute-start(bf16[256,128]{1,0:T(8,128)(2,1)} %refs_0_.1), channel_id=1, source_target_pairs={{0,2},{1,3},{2,0},{3,1},{4,6},{5,7},{6,4},{7,5},{8,10},{9,11},{10,... | collective-permute-start | bytes 196616 | tf_op jit(solution)/shard_map/ppermute | solution.py:36
  10.3 7.5 %copy-start.2 = (bf16[256,128]{1,0:T(8,128)(2,1)S(1)}, bf16[256,128]{1,0:T(8,128)(2,1)}, u32[]{:S(2)}) copy-start(bf16[256,128]{1,0:T(8,128)(2,1)} %refs_0_.1) | copy-start | bytes 196612
  23.7 14.4 %collective-permute-start.6 = (bf16[5,16,4096]{2,1,0:T(8,128)(2,1)S(1)}, bf16[5,16,4096]{2,1,0:T(8,128)(2,1)S(1)}, u32[]{:S(2)}, u32[]{:S(2)}) collective-permute-start(bf16[5,16,4096]{2,1,0:T(8,128)(2,1)S(1)} %get-tuple-element.75), channel_id=1, source_target_pairs={{0,12},{1,13},{2,14},{3,15},{4,0},{5,1},{6,2},{7,3},{8,4},{9,5},{1... | collective-permute-start | bytes 1966088 | tf_op jit(solution)/shard_map/ppermute | solution.py:36
  24.1 15.5 %collective-permute-start.5 = (bf16[5,16,4096]{2,1,0:T(8,128)(2,1)S(1)}, bf16[5,16,4096]{2,1,0:T(8,128)(2,1)S(1)}, u32[]{:S(2)}, u32[]{:S(2)}) collective-permute-start(bf16[5,16,4096]{2,1,0:T(8,128)(2,1)S(1)} %get-tuple-element.76), channel_id=1, source_target_pairs={{0,4},{1,5},{2,6},{3,7},{4,8},{5,9},{6,10},{7,11},{8,12},{9,13},{1... | collective-permute-start | bytes 1966088 | tf_op jit(solution)/shard_map/ppermute | solution.py:36
  25.8 13.8 %collective-permute-start.7 = (bf16[5,16,4096]{2,1,0:T(8,128)(2,1)S(1)}, bf16[5,16,4096]{2,1,0:T(8,128)(2,1)S(1)}, u32[]{:S(2)}, u32[]{:S(2)}) collective-permute-start(bf16[5,16,4096]{2,1,0:T(8,128)(2,1)S(1)} %get-tuple-element.77), channel_id=1, source_target_pairs={{0,2},{1,3},{2,0},{3,1},{4,6},{5,7},{6,4},{7,5},{8,10},{9,11},{10,... | collective-permute-start | bytes 1966088 | tf_op jit(solution)/shard_map/ppermute | solution.py:36
  26.4 17.7 %collective-permute-start.8 = (bf16[18,16,4096]{2,1,0:T(8,128)(2,1)S(1)}, bf16[18,16,4096]{2,1,0:T(8,128)(2,1)S(1)}, u32[]{:S(2)}, u32[]{:S(2)}) collective-permute-start(bf16[18,16,4096]{2,1,0:T(8,128)(2,1)S(1)} %constant_dynamic-update-slice_fusion.refs_0_), channel_id=1, source_target_pairs={{0,1},{1,0},{2,3},{3,2},{4,5},{5,4},{6,7},{7,6},{8,9},{9,8},{10,11... | collective-permute-start | bytes 7077896 | tf_op jit(solution)/shard_map/ppermute | solution.py:36
  39.7 4.3 %copy-start.1 = (bf16[8,8,512]{2,1,0:T(8,128)(2,1)S(1)}, bf16[8,8,512]{2,1,0:T(8,128)(2,1)}, u32[]{:S(2)}) copy-start(bf16[8,8,512]{2,1,0:T(8,128)(2,1)} %slab_amps.1) | copy-start | bytes 196612
  39.9 4.2 %collective-permute-start.10 = (bf16[8,16,4096]{2,1,0:T(8,128)(2,1)S(1)}, bf16[8,16,4096]{2,1,0:T(8,128)(2,1)S(1)}, u32[]{:S(2)}, u32[]{:S(2)}) collective-permute-start(bf16[8,16,4096]{2,1,0:T(8,128)(2,1)S(1)} %pad_maximum_fusion.refs_1_), channel_id=1, source_target_pairs={{0,1},{1,0},{2,3},{3,2},{4,5},{5,4},{6,7},{7,6},{8,9},{9,8},{10,11... | collective-permute-start | bytes 3145736 | tf_op jit(solution)/shard_map/ppermute | solution.py:36
  40.0 4.0 %collective-permute-start.9 = (bf16[7,16,4096]{2,1,0:T(8,128)(2,1)S(1)}, bf16[7,16,4096]{2,1,0:T(8,128)(2,1)S(1)}, u32[]{:S(2)}, u32[]{:S(2)}) collective-permute-start(bf16[7,16,4096]{2,1,0:T(8,128)(2,1)S(1)} %get-tuple-element.66.refs_1_), channel_id=1, source_target_pairs={{0,1},{1,0},{2,3},{3,2},{4,5},{5,4},{6,7},{7,6},{8,9},{9,8},{10,11... | collective-permute-start | bytes 2752520 | tf_op jit(solution)/shard_map/ppermute | solution.py:36
  40.6 9.5 %collective-permute-start.14 = (bf16[2,16,4096]{2,1,0:T(8,128)(2,1)S(1)}, bf16[2,16,4096]{2,1,0:T(8,128)(2,1)S(1)}, u32[]{:S(2)}, u32[]{:S(2)}) collective-permute-start(bf16[2,16,4096]{2,1,0:T(8,128)(2,1)S(1)} %pad_maximum_fusion.6), channel_id=1, source_target_pairs={{0,4},{1,5},{2,6},{3,7},{4,8},{5,9},{6,10},{7,11},{8,12},{9,13},{1... | collective-permute-start | bytes 786440 | tf_op jit(solution)/shard_map/ppermute | solution.py:36
  40.9 9.2 %collective-permute-start.15 = (bf16[2,16,4096]{2,1,0:T(8,128)(2,1)S(1)}, bf16[2,16,4096]{2,1,0:T(8,128)(2,1)S(1)}, u32[]{:S(2)}, u32[]{:S(2)}) collective-permute-start(bf16[2,16,4096]{2,1,0:T(8,128)(2,1)S(1)} %pad_maximum_fusion.7), channel_id=1, source_target_pairs={{0,12},{1,13},{2,14},{3,15},{4,0},{5,1},{6,2},{7,3},{8,4},{9,5},{1... | collective-permute-start | bytes 786440 | tf_op jit(solution)/shard_map/ppermute | solution.py:36
  50.2 6.7 %collective-permute-start.16 = (bf16[4,16,4096]{2,1,0:T(8,128)(2,1)S(1)}, bf16[4,16,4096]{2,1,0:T(8,128)(2,1)S(1)}, u32[]{:S(2)}, u32[]{:S(2)}) collective-permute-start(bf16[4,16,4096]{2,1,0:T(8,128)(2,1)S(1)} %constant_dynamic-update-slice_fusion.6.refs_4_), channel_id=1, source_target_pairs={{0,1},{1,0},{2,3},{3,2},{4,5},{5,4},{6,7},{7,6},{8,9},{9,8},{10,11... | collective-permute-start | bytes 1572872 | tf_op jit(solution)/shard_map/ppermute | solution.py:36
  50.3 10.9 %collective-permute-start.11 = (f32[64,512]{1,0:T(8,128)S(1)}, f32[64,512]{1,0:T(8,128)S(1)}, u32[]{:S(2)}, u32[]{:S(2)}) collective-permute-start(f32[64,512]{1,0:T(8,128)S(1)} %get-tuple-element.47), channel_id=1, source_target_pairs={{0,32},{16,48},{32,64},{48,80},{64,96},{80,112},{96,0},{112,16},{1... | collective-permute-start | bytes 393224 | tf_op jit(solution)/shard_map/ppermute | solution.py:40
  52.3 11.1 %collective-permute-start.12 = (f32[64,512]{1,0:T(8,128)S(1)}, f32[64,512]{1,0:T(8,128)S(1)}, u32[]{:S(2)}, u32[]{:S(2)}) collective-permute-start(f32[64,512]{1,0:T(8,128)S(1)} %get-tuple-element.48), channel_id=1, source_target_pairs={{0,64},{16,80},{32,96},{48,112},{64,0},{80,16},{96,32},{112,48},{1... | collective-permute-start | bytes 393224 | tf_op jit(solution)/shard_map/ppermute | solution.py:40
  55.8 7.5 %collective-permute-start.13 = (f32[64,512]{1,0:T(8,128)S(1)}, f32[64,512]{1,0:T(8,128)S(1)}, u32[]{:S(2)}, u32[]{:S(2)}) collective-permute-start(f32[64,512]{1,0:T(8,128)S(1)} %get-tuple-element.49), channel_id=1, source_target_pairs={{0,96},{16,112},{32,0},{48,16},{64,32},{80,48},{96,64},{112,80},{1... | collective-permute-start | bytes 393224 | tf_op jit(solution)/shard_map/ppermute | solution.py:40
  59.7 9.0 %collective-permute-start.17 = (f32[64,512]{1,0:T(8,128)S(1)}, f32[64,512]{1,0:T(8,128)S(1)}, u32[]{:S(2)}, u32[]{:S(2)}) collective-permute-start(f32[64,512]{1,0:T(8,128)S(1)} %get-tuple-element.56), channel_id=1, source_target_pairs={{0,32},{16,48},{32,64},{48,80},{64,96},{80,112},{96,0},{112,16},{1... | collective-permute-start | bytes 393224 | tf_op jit(solution)/shard_map/ppermute | solution.py:40
  60.7 8.0 %collective-permute-start.18 = (f32[64,512]{1,0:T(8,128)S(1)}, f32[64,512]{1,0:T(8,128)S(1)}, u32[]{:S(2)}, u32[]{:S(2)}) collective-permute-start(f32[64,512]{1,0:T(8,128)S(1)} %get-tuple-element.57), channel_id=1, source_target_pairs={{0,64},{16,80},{32,96},{48,112},{64,0},{80,16},{96,32},{112,48},{1... | collective-permute-start | bytes 393224 | tf_op jit(solution)/shard_map/ppermute | solution.py:40
  61.1 8.1 %collective-permute-start.19 = (f32[64,512]{1,0:T(8,128)S(1)}, f32[64,512]{1,0:T(8,128)S(1)}, u32[]{:S(2)}, u32[]{:S(2)}) collective-permute-start(f32[64,512]{1,0:T(8,128)S(1)} %get-tuple-element.58), channel_id=1, source_target_pairs={{0,96},{16,112},{32,0},{48,16},{64,32},{80,48},{96,64},{112,80},{1... | collective-permute-start | bytes 393224 | tf_op jit(solution)/shard_map/ppermute | solution.py:40
  69.4 6.6 %collective-permute-start.20 = (f32[64,512]{1,0:T(8,128)S(1)}, f32[64,512]{1,0:T(8,128)S(1)}, u32[]{:S(2)}, u32[]{:S(2)}) collective-permute-start(f32[64,512]{1,0:T(8,128)S(1)} %get-tuple-element.59), channel_id=1, source_target_pairs={{0,16},{16,0},{32,48},{48,32},{64,80},{80,64},{96,112},{112,96},{1... | collective-permute-start | bytes 393224 | tf_op jit(solution)/shard_map/ppermute | solution.py:40

commit v5 on v4

--- a/solution.py
+++ b/solution.py
@@ -22,14 +22,13 @@
 
 def blk_moves(dy, dx, dc):
     spots = [(y, x, c) for y in range(NY) for x in range(NX) for c in range(NC)]
-    index = lambda y, x, c: ((y % NY) * NX + x % NX) * NC + c % NC
-    return [(index(y, x, c), index(y + dy, x + dx, c + dc)) for y, x, c in spots]
+    index = lambda y, x, c: (y * NX + x) * NC + c
+    return [(index(y, x, c), index(y ^ dy, x ^ dx, c ^ dc)) for y, x, c in spots]
 
 
 def row_moves(dz, dx):
     spots = [(z, x) for z in range(NZ) for x in range(NH)]
-    index = lambda z, x: (z % NZ) * NH + x % NH
-    return [(index(z, x), index(z + dz, x + dx)) for z, x in spots]
+    return [(z * NH + x, (z ^ dz) * NH + (x ^ dx)) for z, x in spots]
 
 
 def move(value, dy=0, dx=0, dc=0):
@@ -130,10 +129,10 @@
     y, x, c = spot // (NX * NC), (spot // NC) % NX, spot % NC
     z = lax.axis_index("row") // NH
     for dz in range(NZ):
-        dy = (z + dz + NY - y) % NY
+        dy = (z ^ dz) ^ y
         for core in range(NC):
-            here = (dy * NC + (core + NC - c) % NC) * SB
-            there = ((((z + dz) % NZ) * NX + (x + e) % NX) * NC + core) * SB
+            here = (dy * NC + (c ^ core)) * SB
+            there = (((z ^ dz) * NX + (x ^ e)) * NC + core) * SB
             there = pl.ds(pl.multiple_of(there, SB), SB)
             outs[dz][core * SB : (core + 1) * SB, :] = total[
                 pl.ds(pl.multiple_of(here, SB), SB), :
@@ -142,7 +141,6 @@
 
 def ladder(e, amplitudes, cycle, before, pieces):
     places = [(n, *place) for n, (_, held) in enumerate(pieces) for place in held]
-    places = [(n, index, slot, dy % NY, g, h) for n, index, slot, dy, g, h in places]
     rows, q = amplitudes.shape[1], NY * NC * SB
     out = jax.ShapeDtypeStruct((q // NZ, rows), jnp.float32)
     return pl.pallas_call(
@@ -197,7 +195,7 @@
             at = (half * (depth // HALF) + n) * width
             tiles.append(blocks[piece][(*index, slice(None), slice(at, at + width))])
         term = jnp.dot(slab, jnp.concatenate(tiles), preferred_element_type=jnp.float32)
-        block = ((y + dy) % NY * NX + (x + e) % NX) * NC + (c + g) % NC
+        block = ((y ^ dy) * NX + (x ^ e)) * NC + (c ^ g)
         turned[pl.ds(pl.multiple_of(block * width, width), width), :] = term.T
     for b in range(SB):
         rows = turned[pl.ds(b, OW, stride=SB), :].T
@@ -211,7 +209,7 @@
     a_all, depth = ac // SB, k_local * SB
     arrays = list({id(array): array for array, *_ in pieces}.values())
     order = [id(array) for array in arrays]
-    places = [(order.index(id(array)), index, half, dy % NY, e, g) for array, index, half, dy, e, g in pieces]
+    places = [(order.index(id(array)), index, half, dy, e, g) for array, index, half, dy, e, g in pieces]
     width = OW * SB // (NY * NX * NC)
     return pl.pallas_call(
         functools.partial(cycle_kernel, places, width),
@@ -232,7 +230,7 @@
 
 def sum_along_z(parts):
     total = parts[0]
-    for dz in range(1, NZ):
+    for dz in (1, 3, 2):
         total = total + move_row(parts[dz], dz=dz)
     return total
 
@@ -242,29 +240,29 @@
         return (jnp.concatenate(arrays), move(jnp.concatenate(arrays), dc=1))
 
     own = pick_live(live_pairs, integrals.T)
-    below, above, beside = move(own, dy=1), move(own, dy=-1), move(own, dx=1)
+    below, above, beside = move(own, dy=1), move(own, dy=3), move(own, dx=1)
     cycle_beside, cycle_far = move(cycle_integrals, dx=1), move(cycle_integrals, dy=2)
     live_amps, token = load_live(live_pairs, amplitudes, own)
     cycle_beside, token = together(cycle_beside, token)
     pair = pack(cycle_integrals, cycle_beside)
-    below, above, beside, cycle_far, pair, token = together(below, above, beside, cycle_far, pair, token)
+    beside, above, below, cycle_far, pair, token = together(beside, above, below, cycle_far, pair, token)
 
     far = pack(cycle_far)
-    from_below = move(jnp.concatenate([below[0:2], beside[0:2], pair]), dy=1)
-    from_above = move(jnp.concatenate([above[2:4], beside[0:2], pair]), dy=-1)
+    from_above = move(jnp.concatenate([below[0:2], beside[0:2], pair]), dy=3)
+    from_below = move(jnp.concatenate([above[2:4], beside[0:2], pair]), dy=1)
     across = move(jnp.concatenate([below[2:4], above[2:4], far]), dx=1)
     hop = swap(own, below, above, beside, pair, far)
 
-    from_below, from_above, across = together(from_below, from_above, across)
-    last_below = move(jnp.concatenate([from_below[2:3], across[0:1]]), dy=1)
-    last_above = move(jnp.concatenate([from_above[3:4], across[3:4]]), dy=-1)
-    hop_near = swap(from_below[0:2], from_above[0:2], from_below[4:5], from_above[4:5], across[4:5])
-    hop_far = swap(from_below[2:4], from_above[2:4], across[0:4])
+    from_above, from_below, across = together(from_above, from_below, across)
+    last_above = move(jnp.concatenate([from_below[2:3], across[0:1]]), dy=3)
+    last_below = move(jnp.concatenate([from_above[3:4], across[3:4]]), dy=1)
+    hop_near = swap(from_above[0:2], from_below[0:2], from_above[4:5], from_below[4:5], across[4:5])
+    hop_far = swap(from_above[2:4], from_below[2:4], across[0:4])
 
     blocks = []
     for g in range(NC):
         for e in range(2):
-            blocks += [(hop[g], (16,), e, 0, e, g), (hop_near[g], (4,), e, -1, e, g), (hop_near[g], (5,), e, 1, e, g)]
+            blocks += [(hop[g], (16,), e, 0, e, g), (hop_near[g], (4,), e, 3, e, g), (hop_near[g], (5,), e, 1, e, g)]
         blocks += [(hop[g], (17,), 0, 2, 0, g), (hop_near[g], (6,), 0, 2, 1, g)]
     cycle = cycle_sums(slab_amplitudes, blocks, token)
     token, hop_1 = together(token, hop_far[1])
@@ -273,18 +271,18 @@
     halves = [(h, n) for h in range(2) for n in range(2)]
     near = []
     for g in range(NC):
-        places = [((4 * at + 2 * h + n,), n, dy, g, h) for at, dy in enumerate((0, -1, 1)) for h, n in halves]
+        places = [((4 * at + 2 * h + n,), n, dy, g, h) for at, dy in enumerate((0, 1, 3)) for h, n in halves]
         near += [(hop[g], places), (hop_near[g], [((2 * h + n,), n, 2, g, h) for h, n in halves])]
     *near, token = ladder(0, live_amps, cycle, token, near)
     near = sum_along_z(near)
 
-    last_below, last_above, token = together(last_below, last_above, token)
+    last_above, last_below, token = together(last_above, last_below, token)
     far = []
     for g in range(NC):
-        places = [((2 * at + n,), n, dy, g, 0) for at, dy in enumerate((-1, 1)) for n in range(2)]
-        places += [((4 + 2 * at + n,), n, dy, g, 1) for at, dy in enumerate((-1, 1)) for n in range(2)]
+        places = [((2 * at + n,), n, dy, g, 0) for at, dy in enumerate((3, 1)) for n in range(2)]
+        places += [((4 + 2 * at + n,), n, dy, g, 1) for at, dy in enumerate((1, 3)) for n in range(2)]
         far += [(hop[g], [((12 + 2 * h + n,), n, 0, g, h) for h, n in halves]), (hop_far[g], places)]
-    for g, both in enumerate(swap(last_below, last_above)):
+    for g, both in enumerate(swap(last_above, last_below)):
         far.append((both, [((2 * n + h,), n, 2, g, h) for h, n in halves]))
     far = sum_along_z(ladder(1, live_amps, cycle, token, far)[:NZ])
 

time: 76.7 us -> 75.2 us (0.980)
  starting transfers between devices: 27.3 us -> 25.4 us
    ppermute x14, starting transfers between devices: 14.2 us -> 12.7 us  [move(): return lax.ppermute(value, 'blk', blk_moves(dy, dx, dc))]
    ppermute x14, waiting for transfers between devices: 23.5 us -> 24.3 us  [move(): return lax.ppermute(value, 'blk', blk_moves(dy, dx, dc))]
  transfers between devices with their start and end apart: 21 -> 21, of which waited for: 9 -> 10; matrix products, arithmetic and copies ran while one was open for 1% -> 1% of each run, Pallas kernels for 15% -> 15%
where the time goes in v5:
time: 75.2 us; the launch traced here: 75.1 us
  waiting for transfers between devices  33.6 us (45%)
  starting transfers between devices  25.4 us (34%)
  Pallas kernels  12.3 us (16%)
  local copies, waits for them, and re-layouts  2.36 us (3%)
  other arithmetic  1.11 us (1%)
    ppermute x14, waiting for transfers between devices, move(): return lax.ppermute(value, 'blk', blk_moves(dy, dx, dc))  24.3 us
    ppermute x7, starting transfers between devices, move_row(): return lax.ppermute(value, 'row', row_moves(dz, dx))  12.8 us
    ppermute x14, starting transfers between devices, move(): return lax.ppermute(value, 'blk', blk_moves(dy, dx, dc))  12.7 us
    ppermute x7, waiting for transfers between devices, move_row(): return lax.ppermute(value, 'row', row_moves(dz, dx))  9.22 us
    pallas_call x2, Pallas kernels, ladder(): pl.pallas_call(functools.partial(ladder_kernel, places, e, len(pieces)),...  5.24 us
    pallas_call x1, Pallas kernels, load_live(): pl.pallas_call(load_kernel, out_shape=(jax.ShapeDtypeStruct((2 * KT, rows...  4.05 us
    pallas_call x1, Pallas kernels, cycle_sums(): pl.pallas_call(functools.partial(cycle_kernel, places, width), out_shape=...  2.09 us
    unnamed x16, local copies, waits for them, and re-layouts  2.08 us
  transfers between devices with their start and end apart: 21, of which 10 were waited for; matrix products, arithmetic and copies ran while one was open for 1% of the time, Pallas kernels for 15%

profile of v5, /device:TPU:0, one launch (start us, length us, event | category | flops | bytes accessed | tf_op | source)
XLA Modules:
  0.0 75.1 jit_solution(12562749409683625465)
XLA Ops:
  0.0 0.0 copy-start.4
  0.0 0.0 copy-start
  0.0 1.2 %copy-done = bf16[16384,32]{0,1:T(8,128)(2,1)S(1)} copy-done((bf16[16384,32]{0,1:T(8,128)(2,1)S(1)}, bf16[16384,32]{0,1:T(8,128)(2,1)}, u32[]{:S(2)}) %copy-start) | copy-done | bytes 1048600
  1.2 0.0 copy-start.3
  1.2 0.7 copy-done.3
  1.9 0.9 %pick_live.1.after = bf16[4,16,4096]{2,1,0:T(8,128)(2,1)S(1)} custom-call(s32[4]{0:T(128)S(1)} %copy-done.3, bf16[32,16384]{1,0:T(8,128)(2,1)S(1)} %bitcast.3), custom_call_target="tpu_custom_call" | custom-call | tf_op jit(solution)/shard_map/pick_live/pallas_call | solution.py:66
  2.8 1.7 %collective-permute-start.2 = (bf16[4,16,4096]{2,1,0:T(8,128)(2,1)S(1)}, bf16[4,16,4096]{2,1,0:T(8,128)(2,1)S(1)}, u32[]{:S(2)}, u32[]{:S(2)}) collective-permute-start(bf16[4,16,4096]{2,1,0:T(8,128)(2,1)S(1)} %pick_live.1.after), channel_id=1, source_target_pairs={{0,4},{1,5},{2,6},{3,7},{4,0},{5,1},{6,2},{7,3},{8,12},{9,13},{10,... | collective-permute-start | bytes 1572872 | tf_op jit(solution)/shard_map/ppermute | solution.py:35
  4.6 2.2 %collective-permute-start.1 = (bf16[4,16,4096]{2,1,0:T(8,128)(2,1)S(1)}, bf16[4,16,4096]{2,1,0:T(8,128)(2,1)S(1)}, u32[]{:S(2)}, u32[]{:S(2)}) collective-permute-start(bf16[4,16,4096]{2,1,0:T(8,128)(2,1)S(1)} %pick_live.1.after), channel_id=1, source_target_pairs={{0,12},{1,13},{2,14},{3,15},{4,8},{5,9},{6,10},{7,11},{8,4},{9,5},... | collective-permute-start | bytes 1572872 | tf_op jit(solution)/shard_map/ppermute | solution.py:35
  6.8 1.5 %collective-permute-start = (bf16[4,16,4096]{2,1,0:T(8,128)(2,1)S(1)}, bf16[4,16,4096]{2,1,0:T(8,128)(2,1)S(1)}, u32[]{:S(2)}, u32[]{:S(2)}) collective-permute-start(bf16[4,16,4096]{2,1,0:T(8,128)(2,1)S(1)} %pick_live.1.after), channel_id=1, source_target_pairs={{0,2},{1,3},{2,0},{3,1},{4,6},{5,7},{6,4},{7,5},{8,10},{9,11},{10,... | collective-permute-start | bytes 1572872 | tf_op jit(solution)/shard_map/ppermute | solution.py:35
  8.2 0.7 collective-permute-start.3
  9.0 0.5 collective-permute-start.4
  9.5 0.0 copy-done.4
  9.6 0.0 copy-start.2
  9.6 4.1 %load_live.1 = (bf16[8,512,1024]{2,1,0:T(8,128)(2,1)S(1)}, f32[8,128]{1,0:T(8,128)S(1)}) custom-call(s32[4]{0:T(128)S(1)} %copy-done.4, bf16[512,16384]{1,0:T(8,128)(2,1)} %amps.1, bf16[4,16,4096]{2,1,0:T(8,128)(2,1)S(1)} %pick_live.1.after), custom_call_target="tpu_custom_call" | custom-call | tf_op jit(solution)/shard_map/load_live/pallas_call | solution.py:93
  13.6 7.6 %collective-permute-done.4.refs_1_ = bf16[256,128]{1,0:T(8,128)(2,1)S(1)} collective-permute-done((bf16[256,128]{1,0:T(8,128)(2,1)}, bf16[256,128]{1,0:T(8,128)(2,1)S(1)}, u32[]{:S(2)}, u32[]{:S(2)}) %collective-permute-start.4) | collective-permute-done | bytes 65568 | tf_op jit(solution)/shard_map/ppermute | solution.py:35
  21.3 0.0 copy-done.2
  21.3 0.0 collective-permute-done.3.refs_0_
  21.3 0.0 collective-permute-done.2
  21.3 0.0 collective-permute-done.1
  21.3 0.0 collective-permute-done
  21.6 0.2 pad_maximum_fusion.1
  21.8 0.8 %collective-permute-start.6 = (bf16[5,16,4096]{2,1,0:T(8,128)(2,1)S(1)}, bf16[5,16,4096]{2,1,0:T(8,128)(2,1)S(1)}, u32[]{:S(2)}, u32[]{:S(2)}) collective-permute-start(bf16[5,16,4096]{2,1,0:T(8,128)(2,1)S(1)} %get-tuple-element.75), channel_id=1, source_target_pairs={{0,4},{1,5},{2,6},{3,7},{4,0},{5,1},{6,2},{7,3},{8,12},{9,13},{10,... | collective-permute-start | bytes 1966088 | tf_op jit(solution)/shard_map/ppermute | solution.py:35
  22.6 0.9 %collective-permute-start.5 = (bf16[5,16,4096]{2,1,0:T(8,128)(2,1)S(1)}, bf16[5,16,4096]{2,1,0:T(8,128)(2,1)S(1)}, u32[]{:S(2)}, u32[]{:S(2)}) collective-permute-start(bf16[5,16,4096]{2,1,0:T(8,128)(2,1)S(1)} %get-tuple-element.76), channel_id=1, source_target_pairs={{0,12},{1,13},{2,14},{3,15},{4,8},{5,9},{6,10},{7,11},{8,4},{9,5},... | collective-permute-start | bytes 1966088 | tf_op jit(solution)/shard_map/ppermute | solution.py:35
  23.4 1.5 %collective-permute-start.7 = (bf16[5,16,4096]{2,1,0:T(8,128)(2,1)S(1)}, bf16[5,16,4096]{2,1,0:T(8,128)(2,1)S(1)}, u32[]{:S(2)}, u32[]{:S(2)}) collective-permute-start(bf16[5,16,4096]{2,1,0:T(8,128)(2,1)S(1)} %get-tuple-element.77), channel_id=1, source_target_pairs={{0,2},{1,3},{2,0},{3,1},{4,6},{5,7},{6,4},{7,5},{8,10},{9,11},{10,... | collective-permute-start | bytes 1966088 | tf_op jit(solution)/shard_map/ppermute | solution.py:35
  25.0 0.1 collective-permute-start.8
  25.1 11.8 %collective-permute-done.6 = bf16[5,16,4096]{2,1,0:T(8,128)(2,1)S(1)} collective-permute-done((bf16[5,16,4096]{2,1,0:T(8,128)(2,1)S(1)}, bf16[5,16,4096]{2,1,0:T(8,128)(2,1)S(1)}, u32[]{:S(2)}, u32[]{:S(2)}) %collective-permute-start.6) | collective-permute-done | bytes 655392 | tf_op jit(solution)/shard_map/ppermute | solution.py:35
  36.9 1.6 %collective-permute-done.5 = bf16[5,16,4096]{2,1,0:T(8,128)(2,1)S(1)} collective-permute-done((bf16[5,16,4096]{2,1,0:T(8,128)(2,1)S(1)}, bf16[5,16,4096]{2,1,0:T(8,128)(2,1)S(1)}, u32[]{:S(2)}, u32[]{:S(2)}) %collective-permute-start.5) | collective-permute-done | bytes 655392 | tf_op jit(solution)/shard_map/ppermute | solution.py:35
  38.5 0.0 collective-permute-done.7
  38.6 0.0 copy-start.1
  38.6 0.1 pad_maximum_fusion.refs_1_
  38.8 0.1 collective-permute-start.10
  38.9 0.6 collective-permute-start.9
  39.5 1.8 %collective-permute-start.14 = (bf16[2,16,4096]{2,1,0:T(8,128)(2,1)S(1)}, bf16[2,16,4096]{2,1,0:T(8,128)(2,1)S(1)}, u32[]{:S(2)}, u32[]{:S(2)}) collective-permute-start(bf16[2,16,4096]{2,1,0:T(8,128)(2,1)S(1)} %pad_maximum_fusion.6), channel_id=1, source_target_pairs={{0,12},{1,13},{2,14},{3,15},{4,8},{5,9},{6,10},{7,11},{8,4},{9,5},... | collective-permute-start | bytes 786440 | tf_op jit(solution)/shard_map/ppermute | solution.py:35
  41.4 0.2 collective-permute-start.15
  41.6 0.0 collective-permute-done.10.refs_3_
  41.6 1.2 %collective-permute-done.9.refs_3_ = bf16[7,16,4096]{2,1,0:T(8,128)(2,1)S(1)} collective-permute-done((bf16[7,16,4096]{2,1,0:T(8,128)(2,1)S(1)}, bf16[7,16,4096]{2,1,0:T(8,128)(2,1)S(1)}, u32[]{:S(2)}, u32[]{:S(2)}) %collective-permute-start.9) | collective-permute-done | bytes 917536 | tf_op jit(solution)/shard_map/ppermute | solution.py:35
  42.8 0.0 collective-permute-done.8.refs_2_
  42.8 0.0 copy-done.1
  42.8 2.1 %cycle.1 = f32[4,512,128]{2,1,0:T(8,128)S(1)} custom-call(bf16[8,8,512]{2,1,0:T(8,128)(2,1)S(1)} %copy-done.1, f32[8,128]{1,0:T(8,128)S(1)} %get-tuple-element.45.token.before, bf16[18,16,4096]{2,1,0:T(8,128)(2,1)S(1)} %constant_dynamic-update-slice_fusion.refs_0_, bf16[7,16,4096]{2,1,0:T(8,128)(2,1)S(1)} %get-tuple-element.66.refs_1_, ...), custom_call_target="tpu_custom_call" | custom-call | flops 134217728 | bytes 8388608 | tf_op jit(solution)/shard_map/cycle/pallas_call | solution.py:214
  44.9 2.4 %ladder.2 = (f32[64,512]{1,0:T(8,128)S(1)}, f32[64,512]{1,0:T(8,128)S(1)}, f32[64,512]{1,0:T(8,128)S(1)}, f32[64,512]{1,0:T(8,128)S(1)}, f32[8,128]{1,0:T(8,128)S(1)}) custom-call(bf16[8,512,1024]{2,1,0:T(8,128)(2,1)S(1)} %get-tuple-element.32.amps, f32[4,512,128]{2,1,0:T(8,128)S(1)} %cycle.1, f32[8,128]{1,0:T(8,128)S(1)} %get-tuple-element.45.token.before, ...), custom_call_target="tpu_custom_call" | custom-call | flops 2147483648 | bytes 4194304 | tf_op jit(solution)/shard_map/ladder/pallas_call | solution.py:146
  47.3 1.7 %collective-permute-done.14 = bf16[2,16,4096]{2,1,0:T(8,128)(2,1)S(1)} collective-permute-done((bf16[2,16,4096]{2,1,0:T(8,128)(2,1)S(1)}, bf16[2,16,4096]{2,1,0:T(8,128)(2,1)S(1)}, u32[]{:S(2)}, u32[]{:S(2)}) %collective-permute-start.14) | collective-permute-done | bytes 262176 | tf_op jit(solution)/shard_map/ppermute | solution.py:35
  49.0 0.4 collective-permute-done.15
  49.4 0.1 collective-permute-start.16
  49.5 2.0 %collective-permute-start.11 = (f32[64,512]{1,0:T(8,128)S(1)}, f32[64,512]{1,0:T(8,128)S(1)}, u32[]{:S(2)}, u32[]{:S(2)}) collective-permute-start(f32[64,512]{1,0:T(8,128)S(1)} %get-tuple-element.47), channel_id=1, source_target_pairs={{0,32},{16,48},{32,0},{48,16},{64,96},{80,112},{96,64},{112,80},{1... | collective-permute-start | bytes 393224 | tf_op jit(solution)/shard_map/ppermute | solution.py:39
  51.5 2.5 %collective-permute-start.12 = (f32[64,512]{1,0:T(8,128)S(1)}, f32[64,512]{1,0:T(8,128)S(1)}, u32[]{:S(2)}, u32[]{:S(2)}) collective-permute-start(f32[64,512]{1,0:T(8,128)S(1)} %get-tuple-element.48), channel_id=1, source_target_pairs={{0,96},{16,112},{32,64},{48,80},{64,32},{80,48},{96,0},{112,16},{1... | collective-permute-start | bytes 393224 | tf_op jit(solution)/shard_map/ppermute | solution.py:39
  54.1 1.1 %collective-permute-start.13 = (f32[64,512]{1,0:T(8,128)S(1)}, f32[64,512]{1,0:T(8,128)S(1)}, u32[]{:S(2)}, u32[]{:S(2)}) collective-permute-start(f32[64,512]{1,0:T(8,128)S(1)} %get-tuple-element.49), channel_id=1, source_target_pairs={{0,64},{16,80},{32,96},{48,112},{64,0},{80,16},{96,32},{112,48},{1... | collective-permute-start | bytes 393224 | tf_op jit(solution)/shard_map/ppermute | solution.py:39
  55.1 0.0 collective-permute-done.16.refs_5_
  55.1 2.8 %ladder.3 = (f32[64,512]{1,0:T(8,128)S(1)}, f32[64,512]{1,0:T(8,128)S(1)}, f32[64,512]{1,0:T(8,128)S(1)}, f32[64,512]{1,0:T(8,128)S(1)}, f32[8,128]{1,0:T(8,128)}) custom-call(bf16[8,512,1024]{2,1,0:T(8,128)(2,1)S(1)} %get-tuple-element.32.amps, f32[4,512,128]{2,1,0:T(8,128)S(1)} %cycle.1, f32[8,128]{1,0:T(8,128)S(1)} %get-tuple-element.51.before, ...), custom_call_target="tpu_custom_call" | custom-call | flops 2147483648 | bytes 4194304 | tf_op jit(solution)/shard_map/ladder/pallas_call | solution.py:146
  57.9 0.5 collective-permute-start.17
  58.5 2.5 %collective-permute-start.18 = (f32[64,512]{1,0:T(8,128)S(1)}, f32[64,512]{1,0:T(8,128)S(1)}, u32[]{:S(2)}, u32[]{:S(2)}) collective-permute-start(f32[64,512]{1,0:T(8,128)S(1)} %get-tuple-element.57), channel_id=1, source_target_pairs={{0,96},{16,112},{32,64},{48,80},{64,32},{80,48},{96,0},{112,16},{1... | collective-permute-start | bytes 393224 | tf_op jit(solution)/shard_map/ppermute | solution.py:39
  61.0 0.0 collective-permute-done.11
  61.0 1.1 %collective-permute-start.19 = (f32[64,512]{1,0:T(8,128)S(1)}, f32[64,512]{1,0:T(8,128)S(1)}, u32[]{:S(2)}, u32[]{:S(2)}) collective-permute-start(f32[64,512]{1,0:T(8,128)S(1)} %get-tuple-element.58), channel_id=1, source_target_pairs={{0,64},{16,80},{32,96},{48,112},{64,0},{80,16},{96,32},{112,48},{1... | collective-permute-start | bytes 393224 | tf_op jit(solution)/shard_map/ppermute | solution.py:39
  62.0 0.0 collective-permute-done.12
  62.0 0.0 collective-permute-done.13
  62.0 2.2 %collective-permute-done.17 = f32[64,512]{1,0:T(8,128)S(1)} collective-permute-done((f32[64,512]{1,0:T(8,128)S(1)}, f32[64,512]{1,0:T(8,128)S(1)}, u32[]{:S(2)}, u32[]{:S(2)}) %collective-permute-start.17) | collective-permute-done | bytes 131104 | tf_op jit(solution)/shard_map/ppermute | solution.py:39
  64.3 1.8 %collective-permute-done.18 = f32[64,512]{1,0:T(8,128)S(1)} collective-permute-done((f32[64,512]{1,0:T(8,128)S(1)}, f32[64,512]{1,0:T(8,128)S(1)}, u32[]{:S(2)}, u32[]{:S(2)}) %collective-permute-start.18) | collective-permute-done | bytes 131104 | tf_op jit(solution)/shard_map/ppermute | solution.py:39
  66.1 1.8 %collective-permute-done.19 = f32[64,512]{1,0:T(8,128)S(1)} collective-permute-done((f32[64,512]{1,0:T(8,128)S(1)}, f32[64,512]{1,0:T(8,128)S(1)}, u32[]{:S(2)}, u32[]{:S(2)}) %collective-permute-start.19) | collective-permute-done | bytes 131104 | tf_op jit(solution)/shard_map/ppermute | solution.py:39
  67.8 0.1 broadcast_select_fusion
  67.9 3.1 %collective-permute-start.20 = (f32[64,512]{1,0:T(8,128)S(1)}, f32[64,512]{1,0:T(8,128)S(1)}, u32[]{:S(2)}, u32[]{:S(2)}) collective-permute-start(f32[64,512]{1,0:T(8,128)S(1)} %get-tuple-element.59), channel_id=1, source_target_pairs={{0,16},{16,0},{32,48},{48,32},{64,80},{80,64},{96,112},{112,96},{1... | collective-permute-start | bytes 393224 | tf_op jit(solution)/shard_map/ppermute | solution.py:39
  71.0 3.4 %collective-permute-done.20 = f32[64,512]{1,0:T(8,128)S(1)} collective-permute-done((f32[64,512]{1,0:T(8,128)S(1)}, f32[64,512]{1,0:T(8,128)S(1)}, u32[]{:S(2)}, u32[]{:S(2)}) %collective-permute-start.20) | collective-permute-done | bytes 131104 | tf_op jit(solution)/shard_map/ppermute | solution.py:39
  74.5 0.7 fusion
  (21 shorter events, 0.5 us)
Async XLA Ops:
  0.0 9.5 %copy-start.4 = (s32[4]{0:T(128)S(1)}, s32[4]{0:T(128)}, u32[]{:S(2)}) copy-start(s32[4]{0:T(128)} %live.3) | copy-start | bytes 52
  0.0 1.2 %copy-start = (bf16[16384,32]{0,1:T(8,128)(2,1)S(1)}, bf16[16384,32]{0,1:T(8,128)(2,1)}, u32[]{:S(2)}) copy-start(bf16[16384,32]{0,1:T(8,128)(2,1)} %param.6) | copy-start | bytes 3145732
  1.2 0.7 copy-start.3
  2.8 18.5 %collective-permute-start.2 = (bf16[4,16,4096]{2,1,0:T(8,128)(2,1)S(1)}, bf16[4,16,4096]{2,1,0:T(8,128)(2,1)S(1)}, u32[]{:S(2)}, u32[]{:S(2)}) collective-permute-start(bf16[4,16,4096]{2,1,0:T(8,128)(2,1)S(1)} %pick_live.1.after), channel_id=1, source_target_pairs={{0,4},{1,5},{2,6},{3,7},{4,0},{5,1},{6,2},{7,3},{8,12},{9,13},{10,... | collective-permute-start | bytes 1572872 | tf_op jit(solution)/shard_map/ppermute | solution.py:35
  4.6 16.7 %collective-permute-start.1 = (bf16[4,16,4096]{2,1,0:T(8,128)(2,1)S(1)}, bf16[4,16,4096]{2,1,0:T(8,128)(2,1)S(1)}, u32[]{:S(2)}, u32[]{:S(2)}) collective-permute-start(bf16[4,16,4096]{2,1,0:T(8,128)(2,1)S(1)} %pick_live.1.after), channel_id=1, source_target_pairs={{0,12},{1,13},{2,14},{3,15},{4,8},{5,9},{6,10},{7,11},{8,4},{9,5},... | collective-permute-start | bytes 1572872 | tf_op jit(solution)/shard_map/ppermute | solution.py:35
  6.8 14.6 %collective-permute-start = (bf16[4,16,4096]{2,1,0:T(8,128)(2,1)S(1)}, bf16[4,16,4096]{2,1,0:T(8,128)(2,1)S(1)}, u32[]{:S(2)}, u32[]{:S(2)}) collective-permute-start(bf16[4,16,4096]{2,1,0:T(8,128)(2,1)S(1)} %pick_live.1.after), channel_id=1, source_target_pairs={{0,2},{1,3},{2,0},{3,1},{4,6},{5,7},{6,4},{7,5},{8,10},{9,11},{10,... | collective-permute-start | bytes 1572872 | tf_op jit(solution)/shard_map/ppermute | solution.py:35
  8.2 13.0 %collective-permute-start.3 = (bf16[256,128]{1,0:T(8,128)(2,1)}, bf16[256,128]{1,0:T(8,128)(2,1)S(1)}, u32[]{:S(2)}, u32[]{:S(2)}) collective-permute-start(bf16[256,128]{1,0:T(8,128)(2,1)} %refs_0_.1), channel_id=1, source_target_pairs={{0,8},{1,9},{2,10},{3,11},{4,12},{5,13},{6,14},{7,15},{8,0},{9,1},... | collective-permute-start | bytes 196616 | tf_op jit(solution)/shard_map/ppermute | solution.py:35
  9.0 12.3 %collective-permute-start.4 = (bf16[256,128]{1,0:T(8,128)(2,1)}, bf16[256,128]{1,0:T(8,128)(2,1)S(1)}, u32[]{:S(2)}, u32[]{:S(2)}) collective-permute-start(bf16[256,128]{1,0:T(8,128)(2,1)} %refs_0_.1), channel_id=1, source_target_pairs={{0,2},{1,3},{2,0},{3,1},{4,6},{5,7},{6,4},{7,5},{8,10},{9,11},{10,... | collective-permute-start | bytes 196616 | tf_op jit(solution)/shard_map/ppermute | solution.py:35
  9.6 11.7 %copy-start.2 = (bf16[256,128]{1,0:T(8,128)(2,1)S(1)}, bf16[256,128]{1,0:T(8,128)(2,1)}, u32[]{:S(2)}) copy-start(bf16[256,128]{1,0:T(8,128)(2,1)} %refs_0_.1) | copy-start | bytes 196612
  21.8 15.1 %collective-permute-start.6 = (bf16[5,16,4096]{2,1,0:T(8,128)(2,1)S(1)}, bf16[5,16,4096]{2,1,0:T(8,128)(2,1)S(1)}, u32[]{:S(2)}, u32[]{:S(2)}) collective-permute-start(bf16[5,16,4096]{2,1,0:T(8,128)(2,1)S(1)} %get-tuple-element.75), channel_id=1, source_target_pairs={{0,4},{1,5},{2,6},{3,7},{4,0},{5,1},{6,2},{7,3},{8,12},{9,13},{10,... | collective-permute-start | bytes 1966088 | tf_op jit(solution)/shard_map/ppermute | solution.py:35
  22.6 15.9 %collective-permute-start.5 = (bf16[5,16,4096]{2,1,0:T(8,128)(2,1)S(1)}, bf16[5,16,4096]{2,1,0:T(8,128)(2,1)S(1)}, u32[]{:S(2)}, u32[]{:S(2)}) collective-permute-start(bf16[5,16,4096]{2,1,0:T(8,128)(2,1)S(1)} %get-tuple-element.76), channel_id=1, source_target_pairs={{0,12},{1,13},{2,14},{3,15},{4,8},{5,9},{6,10},{7,11},{8,4},{9,5},... | collective-permute-start | bytes 1966088 | tf_op jit(solution)/shard_map/ppermute | solution.py:35
  23.4 15.0 %collective-permute-start.7 = (bf16[5,16,4096]{2,1,0:T(8,128)(2,1)S(1)}, bf16[5,16,4096]{2,1,0:T(8,128)(2,1)S(1)}, u32[]{:S(2)}, u32[]{:S(2)}) collective-permute-start(bf16[5,16,4096]{2,1,0:T(8,128)(2,1)S(1)} %get-tuple-element.77), channel_id=1, source_target_pairs={{0,2},{1,3},{2,0},{3,1},{4,6},{5,7},{6,4},{7,5},{8,10},{9,11},{10,... | collective-permute-start | bytes 1966088 | tf_op jit(solution)/shard_map/ppermute | solution.py:35
  25.0 17.8 %collective-permute-start.8 = (bf16[18,16,4096]{2,1,0:T(8,128)(2,1)S(1)}, bf16[18,16,4096]{2,1,0:T(8,128)(2,1)S(1)}, u32[]{:S(2)}, u32[]{:S(2)}) collective-permute-start(bf16[18,16,4096]{2,1,0:T(8,128)(2,1)S(1)} %constant_dynamic-update-slice_fusion.refs_0_), channel_id=1, source_target_pairs={{0,1},{1,0},{2,3},{3,2},{4,5},{5,4},{6,7},{7,6},{8,9},{9,8},{10,11... | collective-permute-start | bytes 7077896 | tf_op jit(solution)/shard_map/ppermute | solution.py:35
  38.6 4.2 %copy-start.1 = (bf16[8,8,512]{2,1,0:T(8,128)(2,1)S(1)}, bf16[8,8,512]{2,1,0:T(8,128)(2,1)}, u32[]{:S(2)}) copy-start(bf16[8,8,512]{2,1,0:T(8,128)(2,1)} %slab_amps.1) | copy-start | bytes 196612
  38.8 2.8 %collective-permute-start.10 = (bf16[8,16,4096]{2,1,0:T(8,128)(2,1)S(1)}, bf16[8,16,4096]{2,1,0:T(8,128)(2,1)S(1)}, u32[]{:S(2)}, u32[]{:S(2)}) collective-permute-start(bf16[8,16,4096]{2,1,0:T(8,128)(2,1)S(1)} %pad_maximum_fusion.refs_1_), channel_id=1, source_target_pairs={{0,1},{1,0},{2,3},{3,2},{4,5},{5,4},{6,7},{7,6},{8,9},{9,8},{10,11... | collective-permute-start | bytes 3145736 | tf_op jit(solution)/shard_map/ppermute | solution.py:35
  38.9 3.9 %collective-permute-start.9 = (bf16[7,16,4096]{2,1,0:T(8,128)(2,1)S(1)}, bf16[7,16,4096]{2,1,0:T(8,128)(2,1)S(1)}, u32[]{:S(2)}, u32[]{:S(2)}) collective-permute-start(bf16[7,16,4096]{2,1,0:T(8,128)(2,1)S(1)} %get-tuple-element.66.refs_1_), channel_id=1, source_target_pairs={{0,1},{1,0},{2,3},{3,2},{4,5},{5,4},{6,7},{7,6},{8,9},{9,8},{10,11... | collective-permute-start | bytes 2752520 | tf_op jit(solution)/shard_map/ppermute | solution.py:35
  39.5 9.5 %collective-permute-start.14 = (bf16[2,16,4096]{2,1,0:T(8,128)(2,1)S(1)}, bf16[2,16,4096]{2,1,0:T(8,128)(2,1)S(1)}, u32[]{:S(2)}, u32[]{:S(2)}) collective-permute-start(bf16[2,16,4096]{2,1,0:T(8,128)(2,1)S(1)} %pad_maximum_fusion.6), channel_id=1, source_target_pairs={{0,12},{1,13},{2,14},{3,15},{4,8},{5,9},{6,10},{7,11},{8,4},{9,5},... | collective-permute-start | bytes 786440 | tf_op jit(solution)/shard_map/ppermute | solution.py:35
  41.4 8.0 %collective-permute-start.15 = (bf16[2,16,4096]{2,1,0:T(8,128)(2,1)S(1)}, bf16[2,16,4096]{2,1,0:T(8,128)(2,1)S(1)}, u32[]{:S(2)}, u32[]{:S(2)}) collective-permute-start(bf16[2,16,4096]{2,1,0:T(8,128)(2,1)S(1)} %pad_maximum_fusion.7), channel_id=1, source_target_pairs={{0,4},{1,5},{2,6},{3,7},{4,0},{5,1},{6,2},{7,3},{8,12},{9,13},{10,... | collective-permute-start | bytes 786440 | tf_op jit(solution)/shard_map/ppermute | solution.py:35
  49.4 5.7 %collective-permute-start.16 = (bf16[4,16,4096]{2,1,0:T(8,128)(2,1)S(1)}, bf16[4,16,4096]{2,1,0:T(8,128)(2,1)S(1)}, u32[]{:S(2)}, u32[]{:S(2)}) collective-permute-start(bf16[4,16,4096]{2,1,0:T(8,128)(2,1)S(1)} %constant_dynamic-update-slice_fusion.6.refs_4_), channel_id=1, source_target_pairs={{0,1},{1,0},{2,3},{3,2},{4,5},{5,4},{6,7},{7,6},{8,9},{9,8},{10,11... | collective-permute-start | bytes 1572872 | tf_op jit(solution)/shard_map/ppermute | solution.py:35
  49.5 11.4 %collective-permute-start.11 = (f32[64,512]{1,0:T(8,128)S(1)}, f32[64,512]{1,0:T(8,128)S(1)}, u32[]{:S(2)}, u32[]{:S(2)}) collective-permute-start(f32[64,512]{1,0:T(8,128)S(1)} %get-tuple-element.47), channel_id=1, source_target_pairs={{0,32},{16,48},{32,0},{48,16},{64,96},{80,112},{96,64},{112,80},{1... | collective-permute-start | bytes 393224 | tf_op jit(solution)/shard_map/ppermute | solution.py:39
  51.5 10.5 %collective-permute-start.12 = (f32[64,512]{1,0:T(8,128)S(1)}, f32[64,512]{1,0:T(8,128)S(1)}, u32[]{:S(2)}, u32[]{:S(2)}) collective-permute-start(f32[64,512]{1,0:T(8,128)S(1)} %get-tuple-element.48), channel_id=1, source_target_pairs={{0,96},{16,112},{32,64},{48,80},{64,32},{80,48},{96,0},{112,16},{1... | collective-permute-start | bytes 393224 | tf_op jit(solution)/shard_map/ppermute | solution.py:39
  54.1 8.0 %collective-permute-start.13 = (f32[64,512]{1,0:T(8,128)S(1)}, f32[64,512]{1,0:T(8,128)S(1)}, u32[]{:S(2)}, u32[]{:S(2)}) collective-permute-start(f32[64,512]{1,0:T(8,128)S(1)} %get-tuple-element.49), channel_id=1, source_target_pairs={{0,64},{16,80},{32,96},{48,112},{64,0},{80,16},{96,32},{112,48},{1... | collective-permute-start | bytes 393224 | tf_op jit(solution)/shard_map/ppermute | solution.py:39
  57.9 6.3 %collective-permute-start.17 = (f32[64,512]{1,0:T(8,128)S(1)}, f32[64,512]{1,0:T(8,128)S(1)}, u32[]{:S(2)}, u32[]{:S(2)}) collective-permute-start(f32[64,512]{1,0:T(8,128)S(1)} %get-tuple-element.56), channel_id=1, source_target_pairs={{0,32},{16,48},{32,0},{48,16},{64,96},{80,112},{96,64},{112,80},{1... | collective-permute-start | bytes 393224 | tf_op jit(solution)/shard_map/ppermute | solution.py:39
  58.5 7.6 %collective-permute-start.18 = (f32[64,512]{1,0:T(8,128)S(1)}, f32[64,512]{1,0:T(8,128)S(1)}, u32[]{:S(2)}, u32[]{:S(2)}) collective-permute-start(f32[64,512]{1,0:T(8,128)S(1)} %get-tuple-element.57), channel_id=1, source_target_pairs={{0,96},{16,112},{32,64},{48,80},{64,32},{80,48},{96,0},{112,16},{1... | collective-permute-start | bytes 393224 | tf_op jit(solution)/shard_map/ppermute | solution.py:39
  61.0 6.8 %collective-permute-start.19 = (f32[64,512]{1,0:T(8,128)S(1)}, f32[64,512]{1,0:T(8,128)S(1)}, u32[]{:S(2)}, u32[]{:S(2)}) collective-permute-start(f32[64,512]{1,0:T(8,128)S(1)} %get-tuple-element.58), channel_id=1, source_target_pairs={{0,64},{16,80},{32,96},{48,112},{64,0},{80,16},{96,32},{112,48},{1... | collective-permute-start | bytes 393224 | tf_op jit(solution)/shard_map/ppermute | solution.py:39
  67.9 6.6 %collective-permute-start.20 = (f32[64,512]{1,0:T(8,128)S(1)}, f32[64,512]{1,0:T(8,128)S(1)}, u32[]{:S(2)}, u32[]{:S(2)}) collective-permute-start(f32[64,512]{1,0:T(8,128)S(1)} %get-tuple-element.59), channel_id=1, source_target_pairs={{0,16},{16,0},{32,48},{48,32},{64,80},{80,64},{96,112},{112,96},{1... | collective-permute-start | bytes 393224 | tf_op jit(solution)/shard_map/ppermute | solution.py:39

commit v6 on v5

--- a/solution.py
+++ b/solution.py
@@ -105,7 +105,7 @@
 
 
 def ladder_kernel(places, e, count, amps, cycle, before, *refs):
-    pieces, outs, (token, total) = refs[:count], refs[count : count + NZ], refs[count + NZ :]
+    pieces, outs, (token, total) = refs[:count], refs[count:-2], refs[-2:]
     token[...] = jnp.zeros_like(token)
     for n in range(2):
         held = {}
@@ -134,20 +134,27 @@
             here = (dy * NC + (c ^ core)) * SB
             there = (((z ^ dz) * NX + (x ^ e)) * NC + core) * SB
             there = pl.ds(pl.multiple_of(there, SB), SB)
-            outs[dz][core * SB : (core + 1) * SB, :] = total[
-                pl.ds(pl.multiple_of(here, SB), SB), :
-            ] + jnp.concatenate([cycle[n, there, :] for n in range(cycle.shape[0])], axis=1)
-
-
-def ladder(e, amplitudes, cycle, before, pieces):
+            rows = slice(core * SB, (core + 1) * SB)
+            value = total[pl.ds(pl.multiple_of(here, SB), SB), :] + jnp.concatenate(
+                [cycle[n, there, :] for n in range(cycle.shape[0])], axis=1
+            )
+            if dz == 2 and len(outs) > NZ:
+                mine = x == lax.axis_index("row") % NH
+                outs[2][rows, :] = jnp.where(mine, before[rows, :], value)
+                outs[NZ][rows, :] = jnp.where(mine, value, before[rows, :])
+            else:
+                outs[dz][rows, :] = value
+
+
+def ladder(e, amplitudes, cycle, before, pieces, exchange=False):
     places = [(n, *place) for n, (_, held) in enumerate(pieces) for place in held]
     rows, q = amplitudes.shape[1], NY * NC * SB
     out = jax.ShapeDtypeStruct((q // NZ, rows), jnp.float32)
     return pl.pallas_call(
         functools.partial(ladder_kernel, places, e, len(pieces)),
-        out_shape=(out,) * NZ + (jax.ShapeDtypeStruct((8, 128), jnp.float32),),
+        out_shape=(out,) * (NZ + exchange) + (jax.ShapeDtypeStruct((8, 128), jnp.float32),),
         in_specs=[pl.BlockSpec(memory_space=pltpu.VMEM)] * (3 + len(pieces)),
-        out_specs=[pl.BlockSpec(memory_space=pltpu.VMEM)] * (NZ + 1),
+        out_specs=[pl.BlockSpec(memory_space=pltpu.VMEM)] * (NZ + exchange + 1),
         scratch_shapes=[pltpu.VMEM((q, rows), jnp.float32)],
         compiler_params=pltpu.CompilerParams(vmem_limit_bytes=24 * MIB),
         cost_estimate=pl.CostEstimate(
@@ -228,11 +235,8 @@
     )(slab_amplitudes, token, *arrays)
 
 
-def sum_along_z(parts):
-    total = parts[0]
-    for dz in (1, 3, 2):
-        total = total + move_row(parts[dz], dz=dz)
-    return total
+def sum_beside(parts):
+    return parts[0] + move_row(parts[1], dz=1) + move_row(parts[3], dz=3)
 
 
 def per_device(amplitudes, integrals, live_pairs, slab_amplitudes, cycle_integrals):
@@ -274,9 +278,9 @@
         places = [((4 * at + 2 * h + n,), n, dy, g, h) for at, dy in enumerate((0, 1, 3)) for h, n in halves]
         near += [(hop[g], places), (hop_near[g], [((2 * h + n,), n, 2, g, h) for h, n in halves])]
     *near, token = ladder(0, live_amps, cycle, token, near)
-    near = sum_along_z(near)
-
-    last_above, last_below, token = together(last_above, last_below, token)
+    near_sum = sum_beside(near)
+
+    last_above, last_below, before = together(last_above, last_below, near[2])
     far = []
     for g in range(NC):
         places = [((2 * at + n,), n, dy, g, 0) for at, dy in enumerate((3, 1)) for n in range(2)]
@@ -284,10 +288,12 @@
         far += [(hop[g], [((12 + 2 * h + n,), n, 0, g, h) for h, n in halves]), (hop_far[g], places)]
     for g, both in enumerate(swap(last_above, last_below)):
         far.append((both, [((2 * n + h,), n, 2, g, h) for h, n in halves]))
-    far = sum_along_z(ladder(1, live_amps, cycle, token, far)[:NZ])
+    *far, other, _ = ladder(1, live_amps, cycle, before, far, exchange=True)
+    far_sum = sum_beside(far)
 
     mine = lax.axis_index("row") % NH == (lax.axis_index("blk") // NC) % NX
-    total = jnp.where(mine, near, far) + move_row(jnp.where(mine, far, near), dx=1)
+    total = jnp.where(mine, near_sum, far_sum) + move_row(jnp.where(mine, far_sum, near_sum), dx=1)
+    total = total + move_row(other, dz=2, dx=1) + move_row(far[2], dz=2)
     return total.astype(jnp.bfloat16).T
 
 

time: 75.2 us -> 73.1 us (0.972)
  waiting for transfers between devices: 33.6 us -> 28.7 us
  starting transfers between devices: 25.4 us -> 27.8 us
    ppermute x7, waiting for transfers between devices: 9.22 us -> 4.22 us  [move_row(): return lax.ppermute(value, 'row', row_moves(dz, dx))]
    ppermute x7, starting transfers between devices: 12.8 us -> 14.6 us  [move_row(): return lax.ppermute(value, 'row', row_moves(dz, dx))]
  transfers between devices with their start and end apart: 21 -> 21, of which waited for: 10 -> 11; matrix products, arithmetic and copies ran while one was open for 1% -> 1% of each run, Pallas kernels for 15% -> 16%
where the time goes in v6:
time: 73.1 us; the launch traced here: 73 us
  waiting for transfers between devices  28.7 us (39%)
  starting transfers between devices  27.8 us (38%)
  Pallas kernels  12.8 us (18%)
  local copies, waits for them, and re-layouts  2.36 us (3%)
  other arithmetic  1.14 us (2%)
    ppermute x14, waiting for transfers between devices, move(): return lax.ppermute(value, 'blk', blk_moves(dy, dx, dc))  24.5 us
    ppermute x7, starting transfers between devices, move_row(): return lax.ppermute(value, 'row', row_moves(dz, dx))  14.6 us
    ppermute x14, starting transfers between devices, move(): return lax.ppermute(value, 'blk', blk_moves(dy, dx, dc))  13.1 us
    pallas_call x2, Pallas kernels, ladder(): pl.pallas_call(functools.partial(ladder_kernel, places, e, len(pieces)),...  5.7 us
    ppermute x7, waiting for transfers between devices, move_row(): return lax.ppermute(value, 'row', row_moves(dz, dx))  4.22 us
    pallas_call x1, Pallas kernels, load_live(): pl.pallas_call(load_kernel, out_shape=(jax.ShapeDtypeStruct((2 * KT, rows...  4.05 us
    pallas_call x1, Pallas kernels, cycle_sums(): pl.pallas_call(functools.partial(cycle_kernel, places, width), out_shape=...  2.09 us
    unnamed x16, local copies, waits for them, and re-layouts  2.08 us
  transfers between devices with their start and end apart: 21, of which 11 were waited for; matrix products, arithmetic and copies ran while one was open for 1% of the time, Pallas kernels for 16%

profile of v6, /device:TPU:0, one launch (start us, length us, event | category | flops | bytes accessed | tf_op | source)
XLA Modules:
  0.0 73.0 jit_solution(1707636161387080881)
XLA Ops:
  0.0 0.0 copy-start.4
  0.0 0.0 copy-start
  0.0 1.2 %copy-done = bf16[16384,32]{0,1:T(8,128)(2,1)S(1)} copy-done((bf16[16384,32]{0,1:T(8,128)(2,1)S(1)}, bf16[16384,32]{0,1:T(8,128)(2,1)}, u32[]{:S(2)}) %copy-start) | copy-done | bytes 1048600
  1.2 0.0 copy-start.3
  1.2 0.7 copy-done.3
  1.9 0.9 %pick_live.1.after = bf16[4,16,4096]{2,1,0:T(8,128)(2,1)S(1)} custom-call(s32[4]{0:T(128)S(1)} %copy-done.3, bf16[32,16384]{1,0:T(8,128)(2,1)S(1)} %bitcast.3), custom_call_target="tpu_custom_call" | custom-call | tf_op jit(solution)/shard_map/pick_live/pallas_call | solution.py:66
  2.8 1.7 %collective-permute-start = (bf16[4,16,4096]{2,1,0:T(8,128)(2,1)S(1)}, bf16[4,16,4096]{2,1,0:T(8,128)(2,1)S(1)}, u32[]{:S(2)}, u32[]{:S(2)}) collective-permute-start(bf16[4,16,4096]{2,1,0:T(8,128)(2,1)S(1)} %pick_live.1.after), channel_id=1, source_target_pairs={{0,2},{1,3},{2,0},{3,1},{4,6},{5,7},{6,4},{7,5},{8,10},{9,11},{10,... | collective-permute-start | bytes 1572872 | tf_op jit(solution)/shard_map/ppermute | solution.py:35
  4.5 3.0 %collective-permute-start.1 = (bf16[4,16,4096]{2,1,0:T(8,128)(2,1)S(1)}, bf16[4,16,4096]{2,1,0:T(8,128)(2,1)S(1)}, u32[]{:S(2)}, u32[]{:S(2)}) collective-permute-start(bf16[4,16,4096]{2,1,0:T(8,128)(2,1)S(1)} %pick_live.1.after), channel_id=1, source_target_pairs={{0,12},{1,13},{2,14},{3,15},{4,8},{5,9},{6,10},{7,11},{8,4},{9,5},... | collective-permute-start | bytes 1572872 | tf_op jit(solution)/shard_map/ppermute | solution.py:35
  7.5 0.1 collective-permute-start.2
  7.6 1.5 %collective-permute-start.3 = (bf16[256,128]{1,0:T(8,128)(2,1)}, bf16[256,128]{1,0:T(8,128)(2,1)S(1)}, u32[]{:S(2)}, u32[]{:S(2)}) collective-permute-start(bf16[256,128]{1,0:T(8,128)(2,1)} %refs_0_.1), channel_id=1, source_target_pairs={{0,8},{1,9},{2,10},{3,11},{4,12},{5,13},{6,14},{7,15},{8,0},{9,1},... | collective-permute-start | bytes 196616 | tf_op jit(solution)/shard_map/ppermute | solution.py:35
  9.2 0.5 collective-permute-start.4
  9.7 0.0 copy-done.4
  9.7 0.0 copy-start.2
  9.7 4.1 %load_live.1 = (bf16[8,512,1024]{2,1,0:T(8,128)(2,1)S(1)}, f32[8,128]{1,0:T(8,128)S(1)}) custom-call(s32[4]{0:T(128)S(1)} %copy-done.4, bf16[512,16384]{1,0:T(8,128)(2,1)} %amps.1, bf16[4,16,4096]{2,1,0:T(8,128)(2,1)S(1)} %pick_live.1.after), custom_call_target="tpu_custom_call" | custom-call | tf_op jit(solution)/shard_map/load_live/pallas_call | solution.py:93
  13.8 4.1 %collective-permute-done.4.refs_1_ = bf16[256,128]{1,0:T(8,128)(2,1)S(1)} collective-permute-done((bf16[256,128]{1,0:T(8,128)(2,1)}, bf16[256,128]{1,0:T(8,128)(2,1)S(1)}, u32[]{:S(2)}, u32[]{:S(2)}) %collective-permute-start.4) | collective-permute-done | bytes 65568 | tf_op jit(solution)/shard_map/ppermute | solution.py:35
  17.8 0.0 copy-done.2
  17.8 3.9 %collective-permute-done.3.refs_0_ = bf16[256,128]{1,0:T(8,128)(2,1)S(1)} collective-permute-done((bf16[256,128]{1,0:T(8,128)(2,1)}, bf16[256,128]{1,0:T(8,128)(2,1)S(1)}, u32[]{:S(2)}, u32[]{:S(2)}) %collective-permute-start.3) | collective-permute-done | bytes 65568 | tf_op jit(solution)/shard_map/ppermute | solution.py:35
  21.7 0.0 collective-permute-done
  21.7 0.0 collective-permute-done.1
  21.7 0.0 collective-permute-done.2
  22.0 0.2 pad_maximum_fusion.1
  22.2 3.0 %collective-permute-start.5 = (bf16[5,16,4096]{2,1,0:T(8,128)(2,1)S(1)}, bf16[5,16,4096]{2,1,0:T(8,128)(2,1)S(1)}, u32[]{:S(2)}, u32[]{:S(2)}) collective-permute-start(bf16[5,16,4096]{2,1,0:T(8,128)(2,1)S(1)} %get-tuple-element.73), channel_id=1, source_target_pairs={{0,12},{1,13},{2,14},{3,15},{4,8},{5,9},{6,10},{7,11},{8,4},{9,5},... | collective-permute-start | bytes 1966088 | tf_op jit(solution)/shard_map/ppermute | solution.py:35
  25.2 0.0 collective-permute-start.6
  25.2 0.5 collective-permute-start.7
  25.8 0.1 collective-permute-start.8
  25.9 12.4 %collective-permute-done.5 = bf16[5,16,4096]{2,1,0:T(8,128)(2,1)S(1)} collective-permute-done((bf16[5,16,4096]{2,1,0:T(8,128)(2,1)S(1)}, bf16[5,16,4096]{2,1,0:T(8,128)(2,1)S(1)}, u32[]{:S(2)}, u32[]{:S(2)}) %collective-permute-start.5) | collective-permute-done | bytes 655392 | tf_op jit(solution)/shard_map/ppermute | solution.py:35
  38.3 1.4 %collective-permute-done.6 = bf16[5,16,4096]{2,1,0:T(8,128)(2,1)S(1)} collective-permute-done((bf16[5,16,4096]{2,1,0:T(8,128)(2,1)S(1)}, bf16[5,16,4096]{2,1,0:T(8,128)(2,1)S(1)}, u32[]{:S(2)}, u32[]{:S(2)}) %collective-permute-start.6) | collective-permute-done | bytes 655392 | tf_op jit(solution)/shard_map/ppermute | solution.py:35
  39.7 0.0 collective-permute-done.7
  39.8 0.0 copy-start.1
  39.8 0.1 pad_maximum_fusion.refs_1_
  39.9 0.1 collective-permute-start.10
  40.1 0.6 collective-permute-start.9
  40.7 1.6 %collective-permute-start.13 = (bf16[2,16,4096]{2,1,0:T(8,128)(2,1)S(1)}, bf16[2,16,4096]{2,1,0:T(8,128)(2,1)S(1)}, u32[]{:S(2)}, u32[]{:S(2)}) collective-permute-start(bf16[2,16,4096]{2,1,0:T(8,128)(2,1)S(1)} %pad_maximum_fusion.6), channel_id=1, source_target_pairs={{0,12},{1,13},{2,14},{3,15},{4,8},{5,9},{6,10},{7,11},{8,4},{9,5},... | collective-permute-start | bytes 786440 | tf_op jit(solution)/shard_map/ppermute | solution.py:35
  42.3 0.3 collective-permute-start.14
  42.6 0.0 collective-permute-done.10.refs_3_
  42.7 1.3 %collective-permute-done.9.refs_3_ = bf16[7,16,4096]{2,1,0:T(8,128)(2,1)S(1)} collective-permute-done((bf16[7,16,4096]{2,1,0:T(8,128)(2,1)S(1)}, bf16[7,16,4096]{2,1,0:T(8,128)(2,1)S(1)}, u32[]{:S(2)}, u32[]{:S(2)}) %collective-permute-start.9) | collective-permute-done | bytes 917536 | tf_op jit(solution)/shard_map/ppermute | solution.py:35
  44.0 0.0 collective-permute-done.8.refs_2_
  44.0 0.0 copy-done.1
  44.0 2.1 %cycle.1 = f32[4,512,128]{2,1,0:T(8,128)S(1)} custom-call(bf16[8,8,512]{2,1,0:T(8,128)(2,1)S(1)} %copy-done.1, f32[8,128]{1,0:T(8,128)S(1)} %get-tuple-element.45.token.before, bf16[18,16,4096]{2,1,0:T(8,128)(2,1)S(1)} %constant_dynamic-update-slice_fusion.refs_0_, bf16[7,16,4096]{2,1,0:T(8,128)(2,1)S(1)} %get-tuple-element.67.refs_1_, ...), custom_call_target="tpu_custom_call" | custom-call | flops 134217728 | bytes 8388608 | tf_op jit(solution)/shard_map/cycle/pallas_call | solution.py:221
  46.1 2.8 %ladder.2 = (f32[64,512]{1,0:T(8,128)S(1)}, f32[64,512]{1,0:T(8,128)S(1)}, f32[64,512]{1,0:T(8,128)S(1)}, f32[64,512]{1,0:T(8,128)S(1)}, f32[8,128]{1,0:T(8,128)}) custom-call(bf16[8,512,1024]{2,1,0:T(8,128)(2,1)S(1)} %get-tuple-element.32.amps, f32[4,512,128]{2,1,0:T(8,128)S(1)} %cycle.1, f32[8,128]{1,0:T(8,128)S(1)} %get-tuple-element.45.token.before, ...), custom_call_target="tpu_custom_call" | custom-call | flops 2147483648 | bytes 4194304 | tf_op jit(solution)/shard_map/ladder/pallas_call | solution.py:153
  48.9 1.3 %collective-permute-done.13 = bf16[2,16,4096]{2,1,0:T(8,128)(2,1)S(1)} collective-permute-done((bf16[2,16,4096]{2,1,0:T(8,128)(2,1)S(1)}, bf16[2,16,4096]{2,1,0:T(8,128)(2,1)S(1)}, u32[]{:S(2)}, u32[]{:S(2)}) %collective-permute-start.13) | collective-permute-done | bytes 262176 | tf_op jit(solution)/shard_map/ppermute | solution.py:35
  50.2 0.1 collective-permute-done.14
  50.4 0.1 collective-permute-start.15
  50.5 4.1 %collective-permute-start.12 = (f32[64,512]{1,0:T(8,128)S(1)}, f32[64,512]{1,0:T(8,128)S(1)}, u32[]{:S(2)}, u32[]{:S(2)}) collective-permute-start(f32[64,512]{1,0:T(8,128)S(1)} %get-tuple-element.48), channel_id=1, source_target_pairs={{0,96},{16,112},{32,64},{48,80},{64,32},{80,48},{96,0},{112,16},{1... | collective-permute-start | bytes 393224 | tf_op jit(solution)/shard_map/ppermute | solution.py:39
  54.6 0.0 collective-permute-start.11
  54.6 0.0 collective-permute-done.15.refs_5_
  54.6 2.9 %ladder.3 = (f32[64,512]{1,0:T(8,128)S(1)}, f32[64,512]{1,0:T(8,128)S(1)}, f32[64,512]{1,0:T(8,128)S(1)}, f32[64,512]{1,0:T(8,128)S(1)}, f32[64,512]{1,0:T(8,128)S(1)}, /*index=5*/f32[8,128]{1,0:T(8,128)}) custom-call(bf16[8,512,1024]{2,1,0:T(8,128)(2,1)S(1)} %get-tuple-element.32.amps, f32[4,512,128]{2,1,0:T(8,128)S(1)} %cycle.1, ...), custom_call_target="tpu_custom_call" | custom-call | flops 2147483648 | bytes 4194304 | tf_op jit(solution)/shard_map/ladder/pallas_call | solution.py:153
  57.5 1.8 %collective-permute-start.17 = (f32[64,512]{1,0:T(8,128)S(1)}, f32[64,512]{1,0:T(8,128)S(1)}, u32[]{:S(2)}, u32[]{:S(2)}) collective-permute-start(f32[64,512]{1,0:T(8,128)S(1)} %get-tuple-element.56), channel_id=1, source_target_pairs={{0,96},{16,112},{32,64},{48,80},{64,32},{80,48},{96,0},{112,16},{1... | collective-permute-start | bytes 393224 | tf_op jit(solution)/shard_map/ppermute | solution.py:39
  59.3 0.2 collective-permute-start.16
  59.5 2.7 %collective-permute-start.20 = (f32[64,512]{1,0:T(8,128)S(1)}, f32[64,512]{1,0:T(8,128)S(1)}, u32[]{:S(2)}, u32[]{:S(2)}) collective-permute-start(f32[64,512]{1,0:T(8,128)S(1)} %get-tuple-element.58), channel_id=1, source_target_pairs={{0,64},{16,80},{32,96},{48,112},{64,0},{80,16},{96,32},{112,48},{1... | collective-permute-start | bytes 393224 | tf_op jit(solution)/shard_map/ppermute | solution.py:39
  62.2 0.0 collective-permute-done.12
  62.2 3.0 %collective-permute-start.19 = (f32[64,512]{1,0:T(8,128)S(1)}, f32[64,512]{1,0:T(8,128)S(1)}, u32[]{:S(2)}, u32[]{:S(2)}) collective-permute-start(f32[64,512]{1,0:T(8,128)S(1)} %get-tuple-element.57), channel_id=1, source_target_pairs={{0,80},{16,64},{32,112},{48,96},{64,16},{80,0},{96,48},{112,32},{1... | collective-permute-start | bytes 393224 | tf_op jit(solution)/shard_map/ppermute | solution.py:39
  65.2 0.0 collective-permute-done.11
  65.2 0.0 collective-permute-done.17
  65.2 0.5 collective-permute-done.16
  65.7 0.1 broadcast_select_fusion
  65.7 2.8 %collective-permute-start.18 = (f32[64,512]{1,0:T(8,128)S(1)}, f32[64,512]{1,0:T(8,128)S(1)}, u32[]{:S(2)}, u32[]{:S(2)}) collective-permute-start(f32[64,512]{1,0:T(8,128)S(1)} %broadcast_select_fusion), channel_id=1, source_target_pairs={{0,16},{16,0},{32,48},{48,32},{64,80},{80,64},{96,112},{112,96},{1... | collective-permute-start | bytes 393224 | tf_op jit(solution)/shard_map/ppermute | solution.py:39
  68.5 1.1 %collective-permute-done.20 = f32[64,512]{1,0:T(8,128)S(1)} collective-permute-done((f32[64,512]{1,0:T(8,128)S(1)}, f32[64,512]{1,0:T(8,128)S(1)}, u32[]{:S(2)}, u32[]{:S(2)}) %collective-permute-start.20) | collective-permute-done | bytes 131104 | tf_op jit(solution)/shard_map/ppermute | solution.py:39
  69.6 1.9 %collective-permute-done.19 = f32[64,512]{1,0:T(8,128)S(1)} collective-permute-done((f32[64,512]{1,0:T(8,128)S(1)}, f32[64,512]{1,0:T(8,128)S(1)}, u32[]{:S(2)}, u32[]{:S(2)}) %collective-permute-start.19) | collective-permute-done | bytes 131104 | tf_op jit(solution)/shard_map/ppermute | solution.py:39
  71.5 0.8 %collective-permute-done.18 = f32[64,512]{1,0:T(8,128)S(1)} collective-permute-done((f32[64,512]{1,0:T(8,128)S(1)}, f32[64,512]{1,0:T(8,128)S(1)}, u32[]{:S(2)}, u32[]{:S(2)}) %collective-permute-start.18) | collective-permute-done | bytes 131104 | tf_op jit(solution)/shard_map/ppermute | solution.py:39
  72.3 0.7 fusion
  (21 shorter events, 0.5 us)
Async XLA Ops:
  0.0 9.7 %copy-start.4 = (s32[4]{0:T(128)S(1)}, s32[4]{0:T(128)}, u32[]{:S(2)}) copy-start(s32[4]{0:T(128)} %live.3) | copy-start | bytes 52
  0.0 1.2 %copy-start = (bf16[16384,32]{0,1:T(8,128)(2,1)S(1)}, bf16[16384,32]{0,1:T(8,128)(2,1)}, u32[]{:S(2)}) copy-start(bf16[16384,32]{0,1:T(8,128)(2,1)} %param.6) | copy-start | bytes 3145732
  1.2 0.7 copy-start.3
  2.8 18.9 %collective-permute-start = (bf16[4,16,4096]{2,1,0:T(8,128)(2,1)S(1)}, bf16[4,16,4096]{2,1,0:T(8,128)(2,1)S(1)}, u32[]{:S(2)}, u32[]{:S(2)}) collective-permute-start(bf16[4,16,4096]{2,1,0:T(8,128)(2,1)S(1)} %pick_live.1.after), channel_id=1, source_target_pairs={{0,2},{1,3},{2,0},{3,1},{4,6},{5,7},{6,4},{7,5},{8,10},{9,11},{10,... | collective-permute-start | bytes 1572872 | tf_op jit(solution)/shard_map/ppermute | solution.py:35
  4.5 17.2 %collective-permute-start.1 = (bf16[4,16,4096]{2,1,0:T(8,128)(2,1)S(1)}, bf16[4,16,4096]{2,1,0:T(8,128)(2,1)S(1)}, u32[]{:S(2)}, u32[]{:S(2)}) collective-permute-start(bf16[4,16,4096]{2,1,0:T(8,128)(2,1)S(1)} %pick_live.1.after), channel_id=1, source_target_pairs={{0,12},{1,13},{2,14},{3,15},{4,8},{5,9},{6,10},{7,11},{8,4},{9,5},... | collective-permute-start | bytes 1572872 | tf_op jit(solution)/shard_map/ppermute | solution.py:35
  7.5 14.2 %collective-permute-start.2 = (bf16[4,16,4096]{2,1,0:T(8,128)(2,1)S(1)}, bf16[4,16,4096]{2,1,0:T(8,128)(2,1)S(1)}, u32[]{:S(2)}, u32[]{:S(2)}) collective-permute-start(bf16[4,16,4096]{2,1,0:T(8,128)(2,1)S(1)} %pick_live.1.after), channel_id=1, source_target_pairs={{0,4},{1,5},{2,6},{3,7},{4,0},{5,1},{6,2},{7,3},{8,12},{9,13},{10,... | collective-permute-start | bytes 1572872 | tf_op jit(solution)/shard_map/ppermute | solution.py:35
  7.6 14.1 %collective-permute-start.3 = (bf16[256,128]{1,0:T(8,128)(2,1)}, bf16[256,128]{1,0:T(8,128)(2,1)S(1)}, u32[]{:S(2)}, u32[]{:S(2)}) collective-permute-start(bf16[256,128]{1,0:T(8,128)(2,1)} %refs_0_.1), channel_id=1, source_target_pairs={{0,8},{1,9},{2,10},{3,11},{4,12},{5,13},{6,14},{7,15},{8,0},{9,1},... | collective-permute-start | bytes 196616 | tf_op jit(solution)/shard_map/ppermute | solution.py:35
  9.2 8.6 %collective-permute-start.4 = (bf16[256,128]{1,0:T(8,128)(2,1)}, bf16[256,128]{1,0:T(8,128)(2,1)S(1)}, u32[]{:S(2)}, u32[]{:S(2)}) collective-permute-start(bf16[256,128]{1,0:T(8,128)(2,1)} %refs_0_.1), channel_id=1, source_target_pairs={{0,2},{1,3},{2,0},{3,1},{4,6},{5,7},{6,4},{7,5},{8,10},{9,11},{10,... | collective-permute-start | bytes 196616 | tf_op jit(solution)/shard_map/ppermute | solution.py:35
  9.7 8.1 %copy-start.2 = (bf16[256,128]{1,0:T(8,128)(2,1)S(1)}, bf16[256,128]{1,0:T(8,128)(2,1)}, u32[]{:S(2)}) copy-start(bf16[256,128]{1,0:T(8,128)(2,1)} %refs_0_.1) | copy-start | bytes 196612
  22.2 16.0 %collective-permute-start.5 = (bf16[5,16,4096]{2,1,0:T(8,128)(2,1)S(1)}, bf16[5,16,4096]{2,1,0:T(8,128)(2,1)S(1)}, u32[]{:S(2)}, u32[]{:S(2)}) collective-permute-start(bf16[5,16,4096]{2,1,0:T(8,128)(2,1)S(1)} %get-tuple-element.73), channel_id=1, source_target_pairs={{0,12},{1,13},{2,14},{3,15},{4,8},{5,9},{6,10},{7,11},{8,4},{9,5},... | collective-permute-start | bytes 1966088 | tf_op jit(solution)/shard_map/ppermute | solution.py:35
  25.2 14.4 %collective-permute-start.6 = (bf16[5,16,4096]{2,1,0:T(8,128)(2,1)S(1)}, bf16[5,16,4096]{2,1,0:T(8,128)(2,1)S(1)}, u32[]{:S(2)}, u32[]{:S(2)}) collective-permute-start(bf16[5,16,4096]{2,1,0:T(8,128)(2,1)S(1)} %get-tuple-element.72), channel_id=1, source_target_pairs={{0,4},{1,5},{2,6},{3,7},{4,0},{5,1},{6,2},{7,3},{8,12},{9,13},{10,... | collective-permute-start | bytes 1966088 | tf_op jit(solution)/shard_map/ppermute | solution.py:35
  25.2 14.4 %collective-permute-start.7 = (bf16[5,16,4096]{2,1,0:T(8,128)(2,1)S(1)}, bf16[5,16,4096]{2,1,0:T(8,128)(2,1)S(1)}, u32[]{:S(2)}, u32[]{:S(2)}) collective-permute-start(bf16[5,16,4096]{2,1,0:T(8,128)(2,1)S(1)} %get-tuple-element.74), channel_id=1, source_target_pairs={{0,2},{1,3},{2,0},{3,1},{4,6},{5,7},{6,4},{7,5},{8,10},{9,11},{10,... | collective-permute-start | bytes 1966088 | tf_op jit(solution)/shard_map/ppermute | solution.py:35
  25.8 18.2 %collective-permute-start.8 = (bf16[18,16,4096]{2,1,0:T(8,128)(2,1)S(1)}, bf16[18,16,4096]{2,1,0:T(8,128)(2,1)S(1)}, u32[]{:S(2)}, u32[]{:S(2)}) collective-permute-start(bf16[18,16,4096]{2,1,0:T(8,128)(2,1)S(1)} %constant_dynamic-update-slice_fusion.refs_0_), channel_id=1, source_target_pairs={{0,1},{1,0},{2,3},{3,2},{4,5},{5,4},{6,7},{7,6},{8,9},{9,8},{10,11... | collective-permute-start | bytes 7077896 | tf_op jit(solution)/shard_map/ppermute | solution.py:35
  39.8 4.2 %copy-start.1 = (bf16[8,8,512]{2,1,0:T(8,128)(2,1)S(1)}, bf16[8,8,512]{2,1,0:T(8,128)(2,1)}, u32[]{:S(2)}) copy-start(bf16[8,8,512]{2,1,0:T(8,128)(2,1)} %slab_amps.1) | copy-start | bytes 196612
  39.9 2.7 %collective-permute-start.10 = (bf16[8,16,4096]{2,1,0:T(8,128)(2,1)S(1)}, bf16[8,16,4096]{2,1,0:T(8,128)(2,1)S(1)}, u32[]{:S(2)}, u32[]{:S(2)}) collective-permute-start(bf16[8,16,4096]{2,1,0:T(8,128)(2,1)S(1)} %pad_maximum_fusion.refs_1_), channel_id=1, source_target_pairs={{0,1},{1,0},{2,3},{3,2},{4,5},{5,4},{6,7},{7,6},{8,9},{9,8},{10,11... | collective-permute-start | bytes 3145736 | tf_op jit(solution)/shard_map/ppermute | solution.py:35
  40.1 3.9 %collective-permute-start.9 = (bf16[7,16,4096]{2,1,0:T(8,128)(2,1)S(1)}, bf16[7,16,4096]{2,1,0:T(8,128)(2,1)S(1)}, u32[]{:S(2)}, u32[]{:S(2)}) collective-permute-start(bf16[7,16,4096]{2,1,0:T(8,128)(2,1)S(1)} %get-tuple-element.67.refs_1_), channel_id=1, source_target_pairs={{0,1},{1,0},{2,3},{3,2},{4,5},{5,4},{6,7},{7,6},{8,9},{9,8},{10,11... | collective-permute-start | bytes 2752520 | tf_op jit(solution)/shard_map/ppermute | solution.py:35
  40.7 9.5 %collective-permute-start.13 = (bf16[2,16,4096]{2,1,0:T(8,128)(2,1)S(1)}, bf16[2,16,4096]{2,1,0:T(8,128)(2,1)S(1)}, u32[]{:S(2)}, u32[]{:S(2)}) collective-permute-start(bf16[2,16,4096]{2,1,0:T(8,128)(2,1)S(1)} %pad_maximum_fusion.6), channel_id=1, source_target_pairs={{0,12},{1,13},{2,14},{3,15},{4,8},{5,9},{6,10},{7,11},{8,4},{9,5},... | collective-permute-start | bytes 786440 | tf_op jit(solution)/shard_map/ppermute | solution.py:35
  42.3 8.0 %collective-permute-start.14 = (bf16[2,16,4096]{2,1,0:T(8,128)(2,1)S(1)}, bf16[2,16,4096]{2,1,0:T(8,128)(2,1)S(1)}, u32[]{:S(2)}, u32[]{:S(2)}) collective-permute-start(bf16[2,16,4096]{2,1,0:T(8,128)(2,1)S(1)} %pad_maximum_fusion.7), channel_id=1, source_target_pairs={{0,4},{1,5},{2,6},{3,7},{4,0},{5,1},{6,2},{7,3},{8,12},{9,13},{10,... | collective-permute-start | bytes 786440 | tf_op jit(solution)/shard_map/ppermute | solution.py:35
  50.4 4.2 %collective-permute-start.15 = (bf16[4,16,4096]{2,1,0:T(8,128)(2,1)S(1)}, bf16[4,16,4096]{2,1,0:T(8,128)(2,1)S(1)}, u32[]{:S(2)}, u32[]{:S(2)}) collective-permute-start(bf16[4,16,4096]{2,1,0:T(8,128)(2,1)S(1)} %constant_dynamic-update-slice_fusion.6.refs_4_), channel_id=1, source_target_pairs={{0,1},{1,0},{2,3},{3,2},{4,5},{5,4},{6,7},{7,6},{8,9},{9,8},{10,11... | collective-permute-start | bytes 1572872 | tf_op jit(solution)/shard_map/ppermute | solution.py:35
  50.5 11.7 %collective-permute-start.12 = (f32[64,512]{1,0:T(8,128)S(1)}, f32[64,512]{1,0:T(8,128)S(1)}, u32[]{:S(2)}, u32[]{:S(2)}) collective-permute-start(f32[64,512]{1,0:T(8,128)S(1)} %get-tuple-element.48), channel_id=1, source_target_pairs={{0,96},{16,112},{32,64},{48,80},{64,32},{80,48},{96,0},{112,16},{1... | collective-permute-start | bytes 393224 | tf_op jit(solution)/shard_map/ppermute | solution.py:39
  54.6 10.6 %collective-permute-start.11 = (f32[64,512]{1,0:T(8,128)S(1)}, f32[64,512]{1,0:T(8,128)S(1)}, u32[]{:S(2)}, u32[]{:S(2)}) collective-permute-start(f32[64,512]{1,0:T(8,128)S(1)} %get-tuple-element.47), channel_id=1, source_target_pairs={{0,32},{16,48},{32,0},{48,16},{64,96},{80,112},{96,64},{112,80},{1... | collective-permute-start | bytes 393224 | tf_op jit(solution)/shard_map/ppermute | solution.py:39
  57.5 7.7 %collective-permute-start.17 = (f32[64,512]{1,0:T(8,128)S(1)}, f32[64,512]{1,0:T(8,128)S(1)}, u32[]{:S(2)}, u32[]{:S(2)}) collective-permute-start(f32[64,512]{1,0:T(8,128)S(1)} %get-tuple-element.56), channel_id=1, source_target_pairs={{0,96},{16,112},{32,64},{48,80},{64,32},{80,48},{96,0},{112,16},{1... | collective-permute-start | bytes 393224 | tf_op jit(solution)/shard_map/ppermute | solution.py:39
  59.3 6.4 %collective-permute-start.16 = (f32[64,512]{1,0:T(8,128)S(1)}, f32[64,512]{1,0:T(8,128)S(1)}, u32[]{:S(2)}, u32[]{:S(2)}) collective-permute-start(f32[64,512]{1,0:T(8,128)S(1)} %get-tuple-element.55), channel_id=1, source_target_pairs={{0,32},{16,48},{32,0},{48,16},{64,96},{80,112},{96,64},{112,80},{1... | collective-permute-start | bytes 393224 | tf_op jit(solution)/shard_map/ppermute | solution.py:39
  59.5 10.1 %collective-permute-start.20 = (f32[64,512]{1,0:T(8,128)S(1)}, f32[64,512]{1,0:T(8,128)S(1)}, u32[]{:S(2)}, u32[]{:S(2)}) collective-permute-start(f32[64,512]{1,0:T(8,128)S(1)} %get-tuple-element.58), channel_id=1, source_target_pairs={{0,64},{16,80},{32,96},{48,112},{64,0},{80,16},{96,32},{112,48},{1... | collective-permute-start | bytes 393224 | tf_op jit(solution)/shard_map/ppermute | solution.py:39
  62.2 9.3 %collective-permute-start.19 = (f32[64,512]{1,0:T(8,128)S(1)}, f32[64,512]{1,0:T(8,128)S(1)}, u32[]{:S(2)}, u32[]{:S(2)}) collective-permute-start(f32[64,512]{1,0:T(8,128)S(1)} %get-tuple-element.57), channel_id=1, source_target_pairs={{0,80},{16,64},{32,112},{48,96},{64,16},{80,0},{96,48},{112,32},{1... | collective-permute-start | bytes 393224 | tf_op jit(solution)/shard_map/ppermute | solution.py:39
  65.7 6.6 %collective-permute-start.18 = (f32[64,512]{1,0:T(8,128)S(1)}, f32[64,512]{1,0:T(8,128)S(1)}, u32[]{:S(2)}, u32[]{:S(2)}) collective-permute-start(f32[64,512]{1,0:T(8,128)S(1)} %broadcast_select_fusion), channel_id=1, source_target_pairs={{0,16},{16,0},{32,48},{48,32},{64,80},{80,64},{96,112},{112,96},{1... | collective-permute-start | bytes 393224 | tf_op jit(solution)/shard_map/ppermute | solution.py:39

commit v7 on v6

--- a/solution.py
+++ b/solution.py
@@ -249,7 +249,7 @@
     live_amps, token = load_live(live_pairs, amplitudes, own)
     cycle_beside, token = together(cycle_beside, token)
     pair = pack(cycle_integrals, cycle_beside)
-    beside, above, below, cycle_far, pair, token = together(beside, above, below, cycle_far, pair, token)
+    below, above, beside, cycle_far, pair, token = together(below, above, beside, cycle_far, pair, token)
 
     far = pack(cycle_far)
     from_above = move(jnp.concatenate([below[0:2], beside[0:2], pair]), dy=3)
@@ -293,7 +293,7 @@
 
     mine = lax.axis_index("row") % NH == (lax.axis_index("blk") // NC) % NX
     total = jnp.where(mine, near_sum, far_sum) + move_row(jnp.where(mine, far_sum, near_sum), dx=1)
-    total = total + move_row(other, dz=2, dx=1) + move_row(far[2], dz=2)
+    total = total + move_row(far[2], dz=2) + move_row(other, dz=2, dx=1)
     return total.astype(jnp.bfloat16).T
 
 

time: 73.1 us -> 71.7 us (0.981)
  waiting for transfers between devices: 28.7 us -> 27.4 us
    ppermute x14, waiting for transfers between devices: 24.5 us -> 22.9 us  [move(): return lax.ppermute(value, 'blk', blk_moves(dy, dx, dc))]
  transfers between devices with their start and end apart: 21 -> 21, of which waited for: 11 -> 9; matrix products, arithmetic and copies ran while one was open for 1% -> 1% of each run, Pallas kernels for 16% -> 17%
where the time goes in v7:
time: 71.7 us; the launch traced here: 71.5 us
  starting transfers between devices  27.6 us (38%)
  waiting for transfers between devices  27.4 us (38%)
  Pallas kernels  12.8 us (18%)
  local copies, waits for them, and re-layouts  2.36 us (3%)
  other arithmetic  1.17 us (2%)
    ppermute x14, waiting for transfers between devices, move(): return lax.ppermute(value, 'blk', blk_moves(dy, dx, dc))  22.9 us
    ppermute x7, starting transfers between devices, move_row(): return lax.ppermute(value, 'row', row_moves(dz, dx))  14.3 us
    ppermute x14, starting transfers between devices, move(): return lax.ppermute(value, 'blk', blk_moves(dy, dx, dc))  13.3 us
    pallas_call x2, Pallas kernels, ladder(): pl.pallas_call(functools.partial(ladder_kernel, places, e, len(pieces)),...  5.7 us
    ppermute x7, waiting for transfers between devices, move_row(): return lax.ppermute(value, 'row', row_moves(dz, dx))  4.42 us
    pallas_call x1, Pallas kernels, load_live(): pl.pallas_call(load_kernel, out_shape=(jax.ShapeDtypeStruct((2 * KT, rows...  4.05 us
    pallas_call x1, Pallas kernels, cycle_sums(): pl.pallas_call(functools.partial(cycle_kernel, places, width), out_shape=...  2.09 us
    unnamed x16, local copies, waits for them, and re-layouts  2.08 us
  transfers between devices with their start and end apart: 21, of which 9 were waited for; matrix products, arithmetic and copies ran while one was open for 1% of the time, Pallas kernels for 17%

profile of v7, /device:TPU:0, one launch (start us, length us, event | category | flops | bytes accessed | tf_op | source)
XLA Modules:
  0.0 71.5 jit_solution(15569351050485310192)
XLA Ops:
  0.0 0.0 copy-start.4
  0.0 0.0 copy-start
  0.0 1.2 %copy-done = bf16[16384,32]{0,1:T(8,128)(2,1)S(1)} copy-done((bf16[16384,32]{0,1:T(8,128)(2,1)S(1)}, bf16[16384,32]{0,1:T(8,128)(2,1)}, u32[]{:S(2)}) %copy-start) | copy-done | bytes 1048600
  1.2 0.0 copy-start.3
  1.2 0.7 copy-done.3
  1.9 0.9 %pick_live.1.after = bf16[4,16,4096]{2,1,0:T(8,128)(2,1)S(1)} custom-call(s32[4]{0:T(128)S(1)} %copy-done.3, bf16[32,16384]{1,0:T(8,128)(2,1)S(1)} %bitcast.3), custom_call_target="tpu_custom_call" | custom-call | tf_op jit(solution)/shard_map/pick_live/pallas_call | solution.py:66
  2.8 1.7 %collective-permute-start = (bf16[4,16,4096]{2,1,0:T(8,128)(2,1)S(1)}, bf16[4,16,4096]{2,1,0:T(8,128)(2,1)S(1)}, u32[]{:S(2)}, u32[]{:S(2)}) collective-permute-start(bf16[4,16,4096]{2,1,0:T(8,128)(2,1)S(1)} %pick_live.1.after), channel_id=1, source_target_pairs={{0,4},{1,5},{2,6},{3,7},{4,0},{5,1},{6,2},{7,3},{8,12},{9,13},{10,... | collective-permute-start | bytes 1572872 | tf_op jit(solution)/shard_map/ppermute | solution.py:35
  4.6 2.2 %collective-permute-start.1 = (bf16[4,16,4096]{2,1,0:T(8,128)(2,1)S(1)}, bf16[4,16,4096]{2,1,0:T(8,128)(2,1)S(1)}, u32[]{:S(2)}, u32[]{:S(2)}) collective-permute-start(bf16[4,16,4096]{2,1,0:T(8,128)(2,1)S(1)} %pick_live.1.after), channel_id=1, source_target_pairs={{0,12},{1,13},{2,14},{3,15},{4,8},{5,9},{6,10},{7,11},{8,4},{9,5},... | collective-permute-start | bytes 1572872 | tf_op jit(solution)/shard_map/ppermute | solution.py:35
  6.8 1.5 %collective-permute-start.2 = (bf16[4,16,4096]{2,1,0:T(8,128)(2,1)S(1)}, bf16[4,16,4096]{2,1,0:T(8,128)(2,1)S(1)}, u32[]{:S(2)}, u32[]{:S(2)}) collective-permute-start(bf16[4,16,4096]{2,1,0:T(8,128)(2,1)S(1)} %pick_live.1.after), channel_id=1, source_target_pairs={{0,2},{1,3},{2,0},{3,1},{4,6},{5,7},{6,4},{7,5},{8,10},{9,11},{10,... | collective-permute-start | bytes 1572872 | tf_op jit(solution)/shard_map/ppermute | solution.py:35
  8.2 0.7 %collective-permute-start.3 = (bf16[256,128]{1,0:T(8,128)(2,1)}, bf16[256,128]{1,0:T(8,128)(2,1)S(1)}, u32[]{:S(2)}, u32[]{:S(2)}) collective-permute-start(bf16[256,128]{1,0:T(8,128)(2,1)} %refs_0_.1), channel_id=1, source_target_pairs={{0,8},{1,9},{2,10},{3,11},{4,12},{5,13},{6,14},{7,15},{8,0},{9,1},... | collective-permute-start | bytes 196616 | tf_op jit(solution)/shard_map/ppermute | solution.py:35
  9.0 0.5 collective-permute-start.4
  9.5 0.0 copy-done.4
  9.6 0.0 copy-start.2
  9.6 4.1 %load_live.1 = (bf16[8,512,1024]{2,1,0:T(8,128)(2,1)S(1)}, f32[8,128]{1,0:T(8,128)S(1)}) custom-call(s32[4]{0:T(128)S(1)} %copy-done.4, bf16[512,16384]{1,0:T(8,128)(2,1)} %amps.1, bf16[4,16,4096]{2,1,0:T(8,128)(2,1)S(1)} %pick_live.1.after), custom_call_target="tpu_custom_call" | custom-call | tf_op jit(solution)/shard_map/load_live/pallas_call | solution.py:93
  13.6 7.6 %collective-permute-done.4.refs_1_ = bf16[256,128]{1,0:T(8,128)(2,1)S(1)} collective-permute-done((bf16[256,128]{1,0:T(8,128)(2,1)}, bf16[256,128]{1,0:T(8,128)(2,1)S(1)}, u32[]{:S(2)}, u32[]{:S(2)}) %collective-permute-start.4) | collective-permute-done | bytes 65568 | tf_op jit(solution)/shard_map/ppermute | solution.py:35
  21.3 0.0 copy-done.2
  21.3 0.0 collective-permute-done.3.refs_0_
  21.3 0.0 collective-permute-done
  21.3 0.0 collective-permute-done.1
  21.3 0.0 collective-permute-done.2
  21.6 0.2 pad_maximum_fusion.1
  21.8 1.5 %collective-permute-start.5 = (bf16[5,16,4096]{2,1,0:T(8,128)(2,1)S(1)}, bf16[5,16,4096]{2,1,0:T(8,128)(2,1)S(1)}, u32[]{:S(2)}, u32[]{:S(2)}) collective-permute-start(bf16[5,16,4096]{2,1,0:T(8,128)(2,1)S(1)} %get-tuple-element.73), channel_id=1, source_target_pairs={{0,12},{1,13},{2,14},{3,15},{4,8},{5,9},{6,10},{7,11},{8,4},{9,5},... | collective-permute-start | bytes 1966088 | tf_op jit(solution)/shard_map/ppermute | solution.py:35
  23.3 0.0 collective-permute-start.6
  23.3 1.5 %collective-permute-start.7 = (bf16[5,16,4096]{2,1,0:T(8,128)(2,1)S(1)}, bf16[5,16,4096]{2,1,0:T(8,128)(2,1)S(1)}, u32[]{:S(2)}, u32[]{:S(2)}) collective-permute-start(bf16[5,16,4096]{2,1,0:T(8,128)(2,1)S(1)} %get-tuple-element.74), channel_id=1, source_target_pairs={{0,2},{1,3},{2,0},{3,1},{4,6},{5,7},{6,4},{7,5},{8,10},{9,11},{10,... | collective-permute-start | bytes 1966088 | tf_op jit(solution)/shard_map/ppermute | solution.py:35
  24.8 0.1 collective-permute-start.8
  24.9 13.2 %collective-permute-done.5 = bf16[5,16,4096]{2,1,0:T(8,128)(2,1)S(1)} collective-permute-done((bf16[5,16,4096]{2,1,0:T(8,128)(2,1)S(1)}, bf16[5,16,4096]{2,1,0:T(8,128)(2,1)S(1)}, u32[]{:S(2)}, u32[]{:S(2)}) %collective-permute-start.5) | collective-permute-done | bytes 655392 | tf_op jit(solution)/shard_map/ppermute | solution.py:35
  38.1 0.2 collective-permute-done.6
  38.3 0.0 collective-permute-done.7
  38.5 0.0 copy-start.1
  38.5 0.1 pad_maximum_fusion.refs_1_
  38.6 0.1 collective-permute-start.10
  38.8 0.6 collective-permute-start.9
  39.4 1.6 %collective-permute-start.13 = (bf16[2,16,4096]{2,1,0:T(8,128)(2,1)S(1)}, bf16[2,16,4096]{2,1,0:T(8,128)(2,1)S(1)}, u32[]{:S(2)}, u32[]{:S(2)}) collective-permute-start(bf16[2,16,4096]{2,1,0:T(8,128)(2,1)S(1)} %pad_maximum_fusion.6), channel_id=1, source_target_pairs={{0,12},{1,13},{2,14},{3,15},{4,8},{5,9},{6,10},{7,11},{8,4},{9,5},... | collective-permute-start | bytes 786440 | tf_op jit(solution)/shard_map/ppermute | solution.py:35
  41.0 1.2 %collective-permute-start.14 = (bf16[2,16,4096]{2,1,0:T(8,128)(2,1)S(1)}, bf16[2,16,4096]{2,1,0:T(8,128)(2,1)S(1)}, u32[]{:S(2)}, u32[]{:S(2)}) collective-permute-start(bf16[2,16,4096]{2,1,0:T(8,128)(2,1)S(1)} %pad_maximum_fusion.7), channel_id=1, source_target_pairs={{0,4},{1,5},{2,6},{3,7},{4,0},{5,1},{6,2},{7,3},{8,12},{9,13},{10,... | collective-permute-start | bytes 786440 | tf_op jit(solution)/shard_map/ppermute | solution.py:35
  42.2 0.0 collective-permute-done.10.refs_3_
  42.2 0.4 collective-permute-done.9.refs_3_
  42.7 0.0 collective-permute-done.8.refs_2_
  42.7 0.0 copy-done.1
  42.7 2.1 %cycle.1 = f32[4,512,128]{2,1,0:T(8,128)S(1)} custom-call(bf16[8,8,512]{2,1,0:T(8,128)(2,1)S(1)} %copy-done.1, f32[8,128]{1,0:T(8,128)S(1)} %get-tuple-element.45.token.before, bf16[18,16,4096]{2,1,0:T(8,128)(2,1)S(1)} %constant_dynamic-update-slice_fusion.refs_0_, bf16[7,16,4096]{2,1,0:T(8,128)(2,1)S(1)} %get-tuple-element.67.refs_1_, ...), custom_call_target="tpu_custom_call" | custom-call | flops 134217728 | bytes 8388608 | tf_op jit(solution)/shard_map/cycle/pallas_call | solution.py:221
  44.8 2.8 %ladder.2 = (f32[64,512]{1,0:T(8,128)S(1)}, f32[64,512]{1,0:T(8,128)S(1)}, f32[64,512]{1,0:T(8,128)S(1)}, f32[64,512]{1,0:T(8,128)S(1)}, f32[8,128]{1,0:T(8,128)}) custom-call(bf16[8,512,1024]{2,1,0:T(8,128)(2,1)S(1)} %get-tuple-element.32.amps, f32[4,512,128]{2,1,0:T(8,128)S(1)} %cycle.1, f32[8,128]{1,0:T(8,128)S(1)} %get-tuple-element.45.token.before, ...), custom_call_target="tpu_custom_call" | custom-call | flops 2147483648 | bytes 4194304 | tf_op jit(solution)/shard_map/ladder/pallas_call | solution.py:153
  47.6 1.3 %collective-permute-done.13 = bf16[2,16,4096]{2,1,0:T(8,128)(2,1)S(1)} collective-permute-done((bf16[2,16,4096]{2,1,0:T(8,128)(2,1)S(1)}, bf16[2,16,4096]{2,1,0:T(8,128)(2,1)S(1)}, u32[]{:S(2)}, u32[]{:S(2)}) %collective-permute-start.13) | collective-permute-done | bytes 262176 | tf_op jit(solution)/shard_map/ppermute | solution.py:35
  48.9 0.1 collective-permute-done.14
  49.1 0.1 collective-permute-start.15
  49.2 4.1 %collective-permute-start.12 = (f32[64,512]{1,0:T(8,128)S(1)}, f32[64,512]{1,0:T(8,128)S(1)}, u32[]{:S(2)}, u32[]{:S(2)}) collective-permute-start(f32[64,512]{1,0:T(8,128)S(1)} %get-tuple-element.48), channel_id=1, source_target_pairs={{0,96},{16,112},{32,64},{48,80},{64,32},{80,48},{96,0},{112,16},{1... | collective-permute-start | bytes 393224 | tf_op jit(solution)/shard_map/ppermute | solution.py:39
  53.3 0.0 collective-permute-start.11
  53.3 0.0 collective-permute-done.15.refs_5_
  53.3 2.9 %ladder.3 = (f32[64,512]{1,0:T(8,128)S(1)}, f32[64,512]{1,0:T(8,128)S(1)}, f32[64,512]{1,0:T(8,128)S(1)}, f32[64,512]{1,0:T(8,128)S(1)}, f32[64,512]{1,0:T(8,128)S(1)}, /*index=5*/f32[8,128]{1,0:T(8,128)}) custom-call(bf16[8,512,1024]{2,1,0:T(8,128)(2,1)S(1)} %get-tuple-element.32.amps, f32[4,512,128]{2,1,0:T(8,128)S(1)} %cycle.1, ...), custom_call_target="tpu_custom_call" | custom-call | flops 2147483648 | bytes 4194304 | tf_op jit(solution)/shard_map/ladder/pallas_call | solution.py:153
  56.2 1.8 %collective-permute-start.17 = (f32[64,512]{1,0:T(8,128)S(1)}, f32[64,512]{1,0:T(8,128)S(1)}, u32[]{:S(2)}, u32[]{:S(2)}) collective-permute-start(f32[64,512]{1,0:T(8,128)S(1)} %get-tuple-element.56), channel_id=1, source_target_pairs={{0,96},{16,112},{32,64},{48,80},{64,32},{80,48},{96,0},{112,16},{1... | collective-permute-start | bytes 393224 | tf_op jit(solution)/shard_map/ppermute | solution.py:39
  58.0 0.2 collective-permute-start.16
  58.2 5.1 %collective-permute-start.20 = (f32[64,512]{1,0:T(8,128)S(1)}, f32[64,512]{1,0:T(8,128)S(1)}, u32[]{:S(2)}, u32[]{:S(2)}) collective-permute-start(f32[64,512]{1,0:T(8,128)S(1)} %get-tuple-element.58), channel_id=1, source_target_pairs={{0,80},{16,64},{32,112},{48,96},{64,16},{80,0},{96,48},{112,32},{1... | collective-permute-start | bytes 393224 | tf_op jit(solution)/shard_map/ppermute | solution.py:39
  63.3 0.0 collective-permute-done.12
  63.3 0.9 %collective-permute-start.19 = (f32[64,512]{1,0:T(8,128)S(1)}, f32[64,512]{1,0:T(8,128)S(1)}, u32[]{:S(2)}, u32[]{:S(2)}) collective-permute-start(f32[64,512]{1,0:T(8,128)S(1)} %get-tuple-element.57), channel_id=1, source_target_pairs={{0,64},{16,80},{32,96},{48,112},{64,0},{80,16},{96,32},{112,48},{1... | collective-permute-start | bytes 393224 | tf_op jit(solution)/shard_map/ppermute | solution.py:39
  64.2 0.0 collective-permute-done.11
  64.2 0.0 collective-permute-done.17
  64.2 0.0 collective-permute-done.16
  64.2 0.1 broadcast_select_fusion
  64.3 2.1 %collective-permute-start.18 = (f32[64,512]{1,0:T(8,128)S(1)}, f32[64,512]{1,0:T(8,128)S(1)}, u32[]{:S(2)}, u32[]{:S(2)}) collective-permute-start(f32[64,512]{1,0:T(8,128)S(1)} %broadcast_select_fusion), channel_id=1, source_target_pairs={{0,16},{16,0},{32,48},{48,32},{64,80},{80,64},{96,112},{112,96},{1... | collective-permute-start | bytes 393224 | tf_op jit(solution)/shard_map/ppermute | solution.py:39
  66.4 0.8 %collective-permute-done.20 = f32[64,512]{1,0:T(8,128)S(1)} collective-permute-done((f32[64,512]{1,0:T(8,128)S(1)}, f32[64,512]{1,0:T(8,128)S(1)}, u32[]{:S(2)}, u32[]{:S(2)}) %collective-permute-start.20) | collective-permute-done | bytes 131104 | tf_op jit(solution)/shard_map/ppermute | solution.py:39
  67.2 2.8 %collective-permute-done.19 = f32[64,512]{1,0:T(8,128)S(1)} collective-permute-done((f32[64,512]{1,0:T(8,128)S(1)}, f32[64,512]{1,0:T(8,128)S(1)}, u32[]{:S(2)}, u32[]{:S(2)}) %collective-permute-start.19) | collective-permute-done | bytes 131104 | tf_op jit(solution)/shard_map/ppermute | solution.py:39
  70.0 0.9 %collective-permute-done.18 = f32[64,512]{1,0:T(8,128)S(1)} collective-permute-done((f32[64,512]{1,0:T(8,128)S(1)}, f32[64,512]{1,0:T(8,128)S(1)}, u32[]{:S(2)}, u32[]{:S(2)}) %collective-permute-start.18) | collective-permute-done | bytes 131104 | tf_op jit(solution)/shard_map/ppermute | solution.py:39
  70.8 0.7 %fusion = bf16[512,64]{0,1:T(8,128)(2,1)} fusion(f32[64,512]{1,0:T(8,128)S(1)} %collective-permute-done.20, f32[64,512]{1,0:T(8,128)S(1)} %collective-permute-done.19, f32[64,512]{1,0:T(8,128)S(1)} %collective-permute-done.18, pred[]{:T(512)S(6)} %eq.6, f32[64,512]{1,0:T(8,128)S(1)} %collective-permute-done.12, f32[64,512]{1,0:T(8,128)S(1)} %get-tuple-element.46, ...), kind=kLoop, calls=%fused_computation.16 | loop fusion | flops 294912 | bytes 1245185 | tf_op jit(solution)/shard_map/transpose | solution.py:297
  (21 shorter events, 0.5 us)
Async XLA Ops:
  0.0 9.5 %copy-start.4 = (s32[4]{0:T(128)S(1)}, s32[4]{0:T(128)}, u32[]{:S(2)}) copy-start(s32[4]{0:T(128)} %live.3) | copy-start | bytes 52
  0.0 1.2 %copy-start = (bf16[16384,32]{0,1:T(8,128)(2,1)S(1)}, bf16[16384,32]{0,1:T(8,128)(2,1)}, u32[]{:S(2)}) copy-start(bf16[16384,32]{0,1:T(8,128)(2,1)} %param.6) | copy-start | bytes 3145732
  1.2 0.7 copy-start.3
  2.8 18.5 %collective-permute-start = (bf16[4,16,4096]{2,1,0:T(8,128)(2,1)S(1)}, bf16[4,16,4096]{2,1,0:T(8,128)(2,1)S(1)}, u32[]{:S(2)}, u32[]{:S(2)}) collective-permute-start(bf16[4,16,4096]{2,1,0:T(8,128)(2,1)S(1)} %pick_live.1.after), channel_id=1, source_target_pairs={{0,4},{1,5},{2,6},{3,7},{4,0},{5,1},{6,2},{7,3},{8,12},{9,13},{10,... | collective-permute-start | bytes 1572872 | tf_op jit(solution)/shard_map/ppermute | solution.py:35
  4.6 16.7 %collective-permute-start.1 = (bf16[4,16,4096]{2,1,0:T(8,128)(2,1)S(1)}, bf16[4,16,4096]{2,1,0:T(8,128)(2,1)S(1)}, u32[]{:S(2)}, u32[]{:S(2)}) collective-permute-start(bf16[4,16,4096]{2,1,0:T(8,128)(2,1)S(1)} %pick_live.1.after), channel_id=1, source_target_pairs={{0,12},{1,13},{2,14},{3,15},{4,8},{5,9},{6,10},{7,11},{8,4},{9,5},... | collective-permute-start | bytes 1572872 | tf_op jit(solution)/shard_map/ppermute | solution.py:35
  6.8 14.6 %collective-permute-start.2 = (bf16[4,16,4096]{2,1,0:T(8,128)(2,1)S(1)}, bf16[4,16,4096]{2,1,0:T(8,128)(2,1)S(1)}, u32[]{:S(2)}, u32[]{:S(2)}) collective-permute-start(bf16[4,16,4096]{2,1,0:T(8,128)(2,1)S(1)} %pick_live.1.after), channel_id=1, source_target_pairs={{0,2},{1,3},{2,0},{3,1},{4,6},{5,7},{6,4},{7,5},{8,10},{9,11},{10,... | collective-permute-start | bytes 1572872 | tf_op jit(solution)/shard_map/ppermute | solution.py:35
  8.2 13.0 %collective-permute-start.3 = (bf16[256,128]{1,0:T(8,128)(2,1)}, bf16[256,128]{1,0:T(8,128)(2,1)S(1)}, u32[]{:S(2)}, u32[]{:S(2)}) collective-permute-start(bf16[256,128]{1,0:T(8,128)(2,1)} %refs_0_.1), channel_id=1, source_target_pairs={{0,8},{1,9},{2,10},{3,11},{4,12},{5,13},{6,14},{7,15},{8,0},{9,1},... | collective-permute-start | bytes 196616 | tf_op jit(solution)/shard_map/ppermute | solution.py:35
  9.0 12.3 %collective-permute-start.4 = (bf16[256,128]{1,0:T(8,128)(2,1)}, bf16[256,128]{1,0:T(8,128)(2,1)S(1)}, u32[]{:S(2)}, u32[]{:S(2)}) collective-permute-start(bf16[256,128]{1,0:T(8,128)(2,1)} %refs_0_.1), channel_id=1, source_target_pairs={{0,2},{1,3},{2,0},{3,1},{4,6},{5,7},{6,4},{7,5},{8,10},{9,11},{10,... | collective-permute-start | bytes 196616 | tf_op jit(solution)/shard_map/ppermute | solution.py:35
  9.6 11.7 %copy-start.2 = (bf16[256,128]{1,0:T(8,128)(2,1)S(1)}, bf16[256,128]{1,0:T(8,128)(2,1)}, u32[]{:S(2)}) copy-start(bf16[256,128]{1,0:T(8,128)(2,1)} %refs_0_.1) | copy-start | bytes 196612
  21.8 16.3 %collective-permute-start.5 = (bf16[5,16,4096]{2,1,0:T(8,128)(2,1)S(1)}, bf16[5,16,4096]{2,1,0:T(8,128)(2,1)S(1)}, u32[]{:S(2)}, u32[]{:S(2)}) collective-permute-start(bf16[5,16,4096]{2,1,0:T(8,128)(2,1)S(1)} %get-tuple-element.73), channel_id=1, source_target_pairs={{0,12},{1,13},{2,14},{3,15},{4,8},{5,9},{6,10},{7,11},{8,4},{9,5},... | collective-permute-start | bytes 1966088 | tf_op jit(solution)/shard_map/ppermute | solution.py:35
  23.3 15.0 %collective-permute-start.6 = (bf16[5,16,4096]{2,1,0:T(8,128)(2,1)S(1)}, bf16[5,16,4096]{2,1,0:T(8,128)(2,1)S(1)}, u32[]{:S(2)}, u32[]{:S(2)}) collective-permute-start(bf16[5,16,4096]{2,1,0:T(8,128)(2,1)S(1)} %get-tuple-element.72), channel_id=1, source_target_pairs={{0,4},{1,5},{2,6},{3,7},{4,0},{5,1},{6,2},{7,3},{8,12},{9,13},{10,... | collective-permute-start | bytes 1966088 | tf_op jit(solution)/shard_map/ppermute | solution.py:35
  23.3 15.0 %collective-permute-start.7 = (bf16[5,16,4096]{2,1,0:T(8,128)(2,1)S(1)}, bf16[5,16,4096]{2,1,0:T(8,128)(2,1)S(1)}, u32[]{:S(2)}, u32[]{:S(2)}) collective-permute-start(bf16[5,16,4096]{2,1,0:T(8,128)(2,1)S(1)} %get-tuple-element.74), channel_id=1, source_target_pairs={{0,2},{1,3},{2,0},{3,1},{4,6},{5,7},{6,4},{7,5},{8,10},{9,11},{10,... | collective-permute-start | bytes 1966088 | tf_op jit(solution)/shard_map/ppermute | solution.py:35
  24.8 17.8 %collective-permute-start.8 = (bf16[18,16,4096]{2,1,0:T(8,128)(2,1)S(1)}, bf16[18,16,4096]{2,1,0:T(8,128)(2,1)S(1)}, u32[]{:S(2)}, u32[]{:S(2)}) collective-permute-start(bf16[18,16,4096]{2,1,0:T(8,128)(2,1)S(1)} %constant_dynamic-update-slice_fusion.refs_0_), channel_id=1, source_target_pairs={{0,1},{1,0},{2,3},{3,2},{4,5},{5,4},{6,7},{7,6},{8,9},{9,8},{10,11... | collective-permute-start | bytes 7077896 | tf_op jit(solution)/shard_map/ppermute | solution.py:35
  38.5 4.2 %copy-start.1 = (bf16[8,8,512]{2,1,0:T(8,128)(2,1)S(1)}, bf16[8,8,512]{2,1,0:T(8,128)(2,1)}, u32[]{:S(2)}) copy-start(bf16[8,8,512]{2,1,0:T(8,128)(2,1)} %slab_amps.1) | copy-start | bytes 196612
  38.6 3.6 %collective-permute-start.10 = (bf16[8,16,4096]{2,1,0:T(8,128)(2,1)S(1)}, bf16[8,16,4096]{2,1,0:T(8,128)(2,1)S(1)}, u32[]{:S(2)}, u32[]{:S(2)}) collective-permute-start(bf16[8,16,4096]{2,1,0:T(8,128)(2,1)S(1)} %pad_maximum_fusion.refs_1_), channel_id=1, source_target_pairs={{0,1},{1,0},{2,3},{3,2},{4,5},{5,4},{6,7},{7,6},{8,9},{9,8},{10,11... | collective-permute-start | bytes 3145736 | tf_op jit(solution)/shard_map/ppermute | solution.py:35
  38.8 3.9 %collective-permute-start.9 = (bf16[7,16,4096]{2,1,0:T(8,128)(2,1)S(1)}, bf16[7,16,4096]{2,1,0:T(8,128)(2,1)S(1)}, u32[]{:S(2)}, u32[]{:S(2)}) collective-permute-start(bf16[7,16,4096]{2,1,0:T(8,128)(2,1)S(1)} %get-tuple-element.67.refs_1_), channel_id=1, source_target_pairs={{0,1},{1,0},{2,3},{3,2},{4,5},{5,4},{6,7},{7,6},{8,9},{9,8},{10,11... | collective-permute-start | bytes 2752520 | tf_op jit(solution)/shard_map/ppermute | solution.py:35
  39.4 9.5 %collective-permute-start.13 = (bf16[2,16,4096]{2,1,0:T(8,128)(2,1)S(1)}, bf16[2,16,4096]{2,1,0:T(8,128)(2,1)S(1)}, u32[]{:S(2)}, u32[]{:S(2)}) collective-permute-start(bf16[2,16,4096]{2,1,0:T(8,128)(2,1)S(1)} %pad_maximum_fusion.6), channel_id=1, source_target_pairs={{0,12},{1,13},{2,14},{3,15},{4,8},{5,9},{6,10},{7,11},{8,4},{9,5},... | collective-permute-start | bytes 786440 | tf_op jit(solution)/shard_map/ppermute | solution.py:35
  41.0 8.0 %collective-permute-start.14 = (bf16[2,16,4096]{2,1,0:T(8,128)(2,1)S(1)}, bf16[2,16,4096]{2,1,0:T(8,128)(2,1)S(1)}, u32[]{:S(2)}, u32[]{:S(2)}) collective-permute-start(bf16[2,16,4096]{2,1,0:T(8,128)(2,1)S(1)} %pad_maximum_fusion.7), channel_id=1, source_target_pairs={{0,4},{1,5},{2,6},{3,7},{4,0},{5,1},{6,2},{7,3},{8,12},{9,13},{10,... | collective-permute-start | bytes 786440 | tf_op jit(solution)/shard_map/ppermute | solution.py:35
  49.1 4.2 %collective-permute-start.15 = (bf16[4,16,4096]{2,1,0:T(8,128)(2,1)S(1)}, bf16[4,16,4096]{2,1,0:T(8,128)(2,1)S(1)}, u32[]{:S(2)}, u32[]{:S(2)}) collective-permute-start(bf16[4,16,4096]{2,1,0:T(8,128)(2,1)S(1)} %constant_dynamic-update-slice_fusion.6.refs_4_), channel_id=1, source_target_pairs={{0,1},{1,0},{2,3},{3,2},{4,5},{5,4},{6,7},{7,6},{8,9},{9,8},{10,11... | collective-permute-start | bytes 1572872 | tf_op jit(solution)/shard_map/ppermute | solution.py:35
  49.2 14.2 %collective-permute-start.12 = (f32[64,512]{1,0:T(8,128)S(1)}, f32[64,512]{1,0:T(8,128)S(1)}, u32[]{:S(2)}, u32[]{:S(2)}) collective-permute-start(f32[64,512]{1,0:T(8,128)S(1)} %get-tuple-element.48), channel_id=1, source_target_pairs={{0,96},{16,112},{32,64},{48,80},{64,32},{80,48},{96,0},{112,16},{1... | collective-permute-start | bytes 393224 | tf_op jit(solution)/shard_map/ppermute | solution.py:39
  53.3 10.9 %collective-permute-start.11 = (f32[64,512]{1,0:T(8,128)S(1)}, f32[64,512]{1,0:T(8,128)S(1)}, u32[]{:S(2)}, u32[]{:S(2)}) collective-permute-start(f32[64,512]{1,0:T(8,128)S(1)} %get-tuple-element.47), channel_id=1, source_target_pairs={{0,32},{16,48},{32,0},{48,16},{64,96},{80,112},{96,64},{112,80},{1... | collective-permute-start | bytes 393224 | tf_op jit(solution)/shard_map/ppermute | solution.py:39
  56.2 8.0 %collective-permute-start.17 = (f32[64,512]{1,0:T(8,128)S(1)}, f32[64,512]{1,0:T(8,128)S(1)}, u32[]{:S(2)}, u32[]{:S(2)}) collective-permute-start(f32[64,512]{1,0:T(8,128)S(1)} %get-tuple-element.56), channel_id=1, source_target_pairs={{0,96},{16,112},{32,64},{48,80},{64,32},{80,48},{96,0},{112,16},{1... | collective-permute-start | bytes 393224 | tf_op jit(solution)/shard_map/ppermute | solution.py:39
  58.0 6.2 %collective-permute-start.16 = (f32[64,512]{1,0:T(8,128)S(1)}, f32[64,512]{1,0:T(8,128)S(1)}, u32[]{:S(2)}, u32[]{:S(2)}) collective-permute-start(f32[64,512]{1,0:T(8,128)S(1)} %get-tuple-element.55), channel_id=1, source_target_pairs={{0,32},{16,48},{32,0},{48,16},{64,96},{80,112},{96,64},{112,80},{1... | collective-permute-start | bytes 393224 | tf_op jit(solution)/shard_map/ppermute | solution.py:39
  58.2 9.0 %collective-permute-start.20 = (f32[64,512]{1,0:T(8,128)S(1)}, f32[64,512]{1,0:T(8,128)S(1)}, u32[]{:S(2)}, u32[]{:S(2)}) collective-permute-start(f32[64,512]{1,0:T(8,128)S(1)} %get-tuple-element.58), channel_id=1, source_target_pairs={{0,80},{16,64},{32,112},{48,96},{64,16},{80,0},{96,48},{112,32},{1... | collective-permute-start | bytes 393224 | tf_op jit(solution)/shard_map/ppermute | solution.py:39
  63.3 6.6 %collective-permute-start.19 = (f32[64,512]{1,0:T(8,128)S(1)}, f32[64,512]{1,0:T(8,128)S(1)}, u32[]{:S(2)}, u32[]{:S(2)}) collective-permute-start(f32[64,512]{1,0:T(8,128)S(1)} %get-tuple-element.57), channel_id=1, source_target_pairs={{0,64},{16,80},{32,96},{48,112},{64,0},{80,16},{96,32},{112,48},{1... | collective-permute-start | bytes 393224 | tf_op jit(solution)/shard_map/ppermute | solution.py:39
  64.3 6.6 %collective-permute-start.18 = (f32[64,512]{1,0:T(8,128)S(1)}, f32[64,512]{1,0:T(8,128)S(1)}, u32[]{:S(2)}, u32[]{:S(2)}) collective-permute-start(f32[64,512]{1,0:T(8,128)S(1)} %broadcast_select_fusion), channel_id=1, source_target_pairs={{0,16},{16,0},{32,48},{48,32},{64,80},{80,64},{96,112},{112,96},{1... | collective-permute-start | bytes 393224 | tf_op jit(solution)/shard_map/ppermute | solution.py:39

commit v8 on v7

--- a/solution.py
+++ b/solution.py
@@ -249,7 +249,7 @@
     live_amps, token = load_live(live_pairs, amplitudes, own)
     cycle_beside, token = together(cycle_beside, token)
     pair = pack(cycle_integrals, cycle_beside)
-    below, above, beside, cycle_far, pair, token = together(below, above, beside, cycle_far, pair, token)
+    below, above, beside, pair, token = together(below, above, beside, pair, token)
 
     far = pack(cycle_far)
     from_above = move(jnp.concatenate([below[0:2], beside[0:2], pair]), dy=3)

time: 71.7 us -> 71.7 us (level)
  no operation moved by 1% of the time
where the time goes in v8:
time: 71.7 us; the launch traced here: 71.5 us
  starting transfers between devices  27.6 us (38%)
  waiting for transfers between devices  27.4 us (38%)
  Pallas kernels  12.8 us (18%)
  local copies, waits for them, and re-layouts  2.36 us (3%)
  other arithmetic  1.15 us (2%)
    ppermute x14, waiting for transfers between devices, move(): return lax.ppermute(value, 'blk', blk_moves(dy, dx, dc))  22.9 us
    ppermute x7, starting transfers between devices, move_row(): return lax.ppermute(value, 'row', row_moves(dz, dx))  14.3 us
    ppermute x14, starting transfers between devices, move(): return lax.ppermute(value, 'blk', blk_moves(dy, dx, dc))  13.3 us
    pallas_call x2, Pallas kernels, ladder(): pl.pallas_call(functools.partial(ladder_kernel, places, e, len(pieces)),...  5.71 us
    ppermute x7, waiting for transfers between devices, move_row(): return lax.ppermute(value, 'row', row_moves(dz, dx))  4.43 us
    pallas_call x1, Pallas kernels, load_live(): pl.pallas_call(load_kernel, out_shape=(jax.ShapeDtypeStruct((2 * KT, rows...  4.05 us
    pallas_call x1, Pallas kernels, cycle_sums(): pl.pallas_call(functools.partial(cycle_kernel, places, width), out_shape=...  2.09 us
    unnamed x16, local copies, waits for them, and re-layouts  2.08 us
  transfers between devices with their start and end apart: 21, of which 9 were waited for; matrix products, arithmetic and copies ran while one was open for 1% of the time, Pallas kernels for 17%

profile of v8, /device:TPU:0, one launch (start us, length us, event | category | flops | bytes accessed | tf_op | source)
XLA Modules:
  0.0 71.5 jit_solution(17822847953187777195)
XLA Ops:
  0.0 0.0 copy-start.4
  0.0 0.0 copy-start
  0.0 1.2 %copy-done = bf16[16384,32]{0,1:T(8,128)(2,1)S(1)} copy-done((bf16[16384,32]{0,1:T(8,128)(2,1)S(1)}, bf16[16384,32]{0,1:T(8,128)(2,1)}, u32[]{:S(2)}) %copy-start) | copy-done | bytes 1048600
  1.2 0.0 copy-start.3
  1.2 0.7 copy-done.3
  1.9 0.9 %pick_live.1.after = bf16[4,16,4096]{2,1,0:T(8,128)(2,1)S(1)} custom-call(s32[4]{0:T(128)S(1)} %copy-done.3, bf16[32,16384]{1,0:T(8,128)(2,1)S(1)} %bitcast.3), custom_call_target="tpu_custom_call" | custom-call | tf_op jit(solution)/shard_map/pick_live/pallas_call | solution.py:66
  2.8 1.7 %collective-permute-start = (bf16[4,16,4096]{2,1,0:T(8,128)(2,1)S(1)}, bf16[4,16,4096]{2,1,0:T(8,128)(2,1)S(1)}, u32[]{:S(2)}, u32[]{:S(2)}) collective-permute-start(bf16[4,16,4096]{2,1,0:T(8,128)(2,1)S(1)} %pick_live.1.after), channel_id=1, source_target_pairs={{0,4},{1,5},{2,6},{3,7},{4,0},{5,1},{6,2},{7,3},{8,12},{9,13},{10,... | collective-permute-start | bytes 1572872 | tf_op jit(solution)/shard_map/ppermute | solution.py:35
  4.6 2.2 %collective-permute-start.1 = (bf16[4,16,4096]{2,1,0:T(8,128)(2,1)S(1)}, bf16[4,16,4096]{2,1,0:T(8,128)(2,1)S(1)}, u32[]{:S(2)}, u32[]{:S(2)}) collective-permute-start(bf16[4,16,4096]{2,1,0:T(8,128)(2,1)S(1)} %pick_live.1.after), channel_id=1, source_target_pairs={{0,12},{1,13},{2,14},{3,15},{4,8},{5,9},{6,10},{7,11},{8,4},{9,5},... | collective-permute-start | bytes 1572872 | tf_op jit(solution)/shard_map/ppermute | solution.py:35
  6.8 1.5 %collective-permute-start.2 = (bf16[4,16,4096]{2,1,0:T(8,128)(2,1)S(1)}, bf16[4,16,4096]{2,1,0:T(8,128)(2,1)S(1)}, u32[]{:S(2)}, u32[]{:S(2)}) collective-permute-start(bf16[4,16,4096]{2,1,0:T(8,128)(2,1)S(1)} %pick_live.1.after), channel_id=1, source_target_pairs={{0,2},{1,3},{2,0},{3,1},{4,6},{5,7},{6,4},{7,5},{8,10},{9,11},{10,... | collective-permute-start | bytes 1572872 | tf_op jit(solution)/shard_map/ppermute | solution.py:35
  8.2 0.5 collective-permute-start.3
  8.8 0.7 %collective-permute-start.4 = (bf16[256,128]{1,0:T(8,128)(2,1)}, bf16[256,128]{1,0:T(8,128)(2,1)S(1)}, u32[]{:S(2)}, u32[]{:S(2)}) collective-permute-start(bf16[256,128]{1,0:T(8,128)(2,1)} %refs_0_.1), channel_id=1, source_target_pairs={{0,8},{1,9},{2,10},{3,11},{4,12},{5,13},{6,14},{7,15},{8,0},{9,1},... | collective-permute-start | bytes 196616 | tf_op jit(solution)/shard_map/ppermute | solution.py:35
  9.5 0.0 copy-done.4
  9.6 0.0 copy-start.2
  9.6 4.1 %load_live.1 = (bf16[8,512,1024]{2,1,0:T(8,128)(2,1)S(1)}, f32[8,128]{1,0:T(8,128)S(1)}) custom-call(s32[4]{0:T(128)S(1)} %copy-done.4, bf16[512,16384]{1,0:T(8,128)(2,1)} %amps.1, bf16[4,16,4096]{2,1,0:T(8,128)(2,1)S(1)} %pick_live.1.after), custom_call_target="tpu_custom_call" | custom-call | tf_op jit(solution)/shard_map/load_live/pallas_call | solution.py:93
  13.6 7.6 %collective-permute-done.3.refs_1_ = bf16[256,128]{1,0:T(8,128)(2,1)S(1)} collective-permute-done((bf16[256,128]{1,0:T(8,128)(2,1)}, bf16[256,128]{1,0:T(8,128)(2,1)S(1)}, u32[]{:S(2)}, u32[]{:S(2)}) %collective-permute-start.3) | collective-permute-done | bytes 65568 | tf_op jit(solution)/shard_map/ppermute | solution.py:35
  21.3 0.0 copy-done.2
  21.3 0.0 collective-permute-done.4.refs_0_
  21.3 0.0 collective-permute-done
  21.3 0.0 collective-permute-done.1
  21.3 0.0 collective-permute-done.2
  21.6 0.2 pad_maximum_fusion.1
  21.8 1.5 %collective-permute-start.5 = (bf16[5,16,4096]{2,1,0:T(8,128)(2,1)S(1)}, bf16[5,16,4096]{2,1,0:T(8,128)(2,1)S(1)}, u32[]{:S(2)}, u32[]{:S(2)}) collective-permute-start(bf16[5,16,4096]{2,1,0:T(8,128)(2,1)S(1)} %get-tuple-element.71), channel_id=1, source_target_pairs={{0,12},{1,13},{2,14},{3,15},{4,8},{5,9},{6,10},{7,11},{8,4},{9,5},... | collective-permute-start | bytes 1966088 | tf_op jit(solution)/shard_map/ppermute | solution.py:35
  23.3 0.0 collective-permute-start.6
  23.3 1.5 %collective-permute-start.7 = (bf16[5,16,4096]{2,1,0:T(8,128)(2,1)S(1)}, bf16[5,16,4096]{2,1,0:T(8,128)(2,1)S(1)}, u32[]{:S(2)}, u32[]{:S(2)}) collective-permute-start(bf16[5,16,4096]{2,1,0:T(8,128)(2,1)S(1)} %get-tuple-element.72), channel_id=1, source_target_pairs={{0,2},{1,3},{2,0},{3,1},{4,6},{5,7},{6,4},{7,5},{8,10},{9,11},{10,... | collective-permute-start | bytes 1966088 | tf_op jit(solution)/shard_map/ppermute | solution.py:35
  24.8 0.1 collective-permute-start.8
  24.9 13.2 %collective-permute-done.5 = bf16[5,16,4096]{2,1,0:T(8,128)(2,1)S(1)} collective-permute-done((bf16[5,16,4096]{2,1,0:T(8,128)(2,1)S(1)}, bf16[5,16,4096]{2,1,0:T(8,128)(2,1)S(1)}, u32[]{:S(2)}, u32[]{:S(2)}) %collective-permute-start.5) | collective-permute-done | bytes 655392 | tf_op jit(solution)/shard_map/ppermute | solution.py:35
  38.1 0.2 collective-permute-done.6
  38.3 0.0 collective-permute-done.7
  38.4 0.0 copy-start.1
  38.4 0.1 pad_maximum_fusion.refs_1_
  38.6 0.1 collective-permute-start.10
  38.7 0.6 collective-permute-start.9
  39.3 1.6 %collective-permute-start.13 = (bf16[2,16,4096]{2,1,0:T(8,128)(2,1)S(1)}, bf16[2,16,4096]{2,1,0:T(8,128)(2,1)S(1)}, u32[]{:S(2)}, u32[]{:S(2)}) collective-permute-start(bf16[2,16,4096]{2,1,0:T(8,128)(2,1)S(1)} %pad_maximum_fusion.6), channel_id=1, source_target_pairs={{0,12},{1,13},{2,14},{3,15},{4,8},{5,9},{6,10},{7,11},{8,4},{9,5},... | collective-permute-start | bytes 786440 | tf_op jit(solution)/shard_map/ppermute | solution.py:35
  41.0 1.2 %collective-permute-start.14 = (bf16[2,16,4096]{2,1,0:T(8,128)(2,1)S(1)}, bf16[2,16,4096]{2,1,0:T(8,128)(2,1)S(1)}, u32[]{:S(2)}, u32[]{:S(2)}) collective-permute-start(bf16[2,16,4096]{2,1,0:T(8,128)(2,1)S(1)} %pad_maximum_fusion.7), channel_id=1, source_target_pairs={{0,4},{1,5},{2,6},{3,7},{4,0},{5,1},{6,2},{7,3},{8,12},{9,13},{10,... | collective-permute-start | bytes 786440 | tf_op jit(solution)/shard_map/ppermute | solution.py:35
  42.2 0.0 collective-permute-done.10.refs_3_
  42.2 0.4 collective-permute-done.9.refs_3_
  42.6 0.0 collective-permute-done.8.refs_2_
  42.6 0.0 copy-done.1
  42.6 2.1 %cycle.1 = f32[4,512,128]{2,1,0:T(8,128)S(1)} custom-call(bf16[8,8,512]{2,1,0:T(8,128)(2,1)S(1)} %copy-done.1, f32[8,128]{1,0:T(8,128)S(1)} %get-tuple-element.43.token.before, bf16[18,16,4096]{2,1,0:T(8,128)(2,1)S(1)} %constant_dynamic-update-slice_fusion.refs_0_, bf16[7,16,4096]{2,1,0:T(8,128)(2,1)S(1)} %get-tuple-element.65.refs_1_, ...), custom_call_target="tpu_custom_call" | custom-call | flops 134217728 | bytes 8388608 | tf_op jit(solution)/shard_map/cycle/pallas_call | solution.py:221
  44.7 2.8 %ladder.2 = (f32[64,512]{1,0:T(8,128)S(1)}, f32[64,512]{1,0:T(8,128)S(1)}, f32[64,512]{1,0:T(8,128)S(1)}, f32[64,512]{1,0:T(8,128)S(1)}, f32[8,128]{1,0:T(8,128)}) custom-call(bf16[8,512,1024]{2,1,0:T(8,128)(2,1)S(1)} %get-tuple-element.31.amps, f32[4,512,128]{2,1,0:T(8,128)S(1)} %cycle.1, f32[8,128]{1,0:T(8,128)S(1)} %get-tuple-element.43.token.before, ...), custom_call_target="tpu_custom_call" | custom-call | flops 2147483648 | bytes 4194304 | tf_op jit(solution)/shard_map/ladder/pallas_call | solution.py:153
  47.5 1.3 %collective-permute-done.13 = bf16[2,16,4096]{2,1,0:T(8,128)(2,1)S(1)} collective-permute-done((bf16[2,16,4096]{2,1,0:T(8,128)(2,1)S(1)}, bf16[2,16,4096]{2,1,0:T(8,128)(2,1)S(1)}, u32[]{:S(2)}, u32[]{:S(2)}) %collective-permute-start.13) | collective-permute-done | bytes 262176 | tf_op jit(solution)/shard_map/ppermute | solution.py:35
  48.8 0.2 collective-permute-done.14
  49.1 0.1 collective-permute-start.15
  49.1 4.1 %collective-permute-start.12 = (f32[64,512]{1,0:T(8,128)S(1)}, f32[64,512]{1,0:T(8,128)S(1)}, u32[]{:S(2)}, u32[]{:S(2)}) collective-permute-start(f32[64,512]{1,0:T(8,128)S(1)} %get-tuple-element.46), channel_id=1, source_target_pairs={{0,96},{16,112},{32,64},{48,80},{64,32},{80,48},{96,0},{112,16},{1... | collective-permute-start | bytes 393224 | tf_op jit(solution)/shard_map/ppermute | solution.py:39
  53.3 0.0 collective-permute-start.11
  53.3 0.0 collective-permute-done.15.refs_5_
  53.3 2.9 %ladder.3 = (f32[64,512]{1,0:T(8,128)S(1)}, f32[64,512]{1,0:T(8,128)S(1)}, f32[64,512]{1,0:T(8,128)S(1)}, f32[64,512]{1,0:T(8,128)S(1)}, f32[64,512]{1,0:T(8,128)S(1)}, /*index=5*/f32[8,128]{1,0:T(8,128)}) custom-call(bf16[8,512,1024]{2,1,0:T(8,128)(2,1)S(1)} %get-tuple-element.31.amps, f32[4,512,128]{2,1,0:T(8,128)S(1)} %cycle.1, ...), custom_call_target="tpu_custom_call" | custom-call | flops 2147483648 | bytes 4194304 | tf_op jit(solution)/shard_map/ladder/pallas_call | solution.py:153
  56.2 1.8 %collective-permute-start.17 = (f32[64,512]{1,0:T(8,128)S(1)}, f32[64,512]{1,0:T(8,128)S(1)}, u32[]{:S(2)}, u32[]{:S(2)}) collective-permute-start(f32[64,512]{1,0:T(8,128)S(1)} %get-tuple-element.54), channel_id=1, source_target_pairs={{0,96},{16,112},{32,64},{48,80},{64,32},{80,48},{96,0},{112,16},{1... | collective-permute-start | bytes 393224 | tf_op jit(solution)/shard_map/ppermute | solution.py:39
  58.0 0.2 collective-permute-start.16
  58.2 5.1 %collective-permute-start.20 = (f32[64,512]{1,0:T(8,128)S(1)}, f32[64,512]{1,0:T(8,128)S(1)}, u32[]{:S(2)}, u32[]{:S(2)}) collective-permute-start(f32[64,512]{1,0:T(8,128)S(1)} %get-tuple-element.56), channel_id=1, source_target_pairs={{0,80},{16,64},{32,112},{48,96},{64,16},{80,0},{96,48},{112,32},{1... | collective-permute-start | bytes 393224 | tf_op jit(solution)/shard_map/ppermute | solution.py:39
  63.3 0.0 collective-permute-done.12
  63.3 0.9 %collective-permute-start.19 = (f32[64,512]{1,0:T(8,128)S(1)}, f32[64,512]{1,0:T(8,128)S(1)}, u32[]{:S(2)}, u32[]{:S(2)}) collective-permute-start(f32[64,512]{1,0:T(8,128)S(1)} %get-tuple-element.55), channel_id=1, source_target_pairs={{0,64},{16,80},{32,96},{48,112},{64,0},{80,16},{96,32},{112,48},{1... | collective-permute-start | bytes 393224 | tf_op jit(solution)/shard_map/ppermute | solution.py:39
  64.2 0.0 collective-permute-done.11
  64.2 0.0 collective-permute-done.17
  64.2 0.0 collective-permute-done.16
  64.2 0.1 broadcast_select_fusion
  64.3 2.1 %collective-permute-start.18 = (f32[64,512]{1,0:T(8,128)S(1)}, f32[64,512]{1,0:T(8,128)S(1)}, u32[]{:S(2)}, u32[]{:S(2)}) collective-permute-start(f32[64,512]{1,0:T(8,128)S(1)} %broadcast_select_fusion), channel_id=1, source_target_pairs={{0,16},{16,0},{32,48},{48,32},{64,80},{80,64},{96,112},{112,96},{1... | collective-permute-start | bytes 393224 | tf_op jit(solution)/shard_map/ppermute | solution.py:39
  66.4 0.8 %collective-permute-done.20 = f32[64,512]{1,0:T(8,128)S(1)} collective-permute-done((f32[64,512]{1,0:T(8,128)S(1)}, f32[64,512]{1,0:T(8,128)S(1)}, u32[]{:S(2)}, u32[]{:S(2)}) %collective-permute-start.20) | collective-permute-done | bytes 131104 | tf_op jit(solution)/shard_map/ppermute | solution.py:39
  67.2 2.8 %collective-permute-done.19 = f32[64,512]{1,0:T(8,128)S(1)} collective-permute-done((f32[64,512]{1,0:T(8,128)S(1)}, f32[64,512]{1,0:T(8,128)S(1)}, u32[]{:S(2)}, u32[]{:S(2)}) %collective-permute-start.19) | collective-permute-done | bytes 131104 | tf_op jit(solution)/shard_map/ppermute | solution.py:39
  69.9 0.9 %collective-permute-done.18 = f32[64,512]{1,0:T(8,128)S(1)} collective-permute-done((f32[64,512]{1,0:T(8,128)S(1)}, f32[64,512]{1,0:T(8,128)S(1)}, u32[]{:S(2)}, u32[]{:S(2)}) %collective-permute-start.18) | collective-permute-done | bytes 131104 | tf_op jit(solution)/shard_map/ppermute | solution.py:39
  70.8 0.7 %fusion = bf16[512,64]{0,1:T(8,128)(2,1)} fusion(f32[64,512]{1,0:T(8,128)S(1)} %collective-permute-done.20, f32[64,512]{1,0:T(8,128)S(1)} %collective-permute-done.19, f32[64,512]{1,0:T(8,128)S(1)} %collective-permute-done.18, pred[]{:T(512)S(6)} %eq.6, f32[64,512]{1,0:T(8,128)S(1)} %collective-permute-done.12, f32[64,512]{1,0:T(8,128)S(1)} %get-tuple-element.44, ...), kind=kLoop, calls=%fused_computation.16 | loop fusion | flops 294912 | bytes 1245185 | tf_op jit(solution)/shard_map/transpose | solution.py:297
  (21 shorter events, 0.5 us)
Async XLA Ops:
  0.0 9.5 %copy-start.4 = (s32[4]{0:T(128)S(1)}, s32[4]{0:T(128)}, u32[]{:S(2)}) copy-start(s32[4]{0:T(128)} %live.3) | copy-start | bytes 52
  0.0 1.2 %copy-start = (bf16[16384,32]{0,1:T(8,128)(2,1)S(1)}, bf16[16384,32]{0,1:T(8,128)(2,1)}, u32[]{:S(2)}) copy-start(bf16[16384,32]{0,1:T(8,128)(2,1)} %param.6) | copy-start | bytes 3145732
  1.2 0.7 copy-start.3
  2.8 18.5 %collective-permute-start = (bf16[4,16,4096]{2,1,0:T(8,128)(2,1)S(1)}, bf16[4,16,4096]{2,1,0:T(8,128)(2,1)S(1)}, u32[]{:S(2)}, u32[]{:S(2)}) collective-permute-start(bf16[4,16,4096]{2,1,0:T(8,128)(2,1)S(1)} %pick_live.1.after), channel_id=1, source_target_pairs={{0,4},{1,5},{2,6},{3,7},{4,0},{5,1},{6,2},{7,3},{8,12},{9,13},{10,... | collective-permute-start | bytes 1572872 | tf_op jit(solution)/shard_map/ppermute | solution.py:35
  4.6 16.8 %collective-permute-start.1 = (bf16[4,16,4096]{2,1,0:T(8,128)(2,1)S(1)}, bf16[4,16,4096]{2,1,0:T(8,128)(2,1)S(1)}, u32[]{:S(2)}, u32[]{:S(2)}) collective-permute-start(bf16[4,16,4096]{2,1,0:T(8,128)(2,1)S(1)} %pick_live.1.after), channel_id=1, source_target_pairs={{0,12},{1,13},{2,14},{3,15},{4,8},{5,9},{6,10},{7,11},{8,4},{9,5},... | collective-permute-start | bytes 1572872 | tf_op jit(solution)/shard_map/ppermute | solution.py:35
  6.8 14.6 %collective-permute-start.2 = (bf16[4,16,4096]{2,1,0:T(8,128)(2,1)S(1)}, bf16[4,16,4096]{2,1,0:T(8,128)(2,1)S(1)}, u32[]{:S(2)}, u32[]{:S(2)}) collective-permute-start(bf16[4,16,4096]{2,1,0:T(8,128)(2,1)S(1)} %pick_live.1.after), channel_id=1, source_target_pairs={{0,2},{1,3},{2,0},{3,1},{4,6},{5,7},{6,4},{7,5},{8,10},{9,11},{10,... | collective-permute-start | bytes 1572872 | tf_op jit(solution)/shard_map/ppermute | solution.py:35
  8.2 13.0 %collective-permute-start.3 = (bf16[256,128]{1,0:T(8,128)(2,1)}, bf16[256,128]{1,0:T(8,128)(2,1)S(1)}, u32[]{:S(2)}, u32[]{:S(2)}) collective-permute-start(bf16[256,128]{1,0:T(8,128)(2,1)} %refs_0_.1), channel_id=1, source_target_pairs={{0,2},{1,3},{2,0},{3,1},{4,6},{5,7},{6,4},{7,5},{8,10},{9,11},{10,... | collective-permute-start | bytes 196616 | tf_op jit(solution)/shard_map/ppermute | solution.py:35
  8.8 12.5 %collective-permute-start.4 = (bf16[256,128]{1,0:T(8,128)(2,1)}, bf16[256,128]{1,0:T(8,128)(2,1)S(1)}, u32[]{:S(2)}, u32[]{:S(2)}) collective-permute-start(bf16[256,128]{1,0:T(8,128)(2,1)} %refs_0_.1), channel_id=1, source_target_pairs={{0,8},{1,9},{2,10},{3,11},{4,12},{5,13},{6,14},{7,15},{8,0},{9,1},... | collective-permute-start | bytes 196616 | tf_op jit(solution)/shard_map/ppermute | solution.py:35
  9.6 11.7 %copy-start.2 = (bf16[256,128]{1,0:T(8,128)(2,1)S(1)}, bf16[256,128]{1,0:T(8,128)(2,1)}, u32[]{:S(2)}) copy-start(bf16[256,128]{1,0:T(8,128)(2,1)} %refs_0_.1) | copy-start | bytes 196612
  21.8 16.3 %collective-permute-start.5 = (bf16[5,16,4096]{2,1,0:T(8,128)(2,1)S(1)}, bf16[5,16,4096]{2,1,0:T(8,128)(2,1)S(1)}, u32[]{:S(2)}, u32[]{:S(2)}) collective-permute-start(bf16[5,16,4096]{2,1,0:T(8,128)(2,1)S(1)} %get-tuple-element.71), channel_id=1, source_target_pairs={{0,12},{1,13},{2,14},{3,15},{4,8},{5,9},{6,10},{7,11},{8,4},{9,5},... | collective-permute-start | bytes 1966088 | tf_op jit(solution)/shard_map/ppermute | solution.py:35
  23.3 15.0 %collective-permute-start.6 = (bf16[5,16,4096]{2,1,0:T(8,128)(2,1)S(1)}, bf16[5,16,4096]{2,1,0:T(8,128)(2,1)S(1)}, u32[]{:S(2)}, u32[]{:S(2)}) collective-permute-start(bf16[5,16,4096]{2,1,0:T(8,128)(2,1)S(1)} %get-tuple-element.70), channel_id=1, source_target_pairs={{0,4},{1,5},{2,6},{3,7},{4,0},{5,1},{6,2},{7,3},{8,12},{9,13},{10,... | collective-permute-start | bytes 1966088 | tf_op jit(solution)/shard_map/ppermute | solution.py:35
  23.3 15.0 %collective-permute-start.7 = (bf16[5,16,4096]{2,1,0:T(8,128)(2,1)S(1)}, bf16[5,16,4096]{2,1,0:T(8,128)(2,1)S(1)}, u32[]{:S(2)}, u32[]{:S(2)}) collective-permute-start(bf16[5,16,4096]{2,1,0:T(8,128)(2,1)S(1)} %get-tuple-element.72), channel_id=1, source_target_pairs={{0,2},{1,3},{2,0},{3,1},{4,6},{5,7},{6,4},{7,5},{8,10},{9,11},{10,... | collective-permute-start | bytes 1966088 | tf_op jit(solution)/shard_map/ppermute | solution.py:35
  24.8 17.8 %collective-permute-start.8 = (bf16[18,16,4096]{2,1,0:T(8,128)(2,1)S(1)}, bf16[18,16,4096]{2,1,0:T(8,128)(2,1)S(1)}, u32[]{:S(2)}, u32[]{:S(2)}) collective-permute-start(bf16[18,16,4096]{2,1,0:T(8,128)(2,1)S(1)} %constant_dynamic-update-slice_fusion.refs_0_), channel_id=1, source_target_pairs={{0,1},{1,0},{2,3},{3,2},{4,5},{5,4},{6,7},{7,6},{8,9},{9,8},{10,11... | collective-permute-start | bytes 7077896 | tf_op jit(solution)/shard_map/ppermute | solution.py:35
  38.4 4.2 %copy-start.1 = (bf16[8,8,512]{2,1,0:T(8,128)(2,1)S(1)}, bf16[8,8,512]{2,1,0:T(8,128)(2,1)}, u32[]{:S(2)}) copy-start(bf16[8,8,512]{2,1,0:T(8,128)(2,1)} %slab_amps.1) | copy-start | bytes 196612
  38.6 3.6 %collective-permute-start.10 = (bf16[8,16,4096]{2,1,0:T(8,128)(2,1)S(1)}, bf16[8,16,4096]{2,1,0:T(8,128)(2,1)S(1)}, u32[]{:S(2)}, u32[]{:S(2)}) collective-permute-start(bf16[8,16,4096]{2,1,0:T(8,128)(2,1)S(1)} %pad_maximum_fusion.refs_1_), channel_id=1, source_target_pairs={{0,1},{1,0},{2,3},{3,2},{4,5},{5,4},{6,7},{7,6},{8,9},{9,8},{10,11... | collective-permute-start | bytes 3145736 | tf_op jit(solution)/shard_map/ppermute | solution.py:35
  38.7 3.9 %collective-permute-start.9 = (bf16[7,16,4096]{2,1,0:T(8,128)(2,1)S(1)}, bf16[7,16,4096]{2,1,0:T(8,128)(2,1)S(1)}, u32[]{:S(2)}, u32[]{:S(2)}) collective-permute-start(bf16[7,16,4096]{2,1,0:T(8,128)(2,1)S(1)} %get-tuple-element.65.refs_1_), channel_id=1, source_target_pairs={{0,1},{1,0},{2,3},{3,2},{4,5},{5,4},{6,7},{7,6},{8,9},{9,8},{10,11... | collective-permute-start | bytes 2752520 | tf_op jit(solution)/shard_map/ppermute | solution.py:35
  39.3 9.5 %collective-permute-start.13 = (bf16[2,16,4096]{2,1,0:T(8,128)(2,1)S(1)}, bf16[2,16,4096]{2,1,0:T(8,128)(2,1)S(1)}, u32[]{:S(2)}, u32[]{:S(2)}) collective-permute-start(bf16[2,16,4096]{2,1,0:T(8,128)(2,1)S(1)} %pad_maximum_fusion.6), channel_id=1, source_target_pairs={{0,12},{1,13},{2,14},{3,15},{4,8},{5,9},{6,10},{7,11},{8,4},{9,5},... | collective-permute-start | bytes 786440 | tf_op jit(solution)/shard_map/ppermute | solution.py:35
  41.0 8.0 %collective-permute-start.14 = (bf16[2,16,4096]{2,1,0:T(8,128)(2,1)S(1)}, bf16[2,16,4096]{2,1,0:T(8,128)(2,1)S(1)}, u32[]{:S(2)}, u32[]{:S(2)}) collective-permute-start(bf16[2,16,4096]{2,1,0:T(8,128)(2,1)S(1)} %pad_maximum_fusion.7), channel_id=1, source_target_pairs={{0,4},{1,5},{2,6},{3,7},{4,0},{5,1},{6,2},{7,3},{8,12},{9,13},{10,... | collective-permute-start | bytes 786440 | tf_op jit(solution)/shard_map/ppermute | solution.py:35
  49.1 4.2 %collective-permute-start.15 = (bf16[4,16,4096]{2,1,0:T(8,128)(2,1)S(1)}, bf16[4,16,4096]{2,1,0:T(8,128)(2,1)S(1)}, u32[]{:S(2)}, u32[]{:S(2)}) collective-permute-start(bf16[4,16,4096]{2,1,0:T(8,128)(2,1)S(1)} %constant_dynamic-update-slice_fusion.6.refs_4_), channel_id=1, source_target_pairs={{0,1},{1,0},{2,3},{3,2},{4,5},{5,4},{6,7},{7,6},{8,9},{9,8},{10,11... | collective-permute-start | bytes 1572872 | tf_op jit(solution)/shard_map/ppermute | solution.py:35
  49.1 14.2 %collective-permute-start.12 = (f32[64,512]{1,0:T(8,128)S(1)}, f32[64,512]{1,0:T(8,128)S(1)}, u32[]{:S(2)}, u32[]{:S(2)}) collective-permute-start(f32[64,512]{1,0:T(8,128)S(1)} %get-tuple-element.46), channel_id=1, source_target_pairs={{0,96},{16,112},{32,64},{48,80},{64,32},{80,48},{96,0},{112,16},{1... | collective-permute-start | bytes 393224 | tf_op jit(solution)/shard_map/ppermute | solution.py:39
  53.3 10.9 %collective-permute-start.11 = (f32[64,512]{1,0:T(8,128)S(1)}, f32[64,512]{1,0:T(8,128)S(1)}, u32[]{:S(2)}, u32[]{:S(2)}) collective-permute-start(f32[64,512]{1,0:T(8,128)S(1)} %get-tuple-element.45), channel_id=1, source_target_pairs={{0,32},{16,48},{32,0},{48,16},{64,96},{80,112},{96,64},{112,80},{1... | collective-permute-start | bytes 393224 | tf_op jit(solution)/shard_map/ppermute | solution.py:39
  56.2 8.0 %collective-permute-start.17 = (f32[64,512]{1,0:T(8,128)S(1)}, f32[64,512]{1,0:T(8,128)S(1)}, u32[]{:S(2)}, u32[]{:S(2)}) collective-permute-start(f32[64,512]{1,0:T(8,128)S(1)} %get-tuple-element.54), channel_id=1, source_target_pairs={{0,96},{16,112},{32,64},{48,80},{64,32},{80,48},{96,0},{112,16},{1... | collective-permute-start | bytes 393224 | tf_op jit(solution)/shard_map/ppermute | solution.py:39
  58.0 6.2 %collective-permute-start.16 = (f32[64,512]{1,0:T(8,128)S(1)}, f32[64,512]{1,0:T(8,128)S(1)}, u32[]{:S(2)}, u32[]{:S(2)}) collective-permute-start(f32[64,512]{1,0:T(8,128)S(1)} %get-tuple-element.53), channel_id=1, source_target_pairs={{0,32},{16,48},{32,0},{48,16},{64,96},{80,112},{96,64},{112,80},{1... | collective-permute-start | bytes 393224 | tf_op jit(solution)/shard_map/ppermute | solution.py:39
  58.2 9.0 %collective-permute-start.20 = (f32[64,512]{1,0:T(8,128)S(1)}, f32[64,512]{1,0:T(8,128)S(1)}, u32[]{:S(2)}, u32[]{:S(2)}) collective-permute-start(f32[64,512]{1,0:T(8,128)S(1)} %get-tuple-element.56), channel_id=1, source_target_pairs={{0,80},{16,64},{32,112},{48,96},{64,16},{80,0},{96,48},{112,32},{1... | collective-permute-start | bytes 393224 | tf_op jit(solution)/shard_map/ppermute | solution.py:39
  63.3 6.6 %collective-permute-start.19 = (f32[64,512]{1,0:T(8,128)S(1)}, f32[64,512]{1,0:T(8,128)S(1)}, u32[]{:S(2)}, u32[]{:S(2)}) collective-permute-start(f32[64,512]{1,0:T(8,128)S(1)} %get-tuple-element.55), channel_id=1, source_target_pairs={{0,64},{16,80},{32,96},{48,112},{64,0},{80,16},{96,32},{112,48},{1... | collective-permute-start | bytes 393224 | tf_op jit(solution)/shard_map/ppermute | solution.py:39
  64.3 6.6 %collective-permute-start.18 = (f32[64,512]{1,0:T(8,128)S(1)}, f32[64,512]{1,0:T(8,128)S(1)}, u32[]{:S(2)}, u32[]{:S(2)}) collective-permute-start(f32[64,512]{1,0:T(8,128)S(1)} %broadcast_select_fusion), channel_id=1, source_target_pairs={{0,16},{16,0},{32,48},{48,32},{64,80},{80,64},{96,112},{112,96},{1... | collective-permute-start | bytes 393224 | tf_op jit(solution)/shard_map/ppermute | solution.py:39
